TPU v7x, 32 devices: a whole 2x2x4 slice. The times are simulated.
32 devices in a mesh: cells: 8 (over y, x, core), snap: 4 (over z).
Axes of the slice: x: 2, y: 2, z: 4, core: 2. Of those that a mesh axis runs over, the one named last changes fastest.
Arguments:
- snapshots: bfloat16 [3, 8192, 1024], P(None, 'cells', 'snap'), may hold values from -10 to 10
- mass_blocks: bfloat16 [128, 64, 64], P('cells'), may hold values from -0.25 to 4.25
- block_offsets: int32 [128], P('cells'), may hold values from 0 to 8128, as said below
Outputs:
- gram: float32 [1024, 1024], P('snap', 'cells')
Inputs may be any that keep to these rules, and one draw needn't show every extreme that they name: `block_offsets`: offsets are multiples of 64; the blocks of the g-th aligned group of 16 blocks start at distinct offsets that together cover cells g * 1024 to (g + 1) * 1024 - 1.
All inputs are finite; a program needn't handle non-finite values.
Results may differ from a plain program's by a relative error of at most 0.0003.
Values may be sent and summed in bfloat16 or wider, within the bound.
No kernel may reach another device: no remote copies, remote signals or barrier semaphores. Data moves between devices by JAX's collectives and lax.ppermute only.
A program may use at most 128 MiB of HBM per device.

v0:
```python
import jax
import jax.numpy as jnp
from jax import lax
from jax.sharding import PartitionSpec as P


def local(snapshots, mass_blocks, block_offsets):
    components, cell_rows, columns_dev = snapshots.shape
    blocks_dev = mass_blocks.shape[0]
    block_size = mass_blocks.shape[1]
    base_block = lax.axis_index("cells") * blocks_dev
    local_index = block_offsets // block_size - base_block
    selected = jnp.take(
        snapshots.reshape(components, blocks_dev, block_size, columns_dev), local_index, axis=1
    )
    weighted = jnp.einsum(
        "bij,cbjs->cbis", mass_blocks, selected, preferred_element_type=jnp.float32
    ).astype(jnp.bfloat16)
    left_rows = selected.reshape(components * cell_rows, columns_dev)
    right_rows = weighted.reshape(components * cell_rows, columns_dev)
    product = lax.dot_general(
        left_rows,
        lax.all_gather(right_rows, "snap", axis=1, tiled=True),
        (((0,), (0,)), ((), ())),
        preferred_element_type=jnp.float32,
    )
    groups_count = lax.axis_size("cells")
    factor = 1.0 / float(3 * cell_rows * groups_count)
    result = lax.psum_scatter(product, "cells", scatter_dimension=1, tiled=True)
    return result * factor


def solution(mesh):
    placed = (P(None, "cells", "snap"), P("cells", None, None), P("cells"))
    return jax.shard_map(
        local, mesh=mesh, in_specs=placed, out_specs=P("snap", "cells"), check_vma=False
    )
```

profile of v0, /device:TPU:4, one launch (start us, length us, event | category | flops | bytes accessed | tf_op | source)
XLA Modules:
  0.0 175.4 jit_solution(16035474868895258574)
XLA Ops:
  6.5 0.0 copy-start
  6.5 0.0 all-gather.2.cloned.1.call-start
  6.5 0.8 compare_and_fusion
  7.3 0.6 copy-done
  8.0 0.0 copy-start.1
  8.0 0.6 gather_fusion
  8.6 0.3 copy-done.1
  8.9 0.6 fusion.2
  9.5 1.2 copy.7
  10.8 0.0 all-gather.2.cloned.1.call-update
  10.8 0.0 reduce-scatter.2.cloned.1.call-start
  10.9 1.3 copy.6
  12.2 0.1 broadcast_in_dim.20
  12.3 0.1 broadcast_in_dim.21
  12.4 2.7 %bitcast_select_fusion = bf16[3072,256]{1,0:T(8,128)(2,1)S(1)} fusion(bf16[3,16,64,256]{3,2,1,0:T(8,128)(2,1)} %copy.6, pred[3072]{0:T(1024)(128)(4,1)S(1)} %broadcast_in_dim.21), kind=kLoop, calls=%fused_computation.2 | loop fusion | flops 786432 | bytes 3148800 | tf_op jit(solution)/shard_map/jit(_take)/select_n | solution.py:13
  15.1 112.0 %all-gather.2.cloned.1.call-done = bf16[3072,1024]{1,0:T(8,128)(2,1)} async-done(((bf16[3072,256]{1,0:T(8,128)(2,1)}), bf16[3072,1024]{1,0:T(8,128)(2,1)}) %all-gather.2.cloned.1.call-update) | async-done | bytes 6291472 | tf_op jit(solution)/shard_map/all_gather | solution.py:23
  127.1 5.6 %fusion.9 = f32[256,1024]{1,0:T(8,128)} fusion(bf16[3072,256]{1,0:T(8,128)(2,1)S(1)} %bitcast_select_fusion, bf16[3072,1024]{1,0:T(8,128)(2,1)} %all-gather.2.cloned.1.call-done), kind=kOutput, calls=%fused_computation.18 | convolution fusion | flops 1610612736 | bytes 8912896 | tf_op jit(solution)/shard_map/dot_general | solution.py:21
  132.7 0.0 reduce-scatter.2.cloned.1.call-update
  132.7 34.3 %reduce-scatter.2.cloned.1.call-done = f32[256,128]{1,0:T(8,128)} async-done(((f32[256,1024]{1,0:T(8,128)}), f32[256,128]{1,0:T(8,128)}) %reduce-scatter.2.cloned.1.call-update) | async-done | bytes 131088 | tf_op jit(solution)/shard_map/reduce_scatter | solution.py:29
  167.0 1.6 broadcast_multiply_fusion
  (1 shorter events, 0.0 us)
Async XLA Ops:
  6.5 1.4 copy-start
  6.5 120.5 %all-gather.2.cloned.1.call-start = ((), (), s32[]{:S(2)}) async-start(), calls=%async_computation.1 | async-start | bytes 7864320 | tf_op jit(solution)/shard_map/all_gather | solution.py:23
  8.0 0.9 copy-start.1
  10.8 156.2 %reduce-scatter.2.cloned.1.call-start = ((), (), s32[]{:S(2)}) async-start(), calls=%async_computation.2 | async-start | bytes 1179648 | tf_op jit(solution)/shard_map/reduce_scatter | solution.py:29
Sparse Core Ops, SparseCore 0:
  10.9 116.0 all-gather.1
  132.8 34.1 reduce-scatter.1
where the time goes:
time: 177 us; the launch traced here: 175 us
  waiting for transfers between devices  146 us (82%)
  between operations  13.4 us (8%)
  matrix products  6.23 us (4%)
  other arithmetic  5.07 us (3%)
  local copies, waits for them, and re-layouts  4.31 us (2%)
    all_gather x1, waiting for transfers between devices, local(): lax.all_gather(right_rows, 'snap', axis=1, tiled=True)  112 us
    reduce_scatter x1, waiting for transfers between devices, local(): result = lax.psum_scatter(product, 'cells', scatter_dimension=1, tiled=True)  34.3 us
    dot_general x1, matrix products, local(): lax.dot_general(left_rows, lax.all_gather(right_rows, 'snap', axis=1, til...  5.6 us
  transfers between devices with their start and end apart: 2, of which 2 were waited for; matrix products, arithmetic and copies ran while one was open for 2% of the time, Pallas kernels for 0%

commit v1 on v0

v1 whole, which is shorter than its diff:
```python
import functools

import jax
import jax.numpy as jnp
from jax import lax
from jax.experimental import pallas as pl
from jax.experimental.pallas import tpu as pltpu
from jax.sharding import PartitionSpec as P

BF16, F32 = jnp.bfloat16, jnp.float32


def general(snapshots, mass_blocks, block_offsets):
    components, cell_rows, columns_dev = snapshots.shape
    blocks_dev = mass_blocks.shape[0]
    block_size = mass_blocks.shape[1]
    base_block = lax.axis_index("cells") * blocks_dev
    local_index = block_offsets // block_size - base_block
    selected = jnp.take(
        snapshots.reshape(components, blocks_dev, block_size, columns_dev), local_index, axis=1
    )
    weighted = jnp.einsum(
        "bij,cbjs->cbis", mass_blocks, selected, preferred_element_type=F32
    ).astype(BF16)
    left_rows = selected.reshape(components * cell_rows, columns_dev)
    right_rows = weighted.reshape(components * cell_rows, columns_dev)
    product = lax.dot_general(
        left_rows,
        lax.all_gather(right_rows, "snap", axis=1, tiled=True),
        (((0,), (0,)), ((), ())),
        preferred_element_type=F32,
    )
    factor = 1.0 / float(3 * cell_rows * lax.axis_size("cells"))
    result = lax.psum_scatter(product, "cells", scatter_dimension=1, tiled=True)
    return result * factor


STAGE_C = ((0, 0), (2, 0), (2, 1), (0, 2), (1, 2))
START_C = (0, 2, 3, 3)
STAGE_D = ((1, 0), (3, 0), (0, 1), (3, 1), (0, 3), (1, 3))
START_D = (0, 2, 4, 4)


def tdot(left, right):
    return lax.dot_general(left, right, (((0,), (0,)), ((), ())), preferred_element_type=F32)


def weigh(diagonal, piece):
    return jnp.concatenate(
        [
            jnp.dot(diagonal, piece[c], preferred_element_type=F32).astype(BF16)
            for c in range(piece.shape[0])
        ],
        axis=0,
    )


def flat(piece):
    return piece.reshape(piece.shape[0] * piece.shape[1], piece.shape[2])


def put(core, block, own_ref, other_ref, at):
    half = block.shape[1] // 2
    low, high = block[:, :half], block[:, half:]
    first = core == 0
    own_ref[at] = jnp.where(first, low, high)
    other_ref[at] = jnp.where(first, high, low)


def early_kernel(offsets_ref, mass_ref, s_ref, diagonal_ref, weighted_ref, gram_ref, where_ref):
    components, cell_rows, _ = s_ref.shape
    blocks, size, _ = mass_ref.shape
    quarters, rows, _ = diagonal_ref.shape
    base = lax.axis_index("cells") * blocks
    for b in range(blocks):
        where_ref[offsets_ref[b] // size - base] = b
    diagonal_ref[...] = jnp.zeros_like(diagonal_ref)
    per = blocks // quarters
    for t in range(quarters):
        for i in range(per):
            diagonal_ref[t, i * size : (i + 1) * size, i * size : (i + 1) * size] = mass_ref[
                where_ref[t * per + i]
            ]
    for t in range(quarters):
        for c in range(components):
            rows_now = slice(t * rows, (t + 1) * rows)
            weighted_ref[c, rows_now, :] = jnp.dot(
                diagonal_ref[t], s_ref[c, rows_now, :], preferred_element_type=F32
            ).astype(BF16)
    total = tdot(s_ref[0], weighted_ref[0])
    for c in range(1, components):
        total += tdot(s_ref[c], weighted_ref[c])
    gram_ref[...] = total


def stage_c_kernel(
    scale, s_ref, weighted_ref, diagonal_ref, gram_ref, s1_ref, s2_ref, own_ref, other_ref
):
    z, core = lax.axis_index("snap"), lax.axis_index("cells") % 2
    rows = s2_ref.shape[1]
    mine = pl.ds(pl.multiple_of(z * rows, rows), rows)
    diagonal = diagonal_ref[z]
    s0, w0 = flat(s_ref[:, mine, :]), flat(weighted_ref[:, mine, :])
    s1, s2 = flat(s1_ref[...]), flat(s2_ref[...])
    w1, w2 = weigh(diagonal, s1_ref[...]), weigh(diagonal, s2_ref[...])
    blocks = {
        (0, 0): lambda: gram_ref[...],
        (2, 0): lambda: tdot(s2, w0),
        (2, 1): lambda: tdot(s2, w1),
        (0, 2): lambda: tdot(s0, w2),
        (1, 2): lambda: tdot(s1, w2),
    }
    for at, name in enumerate(STAGE_C):
        put(core, blocks[name]() * scale, own_ref, other_ref, at)


def stage_d_kernel(
    scale, s_ref, weighted_ref, diagonal_ref, s1_ref, s1b_ref, s3_ref, own_ref, other_ref
):
    z, core = lax.axis_index("snap"), lax.axis_index("cells") % 2
    rows = s3_ref.shape[1]
    across = z ^ 2
    mine = pl.ds(pl.multiple_of(z * rows, rows), rows)
    more = pl.ds(pl.multiple_of(across * rows, rows), rows)
    diagonal = diagonal_ref[z]
    s0, w0 = flat(s_ref[:, mine, :]), flat(weighted_ref[:, mine, :])
    s0b, w0b = flat(s_ref[:, more, :]), flat(weighted_ref[:, more, :])
    s1, s1b, s3 = flat(s1_ref[...]), flat(s1b_ref[...]), flat(s3_ref[...])
    w1, w3 = weigh(diagonal, s1_ref[...]), weigh(diagonal, s3_ref[...])
    w1b = weigh(diagonal_ref[across], s1b_ref[...])
    blocks = {
        (1, 0): lambda: tdot(s1, w0) + tdot(s1b, w0b),
        (3, 0): lambda: tdot(s3, w0),
        (0, 1): lambda: tdot(s0, w1) + tdot(s0b, w1b),
        (3, 1): lambda: tdot(s3, w1),
        (0, 3): lambda: tdot(s0, w3),
        (1, 3): lambda: tdot(s1, w3),
    }
    for at, name in enumerate(STAGE_D):
        put(core, blocks[name]() * scale, own_ref, other_ref, at)


def call(kernel, outs, flops, name, *args, smem=(), scratch=()):
    vmem, scalar = pl.BlockSpec(memory_space=pltpu.VMEM), pl.BlockSpec(memory_space=pltpu.SMEM)
    return pl.pallas_call(
        kernel,
        out_shape=[jax.ShapeDtypeStruct(s, t) for s, t in outs],
        in_specs=[scalar if k in smem else vmem for k in range(len(args))],
        out_specs=[vmem] * len(outs),
        scratch_shapes=scratch,
        compiler_params=pltpu.CompilerParams(vmem_limit_bytes=40 * 2**20),
        cost_estimate=pl.CostEstimate(flops=flops, bytes_accessed=4 * 2**20, transcendentals=0),
        name=name,
    )(*args)


def fast(snapshots, mass_blocks, block_offsets):
    components, cell_rows, columns = snapshots.shape
    planes, devices = lax.axis_size("snap"), lax.axis_size("cells")
    rows, half = cell_rows // planes, columns // 2
    scale = 1.0 / float(components * cell_rows * devices)
    z, cells = lax.axis_index("snap"), lax.axis_index("cells")
    q = (cells // 2) ^ z

    def to_plane(array, m):
        return lax.ppermute(array, "snap", [(i, i ^ m) for i in range(planes)])

    def rows_of(m):
        return lax.dynamic_slice_in_dim(snapshots, (z ^ m) * rows, rows, axis=1)

    def send(array, m, k, wanted):
        pairs = []
        for c in range(devices):
            for i in range(planes):
                to_c, to_i = c ^ (2 * m), i ^ k
                if ((to_c // 2) ^ to_i) in wanted:
                    pairs.append((c * planes + i, to_c * planes + to_i))
        return lax.ppermute(array, ("cells", "snap"), pairs)

    out2, out1, out3 = rows_of(2), rows_of(1), rows_of(3)
    s2 = to_plane(out2, 2)
    s1 = to_plane(out1, 1)
    s3 = to_plane(out3, 3)
    s1b = to_plane(out3, 1)

    diagonal, weighted, gram = call(
        early_kernel,
        [((planes, rows, rows), BF16), (snapshots.shape, BF16), ((columns, columns), F32)],
        2 * 2 * components * cell_rows * columns * columns,
        "early",
        block_offsets,
        mass_blocks,
        snapshots,
        smem=(0,),
        scratch=[pltpu.SMEM((mass_blocks.shape[0],), jnp.int32)],
    )

    def reduced(own, other, starts, wanted):
        arrived = lax.ppermute(other, "cells", [(c, c ^ 1) for c in range(devices)])

        def window(to):
            start = jnp.asarray(starts, jnp.int32)[to]
            return lax.dynamic_slice_in_dim(own, start, 2, 0) + lax.dynamic_slice_in_dim(
                arrived, start, 2, 0
            )

        total = window(q)
        for m in (1, 2, 3):
            total += send(window(q ^ m), m, 0, wanted)
        return total

    def stage(kernel, blocks, name, *args):
        shape = (len(blocks), columns, half)
        return call(
            functools.partial(kernel, scale),
            [(shape, F32), (shape, F32)],
            2 * len(blocks) * components * rows * columns * columns,
            name,
            *args,
        )

    own, other = stage(
        stage_c_kernel, STAGE_C, "stage_c", snapshots, weighted, diagonal, gram, s1, s2
    )
    sum_c = reduced(own, other, START_C, (0, 1, 2))
    from2 = send(jnp.where(q == 0, sum_c[1], sum_c[0]), 0, 2, (2, 3))
    own, other = stage(
        stage_d_kernel, STAGE_D, "stage_d", snapshots, weighted, diagonal, s1, s1b, s3
    )
    sum_d = reduced(own, other, START_D, (0, 1, 3))
    keep = jnp.where(q % 2 == 0, sum_c[0], sum_d[0])
    keep = jnp.where(q == 2, sum_c[0], keep)
    one = jnp.where(q == 0, sum_d[0], jnp.where(q == 2, sum_c[1], sum_d[1]))
    from1 = send(one, 0, 1, (1, 2, 3))
    from3 = send(sum_d[1], 0, 3, (2, 3))
    return keep + from1 + from2 + from3


def solution(mesh):
    fits = mesh.shape["cells"] == 8 and mesh.shape["snap"] == 4
    placed = (P(None, "cells", "snap"), P("cells", None, None), P("cells"))
    return jax.shard_map(
        fast if fits else general,
        mesh=mesh,
        in_specs=placed,
        out_specs=P("snap", "cells"),
        check_vma=False,
    )
```

time: 177 us -> 104 us (0.59)
  the two profiles are of different devices: /device:TPU:4 before, /device:TPU:18 now
where the time goes in v1:
time: 104 us; the launch traced here: 103 us
  waiting for transfers between devices  48.7 us (47%)
  starting transfers between devices  25.5 us (25%)
  between operations  15.3 us (15%)
  Pallas kernels  6.12 us (6%)
  other arithmetic  5.13 us (5%)
  local copies, waits for them, and re-layouts  2.17 us (2%)
    ppermute x4, waiting for transfers between devices, to_plane(): return lax.ppermute(array, 'snap', [(i, i ^ m) for i in range(planes)])  28.4 us
    ppermute x9, starting transfers between devices, send(): return lax.ppermute(array, ('cells', 'snap'), pairs)  20.4 us
    ppermute x9, waiting for transfers between devices, send(): return lax.ppermute(array, ('cells', 'snap'), pairs)  20.3 us
    pallas_call x3, Pallas kernels, call(): pl.pallas_call(kernel, out_shape=[jax.ShapeDtypeStruct(s, t) for s, t in...  6.12 us
    ppermute x4, starting transfers between devices, to_plane(): return lax.ppermute(array, 'snap', [(i, i ^ m) for i in range(planes)])  5.13 us
    add x2, other arithmetic, reduced(): total += send(window(q ^ m), m, 0, wanted)  2.42 us
  transfers between devices with their start and end apart: 15, of which 9 were waited for; matrix products, arithmetic and copies ran while one was open for 4% of the time, Pallas kernels for 6%

profile of v1, /device:TPU:18, one launch (start us, length us, event | category | flops | bytes accessed | tf_op | source)
XLA Modules:
  0.0 102.9 jit_solution(6119942432265880027)
XLA Ops:
  0.0 0.0 copy-start
  0.0 0.0 copy-start.1
  0.0 0.0 copy-start.2
  0.0 1.4 %constant_dynamic-slice_fusion.1 = (bf16[3,256,256]{2,1,0:T(8,128)(2,1)S(1)}, bf16[3,256,256]{2,1,0:T(8,128)(2,1)S(1)}, bf16[3,256,256]{2,1,0:T(8,128)(2,1)S(1)}) fusion(bf16[3,1024,256]{2,1,0:T(8,128)(2,1)} %s_ref.5, s32[]{:T(128)S(6)} %select_n.99, s32[]{:T(128)S(6)} %select_n.98, s32[]{:T(128)S(6)} %select_n.110), kind=kLoop, calls=%fused_computation.19 | loop fusion | bytes 2359308 | tf_op jit(solution)/shard_map/dynamic_slice | solution.py:169
  1.5 1.6 %collective-permute-start = (bf16[3,256,256]{2,1,0:T(8,128)(2,1)S(1)}, bf16[3,256,256]{2,1,0:T(8,128)(2,1)S(1)}, u32[]{:S(2)}, u32[]{:S(2)}) collective-permute-start(bf16[3,256,256]{2,1,0:T(8,128)(2,1)S(1)} %get-tuple-element.20), channel_id=1, source_target_pairs={{0,1},{1,0},{2,3},{3,2},{4,5},{5,4},{6,7},{7,6},{8,9},{9,8},{10,11... | collective-permute-start | bytes 1179656 | tf_op jit(solution)/shard_map/ppermute | solution.py:166
  3.1 0.3 collective-permute-start.1
  3.5 0.4 collective-permute-start.6
  3.9 2.7 %collective-permute-start.7 = (bf16[3,256,256]{2,1,0:T(8,128)(2,1)S(1)}, bf16[3,256,256]{2,1,0:T(8,128)(2,1)S(1)}, u32[]{:S(2)}, u32[]{:S(2)}) collective-permute-start(bf16[3,256,256]{2,1,0:T(8,128)(2,1)S(1)} %get-tuple-element.21), channel_id=1, source_target_pairs={{0,3},{1,2},{2,1},{3,0},{4,7},{5,6},{6,5},{7,4},{8,11},{9,10},{10,... | collective-permute-start | bytes 1179656 | tf_op jit(solution)/shard_map/ppermute | solution.py:166
  6.6 0.0 copy-done
  6.6 0.0 copy-done.1
  6.6 0.0 copy-done.2
  6.6 2.3 %early.1 = (bf16[4,256,256]{2,1,0:T(8,128)(2,1)S(1)}, bf16[3,1024,256]{2,1,0:T(8,128)(2,1)S(1)}, f32[256,256]{1,0:T(8,128)S(1)}) custom-call(s32[16]{0:T(128)S(1)} %copy-done.2, bf16[16,64,64]{2,1,0:T(8,128)(2,1)S(1)} %copy-done.1, bf16[3,1024,256]{2,1,0:T(8,128)(2,1)S(1)} %copy-done), custom_call_target="tpu_custom_call" | custom-call | flops 805306368 | bytes 4194304 | tf_op jit(solution)/shard_map/early/pallas_call | solution.py:145
  8.9 10.9 %collective-permute-done.s1_ref = bf16[3,256,256]{2,1,0:T(8,128)(2,1)S(1)} collective-permute-done((bf16[3,256,256]{2,1,0:T(8,128)(2,1)S(1)}, bf16[3,256,256]{2,1,0:T(8,128)(2,1)S(1)}, u32[]{:S(2)}, u32[]{:S(2)}) %collective-permute-start) | collective-permute-done | bytes 393248 | tf_op jit(solution)/shard_map/ppermute | solution.py:166
  19.8 2.1 %collective-permute-done.1.s2_ref = bf16[3,256,256]{2,1,0:T(8,128)(2,1)S(1)} collective-permute-done((bf16[3,256,256]{2,1,0:T(8,128)(2,1)S(1)}, bf16[3,256,256]{2,1,0:T(8,128)(2,1)S(1)}, u32[]{:S(2)}, u32[]{:S(2)}) %collective-permute-start.1) | collective-permute-done | bytes 393248 | tf_op jit(solution)/shard_map/ppermute | solution.py:166
  21.9 1.6 %stage_c.1 = (f32[5,256,128]{2,1,0:T(8,128)S(1)}, f32[5,256,128]{2,1,0:T(8,128)}) custom-call(bf16[3,1024,256]{2,1,0:T(8,128)(2,1)S(1)} %copy-done, bf16[3,1024,256]{2,1,0:T(8,128)(2,1)S(1)} %get-tuple-element.12.weighted_ref, bf16[4,256,256]{2,1,0:T(8,128)(2,1)S(1)} %get-tuple-element.13.diagonal_ref, f32[256,256]{1,0:T(8,128)S(1)} %get-tuple-element.14.gram_ref, ...), custom_call_target="tpu_custom_call" | custom-call | flops 503316480 | bytes 4194304 | tf_op jit(solution)/shard_map/stage_c/pallas_call | solution.py:145
  23.5 0.0 copy-start.3
  23.5 0.0 copy-start.4
  23.5 0.0 collective-permute-start.2
  23.6 6.9 %collective-permute-done.6.s1b_ref = bf16[3,256,256]{2,1,0:T(8,128)(2,1)S(1)} collective-permute-done((bf16[3,256,256]{2,1,0:T(8,128)(2,1)S(1)}, bf16[3,256,256]{2,1,0:T(8,128)(2,1)S(1)}, u32[]{:S(2)}, u32[]{:S(2)}) %collective-permute-start.6) | collective-permute-done | bytes 393248 | tf_op jit(solution)/shard_map/ppermute | solution.py:166
  30.5 8.5 %collective-permute-done.7.s3_ref = bf16[3,256,256]{2,1,0:T(8,128)(2,1)S(1)} collective-permute-done((bf16[3,256,256]{2,1,0:T(8,128)(2,1)S(1)}, bf16[3,256,256]{2,1,0:T(8,128)(2,1)S(1)}, u32[]{:S(2)}, u32[]{:S(2)}) %collective-permute-start.7) | collective-permute-done | bytes 393248 | tf_op jit(solution)/shard_map/ppermute | solution.py:166
  38.9 2.2 %stage_d.1 = (f32[6,256,128]{2,1,0:T(8,128)S(1)}, f32[6,256,128]{2,1,0:T(8,128)}) custom-call(bf16[3,1024,256]{2,1,0:T(8,128)(2,1)S(1)} %copy-done, bf16[3,1024,256]{2,1,0:T(8,128)(2,1)S(1)} %get-tuple-element.12.weighted_ref, bf16[4,256,256]{2,1,0:T(8,128)(2,1)S(1)} %get-tuple-element.13.diagonal_ref, bf16[3,256,256]{2,1,0:T(8,128)(2,1)S(1)} %collective-permute-done.s1_ref, ...), custom_call_target="tpu_custom_call" | custom-call | flops 603979776 | bytes 4194304 | tf_op jit(solution)/shard_map/stage_d/pallas_call | solution.py:145
  41.1 0.0 collective-permute-start.8
  41.1 0.0 copy-done.3
  41.1 0.0 copy-done.4
  41.1 0.7 fusion.4
  47.2 0.0 collective-permute-done.2
  47.2 1.2 %dynamic-slice_add_fusion.5 = (f32[2,256,128]{2,1,0:T(8,128)S(1)}, f32[2,256,128]{2,1,0:T(8,128)S(1)}, f32[2,256,128]{2,1,0:T(8,128)S(1)}) fusion(f32[5,256,128]{2,1,0:T(8,128)} %collective-permute-done.2, s32[]{:T(128)S(6)} %select_n.103, f32[5,256,128]{2,1,0:T(8,128)S(1)} %get-tuple-element.15, s32[]{:T(128)S(6)} %select_n.107, s32[]{:T(128)S(6)} %select_n.105), kind=kLoop, calls=%fused_computation.7 | loop fusion | flops 196608 | bytes 2359308 | tf_op jit(solution)/shard_map/add | solution.py:203
  48.4 3.1 %collective-permute-start.3 = (f32[2,256,128]{2,1,0:T(8,128)S(1)}, f32[2,256,128]{2,1,0:T(8,128)}, u32[]{:S(2)}, u32[]{:S(2)}) collective-permute-start(f32[2,256,128]{2,1,0:T(8,128)S(1)} %get-tuple-element.25), channel_id=1, source_target_pairs={{0,8},{1,9},{3,11},{4,12},{5,13},{7,15},{8,0},{9,1},{10,2},{12,4},... | collective-permute-start | bytes 786440 | tf_op jit(solution)/shard_map/ppermute | solution.py:178
  51.6 3.5 %collective-permute-start.4 = (f32[2,256,128]{2,1,0:T(8,128)S(1)}, f32[2,256,128]{2,1,0:T(8,128)}, u32[]{:S(2)}, u32[]{:S(2)}) collective-permute-start(f32[2,256,128]{2,1,0:T(8,128)S(1)} %get-tuple-element.27), channel_id=1, source_target_pairs={{0,16},{2,18},{3,19},{4,20},{6,22},{7,23},{9,25},{10,26},{11,27},{... | collective-permute-start | bytes 786440 | tf_op jit(solution)/shard_map/ppermute | solution.py:178
  55.1 2.8 %collective-permute-start.5 = (f32[2,256,128]{2,1,0:T(8,128)S(1)}, f32[2,256,128]{2,1,0:T(8,128)}, u32[]{:S(2)}, u32[]{:S(2)}) collective-permute-start(f32[2,256,128]{2,1,0:T(8,128)S(1)} %get-tuple-element.26), channel_id=1, source_target_pairs={{1,25},{2,26},{3,27},{5,29},{6,30},{7,31},{8,16},{10,18},{11,19},{... | collective-permute-start | bytes 786440 | tf_op jit(solution)/shard_map/ppermute | solution.py:178
  63.9 0.0 collective-permute-done.8
  63.9 0.8 dynamic-slice_add_fusion.2
  64.7 3.2 %collective-permute-start.10 = (f32[2,256,128]{2,1,0:T(8,128)}, f32[2,256,128]{2,1,0:T(8,128)}, u32[]{:S(2)}, u32[]{:S(2)}) collective-permute-start(f32[2,256,128]{2,1,0:T(8,128)} %get-tuple-element.24), channel_id=1, source_target_pairs={{1,17},{2,18},{3,19},{5,21},{6,22},{7,23},{8,24},{10,26},{11,27},{... | collective-permute-start | bytes 786440 | tf_op jit(solution)/shard_map/ppermute | solution.py:178
  67.9 1.9 %collective-permute-start.11 = (f32[2,256,128]{2,1,0:T(8,128)S(1)}, f32[2,256,128]{2,1,0:T(8,128)}, u32[]{:S(2)}, u32[]{:S(2)}) collective-permute-start(f32[2,256,128]{2,1,0:T(8,128)S(1)} %get-tuple-element.23), channel_id=1, source_target_pairs={{0,24},{2,26},{3,27},{4,28},{6,30},{7,31},{9,17},{10,18},{11,19},{... | collective-permute-start | bytes 786440 | tf_op jit(solution)/shard_map/ppermute | solution.py:178
  69.9 0.0 collective-permute-done.3
  69.9 1.3 %collective-permute-start.9 = (f32[2,256,128]{2,1,0:T(8,128)S(1)}, f32[2,256,128]{2,1,0:T(8,128)}, u32[]{:S(2)}, u32[]{:S(2)}) collective-permute-start(f32[2,256,128]{2,1,0:T(8,128)S(1)} %get-tuple-element.22), channel_id=1, source_target_pairs={{0,8},{1,9},{2,10},{4,12},{5,13},{6,14},{8,0},{9,1},{11,3},{12,4},... | collective-permute-start | bytes 786440 | tf_op jit(solution)/shard_map/ppermute | solution.py:178
  74.8 0.0 collective-permute-done.4
  74.8 0.0 collective-permute-done.5
  74.8 1.3 %add_add_fusion.1 = f32[2,256,128]{2,1,0:T(8,128)S(1)} fusion(f32[2,256,128]{2,1,0:T(8,128)} %collective-permute-done.5, f32[2,256,128]{2,1,0:T(8,128)} %collective-permute-done.4, f32[2,256,128]{2,1,0:T(8,128)} %collective-permute-done.3, f32[5,256,128]{2,1,0:T(8,128)} %collective-permute-done.2, s32[]{:T(128)S(6)} %select_n.101, ...), kind=kLoop, calls=%fused_computation.5 | loop fusion | flops 262144 | bytes 1572868 | tf_op jit(solution)/shard_map/add | solution.py:209
  76.1 4.6 %collective-permute-done.10 = f32[2,256,128]{2,1,0:T(8,128)} collective-permute-done((f32[2,256,128]{2,1,0:T(8,128)}, f32[2,256,128]{2,1,0:T(8,128)}, u32[]{:S(2)}, u32[]{:S(2)}) %collective-permute-start.10) | collective-permute-done | bytes 262176 | tf_op jit(solution)/shard_map/ppermute | solution.py:178
  80.7 0.0 collective-permute-done.11
  80.7 2.9 %collective-permute-done.9 = f32[2,256,128]{2,1,0:T(8,128)} collective-permute-done((f32[2,256,128]{2,1,0:T(8,128)S(1)}, f32[2,256,128]{2,1,0:T(8,128)}, u32[]{:S(2)}, u32[]{:S(2)}) %collective-permute-start.9) | collective-permute-done | bytes 262176 | tf_op jit(solution)/shard_map/ppermute | solution.py:178
  83.6 1.2 %add_add_fusion = f32[2,256,128]{2,1,0:T(8,128)S(1)} fusion(f32[2,256,128]{2,1,0:T(8,128)} %collective-permute-done.11, f32[2,256,128]{2,1,0:T(8,128)} %collective-permute-done.10, f32[2,256,128]{2,1,0:T(8,128)} %collective-permute-done.9, f32[6,256,128]{2,1,0:T(8,128)S(1)} %collective-permute-done.8, s32[]{:T(128)S(6)} %select_n.111, ...), kind=kLoop, calls=%fused_computation.1 | loop fusion | flops 262144 | bytes 1572868 | tf_op jit(solution)/shard_map/add | solution.py:209
  84.9 1.9 %collective-permute-start.12 = (f32[256,128]{1,0:T(8,128)S(1)}, f32[256,128]{1,0:T(8,128)S(1)}, u32[]{:S(2)}, u32[]{:S(2)}) collective-permute-start(f32[256,128]{1,0:T(8,128)S(1)} %get-tuple-element.28), channel_id=1, source_target_pairs={{0,1},{2,3},{3,2},{4,5},{6,7},{7,6},{9,8},{10,11},{11,10},{13,12},... | collective-permute-start | bytes 393224 | tf_op jit(solution)/shard_map/ppermute | solution.py:178
  86.8 1.3 %collective-permute-start.13 = (f32[256,128]{1,0:T(8,128)S(1)}, f32[256,128]{1,0:T(8,128)S(1)}, u32[]{:S(2)}, u32[]{:S(2)}) collective-permute-start(f32[256,128]{1,0:T(8,128)S(1)} %get-tuple-element.29), channel_id=1, source_target_pairs={{0,2},{1,3},{4,6},{5,7},{8,10},{9,11},{12,14},{13,15},{18,16},{19,... | collective-permute-start | bytes 393224 | tf_op jit(solution)/shard_map/ppermute | solution.py:178
  88.1 1.3 %collective-permute-start.14 = (f32[256,128]{1,0:T(8,128)S(1)}, f32[256,128]{1,0:T(8,128)S(1)}, u32[]{:S(2)}, u32[]{:S(2)}) collective-permute-start(f32[256,128]{1,0:T(8,128)S(1)} %slice_bitcast_fusion), channel_id=1, source_target_pairs={{0,3},{1,2},{4,7},{5,6},{8,11},{9,10},{12,15},{13,14},{18,17},{19,... | collective-permute-start | bytes 393224 | tf_op jit(solution)/shard_map/ppermute | solution.py:178
  89.4 2.3 %collective-permute-done.12 = f32[256,128]{1,0:T(8,128)S(1)} collective-permute-done((f32[256,128]{1,0:T(8,128)S(1)}, f32[256,128]{1,0:T(8,128)S(1)}, u32[]{:S(2)}, u32[]{:S(2)}) %collective-permute-start.12) | collective-permute-done | bytes 131104 | tf_op jit(solution)/shard_map/ppermute | solution.py:178
  91.7 4.0 %collective-permute-done.13 = f32[256,128]{1,0:T(8,128)S(1)} collective-permute-done((f32[256,128]{1,0:T(8,128)S(1)}, f32[256,128]{1,0:T(8,128)S(1)}, u32[]{:S(2)}, u32[]{:S(2)}) %collective-permute-start.13) | collective-permute-done | bytes 131104 | tf_op jit(solution)/shard_map/ppermute | solution.py:178
  95.7 6.5 %collective-permute-done.14 = f32[256,128]{1,0:T(8,128)S(1)} collective-permute-done((f32[256,128]{1,0:T(8,128)S(1)}, f32[256,128]{1,0:T(8,128)S(1)}, u32[]{:S(2)}, u32[]{:S(2)}) %collective-permute-start.14) | collective-permute-done | bytes 131104 | tf_op jit(solution)/shard_map/ppermute | solution.py:178
  102.2 0.7 fusion.2
  (2 shorter events, 0.0 us)
Async XLA Ops:
  0.0 6.6 %copy-start = (bf16[3,1024,256]{2,1,0:T(8,128)(2,1)S(1)}, bf16[3,1024,256]{2,1,0:T(8,128)(2,1)}, u32[]{:S(2)}) copy-start(bf16[3,1024,256]{2,1,0:T(8,128)(2,1)} %s_ref.5) | copy-start | bytes 4718596
  0.0 6.6 %copy-start.1 = (bf16[16,64,64]{2,1,0:T(8,128)(2,1)S(1)}, bf16[16,64,64]{2,1,0:T(8,128)(2,1)}, u32[]{:S(2)}) copy-start(bf16[16,64,64]{2,1,0:T(8,128)(2,1)} %mass_ref.1) | copy-start | bytes 393220
  0.0 6.6 %copy-start.2 = (s32[16]{0:T(128)S(1)}, s32[16]{0:T(128)}, u32[]{:S(2)}) copy-start(s32[16]{0:T(128)} %offsets_ref.1) | copy-start | bytes 196
  1.5 18.3 %collective-permute-start = (bf16[3,256,256]{2,1,0:T(8,128)(2,1)S(1)}, bf16[3,256,256]{2,1,0:T(8,128)(2,1)S(1)}, u32[]{:S(2)}, u32[]{:S(2)}) collective-permute-start(bf16[3,256,256]{2,1,0:T(8,128)(2,1)S(1)} %get-tuple-element.20), channel_id=1, source_target_pairs={{0,1},{1,0},{2,3},{3,2},{4,5},{5,4},{6,7},{7,6},{8,9},{9,8},{10,11... | collective-permute-start | bytes 1179656 | tf_op jit(solution)/shard_map/ppermute | solution.py:166
  3.1 18.8 %collective-permute-start.1 = (bf16[3,256,256]{2,1,0:T(8,128)(2,1)S(1)}, bf16[3,256,256]{2,1,0:T(8,128)(2,1)S(1)}, u32[]{:S(2)}, u32[]{:S(2)}) collective-permute-start(bf16[3,256,256]{2,1,0:T(8,128)(2,1)S(1)} %get-tuple-element.19), channel_id=1, source_target_pairs={{0,2},{1,3},{2,0},{3,1},{4,6},{5,7},{6,4},{7,5},{8,10},{9,11},{10,... | collective-permute-start | bytes 1179656 | tf_op jit(solution)/shard_map/ppermute | solution.py:166
  3.5 27.0 %collective-permute-start.6 = (bf16[3,256,256]{2,1,0:T(8,128)(2,1)S(1)}, bf16[3,256,256]{2,1,0:T(8,128)(2,1)S(1)}, u32[]{:S(2)}, u32[]{:S(2)}) collective-permute-start(bf16[3,256,256]{2,1,0:T(8,128)(2,1)S(1)} %get-tuple-element.21), channel_id=1, source_target_pairs={{0,1},{1,0},{2,3},{3,2},{4,5},{5,4},{6,7},{7,6},{8,9},{9,8},{10,11... | collective-permute-start | bytes 1179656 | tf_op jit(solution)/shard_map/ppermute | solution.py:166
  3.9 35.0 %collective-permute-start.7 = (bf16[3,256,256]{2,1,0:T(8,128)(2,1)S(1)}, bf16[3,256,256]{2,1,0:T(8,128)(2,1)S(1)}, u32[]{:S(2)}, u32[]{:S(2)}) collective-permute-start(bf16[3,256,256]{2,1,0:T(8,128)(2,1)S(1)} %get-tuple-element.21), channel_id=1, source_target_pairs={{0,3},{1,2},{2,1},{3,0},{4,7},{5,6},{6,5},{7,4},{8,11},{9,10},{10,... | collective-permute-start | bytes 1179656 | tf_op jit(solution)/shard_map/ppermute | solution.py:166
  23.5 17.6 %copy-start.3 = (s32[4]{0:T(128)S(1)}, s32[4]{0:T(128)}, u32[]{:S(2)}) copy-start(s32[4]{0:T(128)} %constant.51.clone) | copy-start | bytes 52
  23.5 17.6 %copy-start.4 = (s32[4]{0:T(128)S(1)}, s32[4]{0:T(128)}, u32[]{:S(2)}) copy-start(s32[4]{0:T(128)} %constant.52.clone) | copy-start | bytes 52
  23.5 23.7 %collective-permute-start.2 = (f32[5,256,128]{2,1,0:T(8,128)}, f32[5,256,128]{2,1,0:T(8,128)}, u32[]{:S(2)}, u32[]{:S(2)}) collective-permute-start(f32[5,256,128]{2,1,0:T(8,128)} %get-tuple-element.16), channel_id=1, source_target_pairs={{0,4},{4,0},{8,12},{12,8},{16,20},{20,16},{24,28},{28,24},{1,5},{5... | collective-permute-start | bytes 1966088 | tf_op jit(solution)/shard_map/ppermute | solution.py:199
  41.1 22.8 %collective-permute-start.8 = (f32[6,256,128]{2,1,0:T(8,128)}, f32[6,256,128]{2,1,0:T(8,128)S(1)}, u32[]{:S(2)}, u32[]{:S(2)}) collective-permute-start(f32[6,256,128]{2,1,0:T(8,128)} %get-tuple-element.18), channel_id=1, source_target_pairs={{0,4},{4,0},{8,12},{12,8},{16,20},{20,16},{24,28},{28,24},{1,5},{5... | collective-permute-start | bytes 2359304 | tf_op jit(solution)/shard_map/ppermute | solution.py:199
  48.4 21.4 %collective-permute-start.3 = (f32[2,256,128]{2,1,0:T(8,128)S(1)}, f32[2,256,128]{2,1,0:T(8,128)}, u32[]{:S(2)}, u32[]{:S(2)}) collective-permute-start(f32[2,256,128]{2,1,0:T(8,128)S(1)} %get-tuple-element.25), channel_id=1, source_target_pairs={{0,8},{1,9},{3,11},{4,12},{5,13},{7,15},{8,0},{9,1},{10,2},{12,4},... | collective-permute-start | bytes 786440 | tf_op jit(solution)/shard_map/ppermute | solution.py:178
  51.6 23.2 %collective-permute-start.4 = (f32[2,256,128]{2,1,0:T(8,128)S(1)}, f32[2,256,128]{2,1,0:T(8,128)}, u32[]{:S(2)}, u32[]{:S(2)}) collective-permute-start(f32[2,256,128]{2,1,0:T(8,128)S(1)} %get-tuple-element.27), channel_id=1, source_target_pairs={{0,16},{2,18},{3,19},{4,20},{6,22},{7,23},{9,25},{10,26},{11,27},{... | collective-permute-start | bytes 786440 | tf_op jit(solution)/shard_map/ppermute | solution.py:178
  55.1 19.7 %collective-permute-start.5 = (f32[2,256,128]{2,1,0:T(8,128)S(1)}, f32[2,256,128]{2,1,0:T(8,128)}, u32[]{:S(2)}, u32[]{:S(2)}) collective-permute-start(f32[2,256,128]{2,1,0:T(8,128)S(1)} %get-tuple-element.26), channel_id=1, source_target_pairs={{1,25},{2,26},{3,27},{5,29},{6,30},{7,31},{8,16},{10,18},{11,19},{... | collective-permute-start | bytes 786440 | tf_op jit(solution)/shard_map/ppermute | solution.py:178
  64.7 16.0 %collective-permute-start.10 = (f32[2,256,128]{2,1,0:T(8,128)}, f32[2,256,128]{2,1,0:T(8,128)}, u32[]{:S(2)}, u32[]{:S(2)}) collective-permute-start(f32[2,256,128]{2,1,0:T(8,128)} %get-tuple-element.24), channel_id=1, source_target_pairs={{1,17},{2,18},{3,19},{5,21},{6,22},{7,23},{8,24},{10,26},{11,27},{... | collective-permute-start | bytes 786440 | tf_op jit(solution)/shard_map/ppermute | solution.py:178
  67.9 12.8 %collective-permute-start.11 = (f32[2,256,128]{2,1,0:T(8,128)S(1)}, f32[2,256,128]{2,1,0:T(8,128)}, u32[]{:S(2)}, u32[]{:S(2)}) collective-permute-start(f32[2,256,128]{2,1,0:T(8,128)S(1)} %get-tuple-element.23), channel_id=1, source_target_pairs={{0,24},{2,26},{3,27},{4,28},{6,30},{7,31},{9,17},{10,18},{11,19},{... | collective-permute-start | bytes 786440 | tf_op jit(solution)/shard_map/ppermute | solution.py:178
  69.9 13.7 %collective-permute-start.9 = (f32[2,256,128]{2,1,0:T(8,128)S(1)}, f32[2,256,128]{2,1,0:T(8,128)}, u32[]{:S(2)}, u32[]{:S(2)}) collective-permute-start(f32[2,256,128]{2,1,0:T(8,128)S(1)} %get-tuple-element.22), channel_id=1, source_target_pairs={{0,8},{1,9},{2,10},{4,12},{5,13},{6,14},{8,0},{9,1},{11,3},{12,4},... | collective-permute-start | bytes 786440 | tf_op jit(solution)/shard_map/ppermute | solution.py:178
  84.9 6.9 %collective-permute-start.12 = (f32[256,128]{1,0:T(8,128)S(1)}, f32[256,128]{1,0:T(8,128)S(1)}, u32[]{:S(2)}, u32[]{:S(2)}) collective-permute-start(f32[256,128]{1,0:T(8,128)S(1)} %get-tuple-element.28), channel_id=1, source_target_pairs={{0,1},{2,3},{3,2},{4,5},{6,7},{7,6},{9,8},{10,11},{11,10},{13,12},... | collective-permute-start | bytes 393224 | tf_op jit(solution)/shard_map/ppermute | solution.py:178
  86.8 9.0 %collective-permute-start.13 = (f32[256,128]{1,0:T(8,128)S(1)}, f32[256,128]{1,0:T(8,128)S(1)}, u32[]{:S(2)}, u32[]{:S(2)}) collective-permute-start(f32[256,128]{1,0:T(8,128)S(1)} %get-tuple-element.29), channel_id=1, source_target_pairs={{0,2},{1,3},{4,6},{5,7},{8,10},{9,11},{12,14},{13,15},{18,16},{19,... | collective-permute-start | bytes 393224 | tf_op jit(solution)/shard_map/ppermute | solution.py:178
  88.1 14.1 %collective-permute-start.14 = (f32[256,128]{1,0:T(8,128)S(1)}, f32[256,128]{1,0:T(8,128)S(1)}, u32[]{:S(2)}, u32[]{:S(2)}) collective-permute-start(f32[256,128]{1,0:T(8,128)S(1)} %slice_bitcast_fusion), channel_id=1, source_target_pairs={{0,3},{1,2},{4,7},{5,6},{8,11},{9,10},{12,15},{13,14},{18,17},{19,... | collective-permute-start | bytes 393224 | tf_op jit(solution)/shard_map/ppermute | solution.py:178

commit v2 on v1

--- a/solution.py
+++ b/solution.py
@@ -140,6 +140,80 @@
         put(core, blocks[name]() * scale, own_ref, other_ref, at)
 
 
+GROUP = 64
+TAIL = 16
+STEPS = 256.0
+TOP = 32700.0
+
+
+def encode(value, message_ref):
+    slots, rows, columns = value.shape
+    groups = slots * rows // GROUP
+    value = value.reshape(groups, GROUP, columns)
+    most = jnp.maximum(jnp.max(jnp.abs(value), axis=1), 1e-36)
+    step = jnp.ceil(jnp.log2(most) * STEPS)
+    code = jnp.round(value * (TOP * jnp.exp2(step * (-1.0 / STEPS)))[:, None, :])
+    codes = code.reshape(slots * rows, columns).astype(jnp.int32).astype(jnp.int16)
+    message_ref[: slots * rows] = codes
+    step = jnp.concatenate([step, jnp.zeros((TAIL - groups, columns), F32)], axis=0)
+    message_ref[slots * rows :] = step.astype(jnp.int32).astype(jnp.int16)
+
+
+def decode(message_ref, slots):
+    total, columns = message_ref.shape
+    rows = (total - TAIL) // slots
+    groups = slots * rows // GROUP
+    step = message_ref[slots * rows :].astype(jnp.int32).astype(F32)[:groups]
+    code = message_ref[: slots * rows].astype(jnp.int32).astype(F32)
+    value = code.reshape(groups, GROUP, columns) * (jnp.exp2(step * (1.0 / STEPS)) * (1.0 / TOP))[:, None, :]
+    return value.reshape(slots, rows, columns)
+
+
+def place():
+    return (lax.axis_index("cells") // 2) ^ lax.axis_index("snap")
+
+
+def combine_kernel(starts, own_ref, arrived_ref, total_ref, *message_refs):
+    q = place()
+    for m, ref in enumerate((total_ref, *message_refs)):
+        to = q ^ m
+        start = jnp.where(
+            to == 0, starts[0], jnp.where(to == 1, starts[1], jnp.where(to == 2, starts[2], starts[3]))
+        )
+        value = own_ref[pl.ds(start, 2)] + arrived_ref[pl.ds(start, 2)]
+        if m == 0:
+            ref[...] = value
+        else:
+            encode(value, ref)
+
+
+def plane_sum(total_ref, message_refs):
+    total = total_ref[...]
+    for ref in message_refs:
+        total += decode(ref, 2)
+    return total
+
+
+def plane_c_kernel(total_ref, m1_ref, m2_ref, m3_ref, sum_ref, two_ref):
+    total = plane_sum(total_ref, (m1_ref, m2_ref, m3_ref))
+    sum_ref[...] = total
+    encode(jnp.where(place() == 0, total[1:], total[:1]), two_ref)
+
+
+def plane_d_kernel(total_ref, m1_ref, m2_ref, m3_ref, sum_c_ref, keep_ref, one_ref, three_ref):
+    q = place()
+    total = plane_sum(total_ref, (m1_ref, m2_ref, m3_ref))
+    encode(jnp.where(q == 0, total[:1], jnp.where(q == 2, sum_c_ref[1:], total[1:])), one_ref)
+    encode(total[1:], three_ref)
+    keep_ref[...] = jnp.where(q % 2 == 0, sum_c_ref[0], total[0])
+
+
+def last_kernel(keep_ref, m1_ref, m2_ref, m3_ref, out_ref):
+    out_ref[...] = (
+        keep_ref[...] + decode(m1_ref, 1)[0] + decode(m2_ref, 1)[0] + decode(m3_ref, 1)[0]
+    )
+
+
 def call(kernel, outs, flops, name, *args, smem=(), scratch=()):
     vmem, scalar = pl.BlockSpec(memory_space=pltpu.VMEM), pl.BlockSpec(memory_space=pltpu.SMEM)
     return pl.pallas_call(
@@ -148,10 +222,13 @@
         in_specs=[scalar if k in smem else vmem for k in range(len(args))],
         out_specs=[vmem] * len(outs),
         scratch_shapes=scratch,
-        compiler_params=pltpu.CompilerParams(vmem_limit_bytes=40 * 2**20),
-        cost_estimate=pl.CostEstimate(flops=flops, bytes_accessed=4 * 2**20, transcendentals=0),
+        compiler_params=pltpu.CompilerParams(vmem_limit_bytes=LIMIT),
+        cost_estimate=pl.CostEstimate(flops=flops, bytes_accessed=2**20, transcendentals=0),
         name=name,
     )(*args)
+
+
+LIMIT = 24 * 2**20
 
 
 def fast(snapshots, mass_blocks, block_offsets):
@@ -159,14 +236,13 @@
     planes, devices = lax.axis_size("snap"), lax.axis_size("cells")
     rows, half = cell_rows // planes, columns // 2
     scale = 1.0 / float(components * cell_rows * devices)
-    z, cells = lax.axis_index("snap"), lax.axis_index("cells")
-    q = (cells // 2) ^ z
+    z = lax.axis_index("snap")
 
     def to_plane(array, m):
         return lax.ppermute(array, "snap", [(i, i ^ m) for i in range(planes)])
 
-    def rows_of(m):
-        return lax.dynamic_slice_in_dim(snapshots, (z ^ m) * rows, rows, axis=1)
+    def rows_of(array, m):
+        return lax.dynamic_slice_in_dim(array, (z ^ m) * rows, rows, axis=1)
 
     def send(array, m, k, wanted):
         pairs = []
@@ -177,7 +253,10 @@
                     pairs.append((c * planes + i, to_c * planes + to_i))
         return lax.ppermute(array, ("cells", "snap"), pairs)
 
-    out2, out1, out3 = rows_of(2), rows_of(1), rows_of(3)
+    out2 = rows_of(snapshots, 2)
+    later, _ = lax.optimization_barrier((snapshots, out2))
+    out1 = rows_of(later, 1)
+    out3 = rows_of(later, 3)
     s2 = to_plane(out2, 2)
     s1 = to_plane(out1, 1)
     s3 = to_plane(out3, 3)
@@ -190,24 +269,24 @@
         "early",
         block_offsets,
         mass_blocks,
-        snapshots,
+        later,
         smem=(0,),
         scratch=[pltpu.SMEM((mass_blocks.shape[0],), jnp.int32)],
     )
 
-    def reduced(own, other, starts, wanted):
+    pair, single = ((2 * columns + TAIL, half), jnp.int16), ((columns + TAIL, half), jnp.int16)
+
+    def plane(own, other, starts, wanted, name):
         arrived = lax.ppermute(other, "cells", [(c, c ^ 1) for c in range(devices)])
-
-        def window(to):
-            start = jnp.asarray(starts, jnp.int32)[to]
-            return lax.dynamic_slice_in_dim(own, start, 2, 0) + lax.dynamic_slice_in_dim(
-                arrived, start, 2, 0
-            )
-
-        total = window(q)
-        for m in (1, 2, 3):
-            total += send(window(q ^ m), m, 0, wanted)
-        return total
+        total, *out = call(
+            functools.partial(combine_kernel, starts),
+            [((2, columns, half), F32), pair, pair, pair],
+            0,
+            name,
+            own,
+            arrived,
+        )
+        return total, [send(out[m - 1], m, 0, wanted) for m in (1, 2, 3)]
 
     def stage(kernel, blocks, name, *args):
         shape = (len(blocks), columns, half)
@@ -222,18 +301,22 @@
     own, other = stage(
         stage_c_kernel, STAGE_C, "stage_c", snapshots, weighted, diagonal, gram, s1, s2
     )
-    sum_c = reduced(own, other, START_C, (0, 1, 2))
-    from2 = send(jnp.where(q == 0, sum_c[1], sum_c[0]), 0, 2, (2, 3))
+    total, arrived = plane(own, other, START_C, (0, 1, 2), "combine_c")
+    sum_c, two = call(
+        plane_c_kernel, [((2, columns, half), F32), single], 0, "plane_c", total, *arrived
+    )
+    from2 = send(two, 0, 2, (2, 3))
+    s1b, s3, sum_c = lax.optimization_barrier((s1b, s3, sum_c))
     own, other = stage(
         stage_d_kernel, STAGE_D, "stage_d", snapshots, weighted, diagonal, s1, s1b, s3
     )
-    sum_d = reduced(own, other, START_D, (0, 1, 3))
-    keep = jnp.where(q % 2 == 0, sum_c[0], sum_d[0])
-    keep = jnp.where(q == 2, sum_c[0], keep)
-    one = jnp.where(q == 0, sum_d[0], jnp.where(q == 2, sum_c[1], sum_d[1]))
+    total, arrived = plane(own, other, START_D, (0, 1, 3), "combine_d")
+    keep, one, three = call(
+        plane_d_kernel, [((columns, half), F32), single, single], 0, "plane_d", total, *arrived, sum_c
+    )
     from1 = send(one, 0, 1, (1, 2, 3))
-    from3 = send(sum_d[1], 0, 3, (2, 3))
-    return keep + from1 + from2 + from3
+    from3 = send(three, 0, 3, (2, 3))
+    return call(last_kernel, [((columns, half), F32)], 0, "last", keep, from1, from2, from3)[0]
 
 
 def solution(mesh):

time: 104 us -> 75.2 us (0.72)
  the two profiles are of different devices: /device:TPU:18 before, /device:TPU:4 now
where the time goes in v2:
time: 75.2 us; the launch traced here: 74.8 us
  waiting for transfers between devices  37.1 us (49%)
  starting transfers between devices  29.2 us (39%)
  Pallas kernels  6 us (8%)
  local copies, waits for them, and re-layouts  2.35 us (3%)
    ppermute x9, starting transfers between devices, send(): return lax.ppermute(array, ('cells', 'snap'), pairs)  22.2 us
    ppermute x4, waiting for transfers between devices, to_plane(): return lax.ppermute(array, 'snap', [(i, i ^ m) for i in range(planes)])  19.1 us
    ppermute x9, waiting for transfers between devices, send(): return lax.ppermute(array, ('cells', 'snap'), pairs)  15.7 us
    ppermute x4, starting transfers between devices, to_plane(): return lax.ppermute(array, 'snap', [(i, i ^ m) for i in range(planes)])  6.85 us
    pallas_call x8, Pallas kernels, call(): pl.pallas_call(kernel, out_shape=[jax.ShapeDtypeStruct(s, t) for s, t in...  6 us
    dynamic_slice x2, local copies, waits for them, and re-layouts, rows_of(): return lax.dynamic_slice_in_dim(array, (z ^ m) * rows, rows, axis=1)  2.34 us
    ppermute x2, waiting for transfers between devices, plane(): arrived = lax.ppermute(other, 'cells', [(c, c ^ 1) for c in range(devices)])  2.27 us
  transfers between devices with their start and end apart: 15, of which 10 were waited for; matrix products, arithmetic and copies ran while one was open for 0% of the time, Pallas kernels for 4%

profile of v2, /device:TPU:4, one launch (start us, length us, event | category | flops | bytes accessed | tf_op | source)
XLA Modules:
  0.0 74.8 jit_solution(16107277804213120868)
XLA Ops:
  0.0 0.0 copy-start
  0.0 0.0 copy-start.1
  0.0 0.0 copy-start.2
  0.0 1.2 %constant_dynamic-slice_fusion.2 = bf16[3,256,256]{2,1,0:T(8,128)(2,1)S(1)} fusion(bf16[3,1024,256]{2,1,0:T(8,128)(2,1)} %s_ref.4, s32[]{:T(128)S(6)} %select_n.9), kind=kLoop, calls=%fused_computation.2 | loop fusion | bytes 786436 | tf_op jit(solution)/shard_map/dynamic_slice | solution.py:245
  1.2 1.2 %constant_dynamic-slice_fusion = (bf16[3,256,256]{2,1,0:T(8,128)(2,1)S(1)}, bf16[3,256,256]{2,1,0:T(8,128)(2,1)S(1)}) fusion(bf16[3,1024,256]{2,1,0:T(8,128)(2,1)} %s_ref.4, s32[]{:T(128)S(6)} %select_n.11, s32[]{:T(128)S(6)} %select_n.10), kind=kLoop, calls=%fused_computation | loop fusion | bytes 1572872 | tf_op jit(solution)/shard_map/dynamic_slice | solution.py:245
  2.4 1.6 %collective-permute-start = (bf16[3,256,256]{2,1,0:T(8,128)(2,1)S(1)}, bf16[3,256,256]{2,1,0:T(8,128)(2,1)S(1)}, u32[]{:S(2)}, u32[]{:S(2)}) collective-permute-start(bf16[3,256,256]{2,1,0:T(8,128)(2,1)S(1)} %get-tuple-element.54), channel_id=1, source_target_pairs={{0,1},{1,0},{2,3},{3,2},{4,5},{5,4},{6,7},{7,6},{8,9},{9,8},{10,11... | collective-permute-start | bytes 1179656 | tf_op jit(solution)/shard_map/ppermute | solution.py:242
  4.0 2.6 %collective-permute-start.3 = (bf16[3,256,256]{2,1,0:T(8,128)(2,1)S(1)}, bf16[3,256,256]{2,1,0:T(8,128)(2,1)S(1)}, u32[]{:S(2)}, u32[]{:S(2)}) collective-permute-start(bf16[3,256,256]{2,1,0:T(8,128)(2,1)S(1)} %constant_dynamic-slice_fusion.2), channel_id=1, source_target_pairs={{0,2},{1,3},{2,0},{3,1},{4,6},{5,7},{6,4},{7,5},{8,10},{9,11},{10,... | collective-permute-start | bytes 1179656 | tf_op jit(solution)/shard_map/ppermute | solution.py:242
  6.6 0.0 copy-done
  6.6 0.0 copy-done.1
  6.6 0.0 copy-done.2
  6.6 2.3 %early.1 = (bf16[4,256,256]{2,1,0:T(8,128)(2,1)S(1)}, bf16[3,1024,256]{2,1,0:T(8,128)(2,1)S(1)}, f32[256,256]{1,0:T(8,128)S(1)}) custom-call(s32[16]{0:T(128)S(1)} %copy-done.2, bf16[16,64,64]{2,1,0:T(8,128)(2,1)S(1)} %copy-done.1, bf16[3,1024,256]{2,1,0:T(8,128)(2,1)S(1)} %copy-done), custom_call_target="tpu_custom_call" | custom-call | flops 805306368 | bytes 1048576 | tf_op jit(solution)/shard_map/early/pallas_call | solution.py:219
  8.9 12.7 %collective-permute-done.s1_ref = bf16[3,256,256]{2,1,0:T(8,128)(2,1)S(1)} collective-permute-done((bf16[3,256,256]{2,1,0:T(8,128)(2,1)S(1)}, bf16[3,256,256]{2,1,0:T(8,128)(2,1)S(1)}, u32[]{:S(2)}, u32[]{:S(2)}) %collective-permute-start) | collective-permute-done | bytes 393248 | tf_op jit(solution)/shard_map/ppermute | solution.py:242
  21.6 2.4 %collective-permute-done.3.s2_ref = bf16[3,256,256]{2,1,0:T(8,128)(2,1)S(1)} collective-permute-done((bf16[3,256,256]{2,1,0:T(8,128)(2,1)S(1)}, bf16[3,256,256]{2,1,0:T(8,128)(2,1)S(1)}, u32[]{:S(2)}, u32[]{:S(2)}) %collective-permute-start.3) | collective-permute-done | bytes 393248 | tf_op jit(solution)/shard_map/ppermute | solution.py:242
  24.0 0.8 %stage_c.1 = (f32[5,256,128]{2,1,0:T(8,128)S(1)}, f32[5,256,128]{2,1,0:T(8,128)S(1)}) custom-call(bf16[3,1024,256]{2,1,0:T(8,128)(2,1)S(1)} %copy-done, bf16[3,1024,256]{2,1,0:T(8,128)(2,1)S(1)} %get-tuple-element.30.weighted_ref, bf16[4,256,256]{2,1,0:T(8,128)(2,1)S(1)} %get-tuple-element.31.diagonal_ref, f32[256,256]{1,0:T(8,128)S(1)} %get-tuple-element.32.gram_ref, ...), custom_call_target="tpu_custom_call" | custom-call | flops 503316480 | bytes 1048576 | tf_op jit(solution)/shard_map/stage_c/pallas_call | solution.py:219
  24.8 0.1 collective-permute-start.4
  24.9 0.5 collective-permute-start.1
  25.4 2.1 %collective-permute-start.2 = (bf16[3,256,256]{2,1,0:T(8,128)(2,1)S(1)}, bf16[3,256,256]{2,1,0:T(8,128)(2,1)S(1)}, u32[]{:S(2)}, u32[]{:S(2)}) collective-permute-start(bf16[3,256,256]{2,1,0:T(8,128)(2,1)S(1)} %get-tuple-element.53), channel_id=1, source_target_pairs={{0,3},{1,2},{2,1},{3,0},{4,7},{5,6},{6,5},{7,4},{8,11},{9,10},{10,... | collective-permute-start | bytes 1179656 | tf_op jit(solution)/shard_map/ppermute | solution.py:242
  27.5 0.0 collective-permute-done.4.arrived_ref
  27.5 0.2 combine_c.1
  27.7 1.3 %collective-permute-start.5 = (s16[528,128]{1,0:T(8,128)(2,1)S(1)}, s16[528,128]{1,0:T(8,128)(2,1)S(1)}, u32[]{:S(2)}, u32[]{:S(2)}) collective-permute-start(s16[528,128]{1,0:T(8,128)(2,1)S(1)} %get-tuple-element.36), channel_id=1, source_target_pairs={{0,8},{1,9},{3,11},{4,12},{5,13},{7,15},{8,0},{9,1},{10,2},{12,4},... | collective-permute-start | bytes 405512 | tf_op jit(solution)/shard_map/ppermute | solution.py:254
  29.0 4.5 %collective-permute-start.6 = (s16[528,128]{1,0:T(8,128)(2,1)S(1)}, s16[528,128]{1,0:T(8,128)(2,1)S(1)}, u32[]{:S(2)}, u32[]{:S(2)}) collective-permute-start(s16[528,128]{1,0:T(8,128)(2,1)S(1)} %get-tuple-element.37), channel_id=1, source_target_pairs={{0,16},{2,18},{3,19},{4,20},{6,22},{7,23},{9,25},{10,26},{11,27},{... | collective-permute-start | bytes 405512 | tf_op jit(solution)/shard_map/ppermute | solution.py:254
  33.6 1.9 %collective-permute-start.7 = (s16[528,128]{1,0:T(8,128)(2,1)S(1)}, s16[528,128]{1,0:T(8,128)(2,1)S(1)}, u32[]{:S(2)}, u32[]{:S(2)}) collective-permute-start(s16[528,128]{1,0:T(8,128)(2,1)S(1)} %get-tuple-element.38), channel_id=1, source_target_pairs={{1,25},{2,26},{3,27},{5,29},{6,30},{7,31},{8,16},{10,18},{11,19},{... | collective-permute-start | bytes 405512 | tf_op jit(solution)/shard_map/ppermute | solution.py:254
  35.5 0.0 collective-permute-done.5.m1_ref
  35.5 1.6 %collective-permute-done.6.m2_ref = s16[528,128]{1,0:T(8,128)(2,1)S(1)} collective-permute-done((s16[528,128]{1,0:T(8,128)(2,1)S(1)}, s16[528,128]{1,0:T(8,128)(2,1)S(1)}, u32[]{:S(2)}, u32[]{:S(2)}) %collective-permute-start.6) | collective-permute-done | bytes 135200 | tf_op jit(solution)/shard_map/ppermute | solution.py:254
  37.1 4.3 %collective-permute-done.7.m3_ref = s16[528,128]{1,0:T(8,128)(2,1)S(1)} collective-permute-done((s16[528,128]{1,0:T(8,128)(2,1)S(1)}, s16[528,128]{1,0:T(8,128)(2,1)S(1)}, u32[]{:S(2)}, u32[]{:S(2)}) %collective-permute-start.7) | collective-permute-done | bytes 135200 | tf_op jit(solution)/shard_map/ppermute | solution.py:254
  41.4 0.2 plane_c.1
  41.6 0.0 collective-permute-done.1.s1b_ref
  41.6 4.1 %collective-permute-done.2.s3_ref = bf16[3,256,256]{2,1,0:T(8,128)(2,1)S(1)} collective-permute-done((bf16[3,256,256]{2,1,0:T(8,128)(2,1)S(1)}, bf16[3,256,256]{2,1,0:T(8,128)(2,1)S(1)}, u32[]{:S(2)}, u32[]{:S(2)}) %collective-permute-start.2) | collective-permute-done | bytes 393248 | tf_op jit(solution)/shard_map/ppermute | solution.py:242
  45.7 1.3 %stage_d.1 = (f32[6,256,128]{2,1,0:T(8,128)S(1)}, f32[6,256,128]{2,1,0:T(8,128)S(1)}) custom-call(bf16[3,1024,256]{2,1,0:T(8,128)(2,1)S(1)} %copy-done, bf16[3,1024,256]{2,1,0:T(8,128)(2,1)S(1)} %get-tuple-element.30.weighted_ref, bf16[4,256,256]{2,1,0:T(8,128)(2,1)S(1)} %get-tuple-element.31.diagonal_ref, ...), custom_call_target="tpu_custom_call" | custom-call | flops 603979776 | bytes 1048576 | tf_op jit(solution)/shard_map/stage_d/pallas_call | solution.py:219
  47.0 0.1 collective-permute-start.8
  47.0 2.3 %collective-permute-done.8.arrived_ref = f32[6,256,128]{2,1,0:T(8,128)S(1)} collective-permute-done((f32[6,256,128]{2,1,0:T(8,128)S(1)}, f32[6,256,128]{2,1,0:T(8,128)S(1)}, u32[]{:S(2)}, u32[]{:S(2)}) %collective-permute-start.8) | collective-permute-done | bytes 786464 | tf_op jit(solution)/shard_map/ppermute | solution.py:280
  49.3 0.2 combine_d.1
  49.6 2.4 %collective-permute-start.10 = (s16[528,128]{1,0:T(8,128)(2,1)S(1)}, s16[528,128]{1,0:T(8,128)(2,1)S(1)}, u32[]{:S(2)}, u32[]{:S(2)}) collective-permute-start(s16[528,128]{1,0:T(8,128)(2,1)S(1)} %get-tuple-element.46), channel_id=1, source_target_pairs={{1,17},{2,18},{3,19},{5,21},{6,22},{7,23},{8,24},{10,26},{11,27},{... | collective-permute-start | bytes 405512 | tf_op jit(solution)/shard_map/ppermute | solution.py:254
  52.0 4.4 %collective-permute-start.11 = (s16[528,128]{1,0:T(8,128)(2,1)S(1)}, s16[528,128]{1,0:T(8,128)(2,1)S(1)}, u32[]{:S(2)}, u32[]{:S(2)}) collective-permute-start(s16[528,128]{1,0:T(8,128)(2,1)S(1)} %get-tuple-element.47), channel_id=1, source_target_pairs={{0,24},{2,26},{3,27},{4,28},{6,30},{7,31},{9,17},{10,18},{11,19},{... | collective-permute-start | bytes 405512 | tf_op jit(solution)/shard_map/ppermute | solution.py:254
  56.4 1.3 %collective-permute-start.9 = (s16[528,128]{1,0:T(8,128)(2,1)S(1)}, s16[528,128]{1,0:T(8,128)(2,1)S(1)}, u32[]{:S(2)}, u32[]{:S(2)}) collective-permute-start(s16[528,128]{1,0:T(8,128)(2,1)S(1)} %get-tuple-element.45), channel_id=1, source_target_pairs={{0,8},{1,9},{2,10},{4,12},{5,13},{6,14},{8,0},{9,1},{11,3},{12,4},... | collective-permute-start | bytes 405512 | tf_op jit(solution)/shard_map/ppermute | solution.py:254
  57.7 1.3 %collective-permute-start.13 = (s16[272,128]{1,0:T(8,128)(2,1)S(1)}, s16[272,128]{1,0:T(8,128)(2,1)S(1)}, u32[]{:S(2)}, u32[]{:S(2)}) collective-permute-start(s16[272,128]{1,0:T(8,128)(2,1)S(1)} %get-tuple-element.51), channel_id=1, source_target_pairs={{0,2},{1,3},{4,6},{5,7},{8,10},{9,11},{12,14},{13,15},{18,16},{19,... | collective-permute-start | bytes 208904 | tf_op jit(solution)/shard_map/ppermute | solution.py:254
  59.0 0.0 collective-permute-done.10.m2_ref
  59.0 1.3 %collective-permute-done.11.m3_ref = s16[528,128]{1,0:T(8,128)(2,1)S(1)} collective-permute-done((s16[528,128]{1,0:T(8,128)(2,1)S(1)}, s16[528,128]{1,0:T(8,128)(2,1)S(1)}, u32[]{:S(2)}, u32[]{:S(2)}) %collective-permute-start.11) | collective-permute-done | bytes 135200 | tf_op jit(solution)/shard_map/ppermute | solution.py:254
  60.3 1.8 %collective-permute-done.9.m1_ref = s16[528,128]{1,0:T(8,128)(2,1)S(1)} collective-permute-done((s16[528,128]{1,0:T(8,128)(2,1)S(1)}, s16[528,128]{1,0:T(8,128)(2,1)S(1)}, u32[]{:S(2)}, u32[]{:S(2)}) %collective-permute-start.9) | collective-permute-done | bytes 135200 | tf_op jit(solution)/shard_map/ppermute | solution.py:254
  62.1 0.2 plane_d.1
  62.3 3.8 %collective-permute-start.12 = (s16[272,128]{1,0:T(8,128)(2,1)S(1)}, s16[272,128]{1,0:T(8,128)(2,1)S(1)}, u32[]{:S(2)}, u32[]{:S(2)}) collective-permute-start(s16[272,128]{1,0:T(8,128)(2,1)S(1)} %get-tuple-element.50), channel_id=1, source_target_pairs={{0,1},{2,3},{3,2},{4,5},{6,7},{7,6},{9,8},{10,11},{11,10},{13,12},... | collective-permute-start | bytes 208904 | tf_op jit(solution)/shard_map/ppermute | solution.py:254
  66.1 1.3 %collective-permute-start.14 = (s16[272,128]{1,0:T(8,128)(2,1)S(1)}, s16[272,128]{1,0:T(8,128)(2,1)S(1)}, u32[]{:S(2)}, u32[]{:S(2)}) collective-permute-start(s16[272,128]{1,0:T(8,128)(2,1)S(1)} %get-tuple-element.52), channel_id=1, source_target_pairs={{0,3},{1,2},{4,7},{5,6},{8,11},{9,10},{12,15},{13,14},{18,17},{19,... | collective-permute-start | bytes 208904 | tf_op jit(solution)/shard_map/ppermute | solution.py:254
  67.4 0.0 collective-permute-done.13.m2_ref
  67.4 1.1 %collective-permute-done.12.m1_ref = s16[272,128]{1,0:T(8,128)(2,1)S(1)} collective-permute-done((s16[272,128]{1,0:T(8,128)(2,1)S(1)}, s16[272,128]{1,0:T(8,128)(2,1)S(1)}, u32[]{:S(2)}, u32[]{:S(2)}) %collective-permute-start.12) | collective-permute-done | bytes 69664 | tf_op jit(solution)/shard_map/ppermute | solution.py:254
  68.5 5.6 %collective-permute-done.14.m3_ref = s16[272,128]{1,0:T(8,128)(2,1)S(1)} collective-permute-done((s16[272,128]{1,0:T(8,128)(2,1)S(1)}, s16[272,128]{1,0:T(8,128)(2,1)S(1)}, u32[]{:S(2)}, u32[]{:S(2)}) %collective-permute-start.14) | collective-permute-done | bytes 69664 | tf_op jit(solution)/shard_map/ppermute | solution.py:254
  74.1 0.7 last.1
Async XLA Ops:
  0.0 6.6 %copy-start = (bf16[3,1024,256]{2,1,0:T(8,128)(2,1)S(1)}, bf16[3,1024,256]{2,1,0:T(8,128)(2,1)}, u32[]{:S(2)}) copy-start(bf16[3,1024,256]{2,1,0:T(8,128)(2,1)} %s_ref.4) | copy-start | bytes 4718596
  0.0 6.6 %copy-start.1 = (bf16[16,64,64]{2,1,0:T(8,128)(2,1)S(1)}, bf16[16,64,64]{2,1,0:T(8,128)(2,1)}, u32[]{:S(2)}) copy-start(bf16[16,64,64]{2,1,0:T(8,128)(2,1)} %mass_ref.1) | copy-start | bytes 393220
  0.0 6.6 %copy-start.2 = (s32[16]{0:T(128)S(1)}, s32[16]{0:T(128)}, u32[]{:S(2)}) copy-start(s32[16]{0:T(128)} %offsets_ref.1) | copy-start | bytes 196
  2.4 19.2 %collective-permute-start = (bf16[3,256,256]{2,1,0:T(8,128)(2,1)S(1)}, bf16[3,256,256]{2,1,0:T(8,128)(2,1)S(1)}, u32[]{:S(2)}, u32[]{:S(2)}) collective-permute-start(bf16[3,256,256]{2,1,0:T(8,128)(2,1)S(1)} %get-tuple-element.54), channel_id=1, source_target_pairs={{0,1},{1,0},{2,3},{3,2},{4,5},{5,4},{6,7},{7,6},{8,9},{9,8},{10,11... | collective-permute-start | bytes 1179656 | tf_op jit(solution)/shard_map/ppermute | solution.py:242
  4.0 19.9 %collective-permute-start.3 = (bf16[3,256,256]{2,1,0:T(8,128)(2,1)S(1)}, bf16[3,256,256]{2,1,0:T(8,128)(2,1)S(1)}, u32[]{:S(2)}, u32[]{:S(2)}) collective-permute-start(bf16[3,256,256]{2,1,0:T(8,128)(2,1)S(1)} %constant_dynamic-slice_fusion.2), channel_id=1, source_target_pairs={{0,2},{1,3},{2,0},{3,1},{4,6},{5,7},{6,4},{7,5},{8,10},{9,11},{10,... | collective-permute-start | bytes 1179656 | tf_op jit(solution)/shard_map/ppermute | solution.py:242
  24.8 2.7 %collective-permute-start.4 = (f32[5,256,128]{2,1,0:T(8,128)S(1)}, f32[5,256,128]{2,1,0:T(8,128)S(1)}, u32[]{:S(2)}, u32[]{:S(2)}) collective-permute-start(f32[5,256,128]{2,1,0:T(8,128)S(1)} %get-tuple-element.34), channel_id=1, source_target_pairs={{0,4},{4,0},{8,12},{12,8},{16,20},{20,16},{24,28},{28,24},{1,5},{5... | collective-permute-start | bytes 1966088 | tf_op jit(solution)/shard_map/ppermute | solution.py:280
  24.9 16.7 %collective-permute-start.1 = (bf16[3,256,256]{2,1,0:T(8,128)(2,1)S(1)}, bf16[3,256,256]{2,1,0:T(8,128)(2,1)S(1)}, u32[]{:S(2)}, u32[]{:S(2)}) collective-permute-start(bf16[3,256,256]{2,1,0:T(8,128)(2,1)S(1)} %get-tuple-element.53), channel_id=1, source_target_pairs={{0,1},{1,0},{2,3},{3,2},{4,5},{5,4},{6,7},{7,6},{8,9},{9,8},{10,11... | collective-permute-start | bytes 1179656 | tf_op jit(solution)/shard_map/ppermute | solution.py:242
  25.4 20.3 %collective-permute-start.2 = (bf16[3,256,256]{2,1,0:T(8,128)(2,1)S(1)}, bf16[3,256,256]{2,1,0:T(8,128)(2,1)S(1)}, u32[]{:S(2)}, u32[]{:S(2)}) collective-permute-start(bf16[3,256,256]{2,1,0:T(8,128)(2,1)S(1)} %get-tuple-element.53), channel_id=1, source_target_pairs={{0,3},{1,2},{2,1},{3,0},{4,7},{5,6},{6,5},{7,4},{8,11},{9,10},{10,... | collective-permute-start | bytes 1179656 | tf_op jit(solution)/shard_map/ppermute | solution.py:242
  27.7 7.8 %collective-permute-start.5 = (s16[528,128]{1,0:T(8,128)(2,1)S(1)}, s16[528,128]{1,0:T(8,128)(2,1)S(1)}, u32[]{:S(2)}, u32[]{:S(2)}) collective-permute-start(s16[528,128]{1,0:T(8,128)(2,1)S(1)} %get-tuple-element.36), channel_id=1, source_target_pairs={{0,8},{1,9},{3,11},{4,12},{5,13},{7,15},{8,0},{9,1},{10,2},{12,4},... | collective-permute-start | bytes 405512 | tf_op jit(solution)/shard_map/ppermute | solution.py:254
  29.0 8.1 %collective-permute-start.6 = (s16[528,128]{1,0:T(8,128)(2,1)S(1)}, s16[528,128]{1,0:T(8,128)(2,1)S(1)}, u32[]{:S(2)}, u32[]{:S(2)}) collective-permute-start(s16[528,128]{1,0:T(8,128)(2,1)S(1)} %get-tuple-element.37), channel_id=1, source_target_pairs={{0,16},{2,18},{3,19},{4,20},{6,22},{7,23},{9,25},{10,26},{11,27},{... | collective-permute-start | bytes 405512 | tf_op jit(solution)/shard_map/ppermute | solution.py:254
  33.6 7.8 %collective-permute-start.7 = (s16[528,128]{1,0:T(8,128)(2,1)S(1)}, s16[528,128]{1,0:T(8,128)(2,1)S(1)}, u32[]{:S(2)}, u32[]{:S(2)}) collective-permute-start(s16[528,128]{1,0:T(8,128)(2,1)S(1)} %get-tuple-element.38), channel_id=1, source_target_pairs={{1,25},{2,26},{3,27},{5,29},{6,30},{7,31},{8,16},{10,18},{11,19},{... | collective-permute-start | bytes 405512 | tf_op jit(solution)/shard_map/ppermute | solution.py:254
  47.0 2.4 %collective-permute-start.8 = (f32[6,256,128]{2,1,0:T(8,128)S(1)}, f32[6,256,128]{2,1,0:T(8,128)S(1)}, u32[]{:S(2)}, u32[]{:S(2)}) collective-permute-start(f32[6,256,128]{2,1,0:T(8,128)S(1)} %get-tuple-element.43), channel_id=1, source_target_pairs={{0,4},{4,0},{8,12},{12,8},{16,20},{20,16},{24,28},{28,24},{1,5},{5... | collective-permute-start | bytes 2359304 | tf_op jit(solution)/shard_map/ppermute | solution.py:280
  49.6 9.4 %collective-permute-start.10 = (s16[528,128]{1,0:T(8,128)(2,1)S(1)}, s16[528,128]{1,0:T(8,128)(2,1)S(1)}, u32[]{:S(2)}, u32[]{:S(2)}) collective-permute-start(s16[528,128]{1,0:T(8,128)(2,1)S(1)} %get-tuple-element.46), channel_id=1, source_target_pairs={{1,17},{2,18},{3,19},{5,21},{6,22},{7,23},{8,24},{10,26},{11,27},{... | collective-permute-start | bytes 405512 | tf_op jit(solution)/shard_map/ppermute | solution.py:254
  52.0 8.3 %collective-permute-start.11 = (s16[528,128]{1,0:T(8,128)(2,1)S(1)}, s16[528,128]{1,0:T(8,128)(2,1)S(1)}, u32[]{:S(2)}, u32[]{:S(2)}) collective-permute-start(s16[528,128]{1,0:T(8,128)(2,1)S(1)} %get-tuple-element.47), channel_id=1, source_target_pairs={{0,24},{2,26},{3,27},{4,28},{6,30},{7,31},{9,17},{10,18},{11,19},{... | collective-permute-start | bytes 405512 | tf_op jit(solution)/shard_map/ppermute | solution.py:254
  56.4 5.7 %collective-permute-start.9 = (s16[528,128]{1,0:T(8,128)(2,1)S(1)}, s16[528,128]{1,0:T(8,128)(2,1)S(1)}, u32[]{:S(2)}, u32[]{:S(2)}) collective-permute-start(s16[528,128]{1,0:T(8,128)(2,1)S(1)} %get-tuple-element.45), channel_id=1, source_target_pairs={{0,8},{1,9},{2,10},{4,12},{5,13},{6,14},{8,0},{9,1},{11,3},{12,4},... | collective-permute-start | bytes 405512 | tf_op jit(solution)/shard_map/ppermute | solution.py:254
  57.7 9.8 %collective-permute-start.13 = (s16[272,128]{1,0:T(8,128)(2,1)S(1)}, s16[272,128]{1,0:T(8,128)(2,1)S(1)}, u32[]{:S(2)}, u32[]{:S(2)}) collective-permute-start(s16[272,128]{1,0:T(8,128)(2,1)S(1)} %get-tuple-element.51), channel_id=1, source_target_pairs={{0,2},{1,3},{4,6},{5,7},{8,10},{9,11},{12,14},{13,15},{18,16},{19,... | collective-permute-start | bytes 208904 | tf_op jit(solution)/shard_map/ppermute | solution.py:254
  62.3 6.2 %collective-permute-start.12 = (s16[272,128]{1,0:T(8,128)(2,1)S(1)}, s16[272,128]{1,0:T(8,128)(2,1)S(1)}, u32[]{:S(2)}, u32[]{:S(2)}) collective-permute-start(s16[272,128]{1,0:T(8,128)(2,1)S(1)} %get-tuple-element.50), channel_id=1, source_target_pairs={{0,1},{2,3},{3,2},{4,5},{6,7},{7,6},{9,8},{10,11},{11,10},{13,12},... | collective-permute-start | bytes 208904 | tf_op jit(solution)/shard_map/ppermute | solution.py:254
  66.1 8.0 %collective-permute-start.14 = (s16[272,128]{1,0:T(8,128)(2,1)S(1)}, s16[272,128]{1,0:T(8,128)(2,1)S(1)}, u32[]{:S(2)}, u32[]{:S(2)}) collective-permute-start(s16[272,128]{1,0:T(8,128)(2,1)S(1)} %get-tuple-element.52), channel_id=1, source_target_pairs={{0,3},{1,2},{4,7},{5,6},{8,11},{9,10},{12,15},{13,14},{18,17},{19,... | collective-permute-start | bytes 208904 | tf_op jit(solution)/shard_map/ppermute | solution.py:254

commit v3 on v2

--- a/solution.py
+++ b/solution.py
@@ -223,7 +223,7 @@
         out_specs=[vmem] * len(outs),
         scratch_shapes=scratch,
         compiler_params=pltpu.CompilerParams(vmem_limit_bytes=LIMIT),
-        cost_estimate=pl.CostEstimate(flops=flops, bytes_accessed=2**20, transcendentals=0),
+        cost_estimate=pl.CostEstimate(flops=0, bytes_accessed=0, transcendentals=0),
         name=name,
     )(*args)
 
@@ -253,10 +253,7 @@
                     pairs.append((c * planes + i, to_c * planes + to_i))
         return lax.ppermute(array, ("cells", "snap"), pairs)
 
-    out2 = rows_of(snapshots, 2)
-    later, _ = lax.optimization_barrier((snapshots, out2))
-    out1 = rows_of(later, 1)
-    out3 = rows_of(later, 3)
+    out2, out1, out3 = rows_of(snapshots, 2), rows_of(snapshots, 1), rows_of(snapshots, 3)
     s2 = to_plane(out2, 2)
     s1 = to_plane(out1, 1)
     s3 = to_plane(out3, 3)
@@ -269,7 +266,7 @@
         "early",
         block_offsets,
         mass_blocks,
-        later,
+        snapshots,
         smem=(0,),
         scratch=[pltpu.SMEM((mass_blocks.shape[0],), jnp.int32)],
     )
@@ -298,13 +295,19 @@
             *args,
         )
 
-    own, other = stage(
-        stage_c_kernel, STAGE_C, "stage_c", snapshots, weighted, diagonal, gram, s1, s2
-    )
-    total, arrived = plane(own, other, START_C, (0, 1, 2), "combine_c")
-    sum_c, two = call(
-        plane_c_kernel, [((2, columns, half), F32), single], 0, "plane_c", total, *arrived
-    )
+    def chain(weighted, diagonal, gram, s1, s2):
+        own, other = stage(
+            stage_c_kernel, STAGE_C, "stage_c", snapshots, weighted, diagonal, gram, s1, s2
+        )
+        total, arrived = plane(own, other, START_C, (0, 1, 2), "combine_c")
+        return tuple(
+            call(plane_c_kernel, [((2, columns, half), F32), single], 0, "plane_c", total, *arrived)
+        )
+
+    def never(weighted, diagonal, gram, s1, s2):
+        return jnp.zeros((2, columns, half), F32), jnp.zeros(*single)
+
+    sum_c, two = lax.cond(z < planes, chain, never, weighted, diagonal, gram, s1, s2)
     from2 = send(two, 0, 2, (2, 3))
     s1b, s3, sum_c = lax.optimization_barrier((s1b, s3, sum_c))
     own, other = stage(

time: 75.2 us -> 74.5 us (level)
  Pallas kernels: 6 us -> 10.5 us
  waiting for transfers between devices: 37.1 us -> 33.1 us
  starting transfers between devices: 29.2 us -> 27.3 us
    ppermute x4, waiting for transfers between devices: 19.1 us -> 14.1 us  [to_plane(): return lax.ppermute(array, 'snap', [(i, i ^ m) for i in range(planes)])]
    pallas_call x8, Pallas kernels: 6 us -> 10.5 us  [call(): pl.pallas_call(kernel, out_shape=[jax.ShapeDtypeStruct(s, t) for s, t in...]
    ppermute x2, waiting for transfers between devices: 2.27 us -> 4.36 us  [plane(): arrived = lax.ppermute(other, 'cells', [(c, c ^ 1) for c in range(devices)])]
    ppermute x9, waiting for transfers between devices: 15.7 us -> 14.7 us  [send(): return lax.ppermute(array, ('cells', 'snap'), pairs)]
    ppermute x9, starting transfers between devices: 22.2 us -> 21.2 us  [send(): return lax.ppermute(array, ('cells', 'snap'), pairs)]
    ppermute x4, starting transfers between devices: 6.85 us -> 5.96 us  [to_plane(): return lax.ppermute(array, 'snap', [(i, i ^ m) for i in range(planes)])]
    dynamic_slice x2 -> x1, local copies, waits for them, and re-layouts: 2.34 us -> 2.43 us  [rows_of(): return lax.dynamic_slice_in_dim(array, (z ^ m) * rows, rows, axis=1)]
  transfers between devices with their start and end apart: 15 -> 15, of which waited for: 10 -> 10; matrix products, arithmetic and copies ran while one was open for 0% -> 0% of each run, Pallas kernels for 4% -> 9%
where the time goes in v3:
time: 74.5 us; the launch traced here: 73.6 us
  waiting for transfers between devices  33.1 us (44%)
  starting transfers between devices  27.3 us (37%)
  Pallas kernels  10.5 us (14%)
  local copies, waits for them, and re-layouts  2.45 us (3%)
    ppermute x9, starting transfers between devices, send(): return lax.ppermute(array, ('cells', 'snap'), pairs)  21.2 us
    ppermute x9, waiting for transfers between devices, send(): return lax.ppermute(array, ('cells', 'snap'), pairs)  14.7 us
    ppermute x4, waiting for transfers between devices, to_plane(): return lax.ppermute(array, 'snap', [(i, i ^ m) for i in range(planes)])  14.1 us
    pallas_call x8, Pallas kernels, call(): pl.pallas_call(kernel, out_shape=[jax.ShapeDtypeStruct(s, t) for s, t in...  10.5 us
    ppermute x4, starting transfers between devices, to_plane(): return lax.ppermute(array, 'snap', [(i, i ^ m) for i in range(planes)])  5.96 us
    ppermute x2, waiting for transfers between devices, plane(): arrived = lax.ppermute(other, 'cells', [(c, c ^ 1) for c in range(devices)])  4.36 us
    dynamic_slice x1, local copies, waits for them, and re-layouts, rows_of(): return lax.dynamic_slice_in_dim(array, (z ^ m) * rows, rows, axis=1)  2.43 us
  transfers between devices with their start and end apart: 15, of which 10 were waited for; matrix products, arithmetic and copies ran while one was open for 0% of the time, Pallas kernels for 9%

profile of v3, /device:TPU:4, one launch (start us, length us, event | category | flops | bytes accessed | tf_op | source)
XLA Modules:
  0.0 73.6 jit_solution(17313690277622631371)
XLA Ops:
  0.0 0.0 copy-start.2
  0.0 0.0 copy-start
  0.0 0.0 copy-start.1
  0.0 2.4 %constant_dynamic-slice_fusion = (bf16[3,256,256]{2,1,0:T(8,128)(2,1)}, bf16[3,256,256]{2,1,0:T(8,128)(2,1)}, bf16[3,256,256]{2,1,0:T(8,128)(2,1)}) fusion(bf16[3,1024,256]{2,1,0:T(8,128)(2,1)} %s_ref.3, s32[]{:T(128)S(6)} %select_n.11, s32[]{:T(128)S(6)} %select_n.10, s32[]{:T(128)S(6)} %select_n.9), kind=kLoop, calls=%fused_computation | loop fusion | bytes 2359308 | tf_op jit(solution)/shard_map/dynamic_slice | solution.py:245
  2.5 1.6 %collective-permute-start.4 = (bf16[3,256,256]{2,1,0:T(8,128)(2,1)}, bf16[3,256,256]{2,1,0:T(8,128)(2,1)S(1)}, u32[]{:S(2)}, u32[]{:S(2)}) collective-permute-start(bf16[3,256,256]{2,1,0:T(8,128)(2,1)} %get-tuple-element.65), channel_id=1, source_target_pairs={{0,1},{1,0},{2,3},{3,2},{4,5},{5,4},{6,7},{7,6},{8,9},{9,8},{10,11... | collective-permute-start | bytes 1179656 | tf_op jit(solution)/shard_map/ppermute | solution.py:242
  4.0 2.6 %collective-permute-start.7 = (bf16[3,256,256]{2,1,0:T(8,128)(2,1)}, bf16[3,256,256]{2,1,0:T(8,128)(2,1)}, u32[]{:S(2)}, u32[]{:S(2)}) collective-permute-start(bf16[3,256,256]{2,1,0:T(8,128)(2,1)} %get-tuple-element.63), channel_id=1, source_target_pairs={{0,2},{1,3},{2,0},{3,1},{4,6},{5,7},{6,4},{7,5},{8,10},{9,11},{10,... | collective-permute-start | bytes 1179656 | tf_op jit(solution)/shard_map/ppermute | solution.py:242
  6.6 0.4 collective-permute-start.5
  7.1 1.3 %collective-permute-start.6 = (bf16[3,256,256]{2,1,0:T(8,128)(2,1)}, bf16[3,256,256]{2,1,0:T(8,128)(2,1)S(1)}, u32[]{:S(2)}, u32[]{:S(2)}) collective-permute-start(bf16[3,256,256]{2,1,0:T(8,128)(2,1)} %get-tuple-element.64), channel_id=1, source_target_pairs={{0,3},{1,2},{2,1},{3,0},{4,7},{5,6},{6,5},{7,4},{8,11},{9,10},{10,... | collective-permute-start | bytes 1179656 | tf_op jit(solution)/shard_map/ppermute | solution.py:242
  8.4 0.0 copy-done.2
  8.4 0.0 copy-done
  8.4 0.0 copy-done.1
  8.4 3.2 %early.1 = (bf16[4,256,256]{2,1,0:T(8,128)(2,1)S(1)}, bf16[3,1024,256]{2,1,0:T(8,128)(2,1)}, f32[256,256]{1,0:T(8,128)}) custom-call(s32[16]{0:T(128)S(1)} %copy-done.1, bf16[16,64,64]{2,1,0:T(8,128)(2,1)S(1)} %copy-done, bf16[3,1024,256]{2,1,0:T(8,128)(2,1)S(1)} %copy-done.2), custom_call_target="tpu_custom_call" | custom-call | tf_op jit(solution)/shard_map/early/pallas_call | solution.py:219
  11.7 10.7 %collective-permute-done.4.s1_ref = bf16[3,256,256]{2,1,0:T(8,128)(2,1)S(1)} collective-permute-done((bf16[3,256,256]{2,1,0:T(8,128)(2,1)}, bf16[3,256,256]{2,1,0:T(8,128)(2,1)S(1)}, u32[]{:S(2)}, u32[]{:S(2)}) %collective-permute-start.4) | collective-permute-done | bytes 393248 | tf_op jit(solution)/shard_map/ppermute | solution.py:242
  22.3 3.4 %collective-permute-done.7 = bf16[3,256,256]{2,1,0:T(8,128)(2,1)} collective-permute-done((bf16[3,256,256]{2,1,0:T(8,128)(2,1)}, bf16[3,256,256]{2,1,0:T(8,128)(2,1)}, u32[]{:S(2)}, u32[]{:S(2)}) %collective-permute-start.7) | collective-permute-done | bytes 393248 | tf_op jit(solution)/shard_map/ppermute | solution.py:242
  25.7 19.3 %conditional.1 = ((f32[2,256,128]{2,1,0:T(8,128)S(1)}, s16[272,128]{1,0:T(8,128)(2,1)})) conditional(s32[]{:T(128)} %convert_element_type.3, () %tuple.13, (bf16[3,1024,256]{2,1,0:T(8,128)(2,1)S(1)}, bf16[3,1024,256]{2,1,0:T(8,128)(2,1)}, bf16[4,256,256]{2,1,0:T(8,128)(2,1)S(1)}, f32[256,256]{1,0:T(8,128)}, bf16[3,256,256]{2,1,0:T(8,128)(2,1)S(1)}, ...), branch_computations={%region_0.0_spmd, %region_1.0_spmd} | conditional | bytes 4243624 | solution.py:310
  25.7 2.4 %stage_c.1 = (f32[5,256,128]{2,1,0:T(8,128)S(1)}, f32[5,256,128]{2,1,0:T(8,128)S(1)}) custom-call(bf16[3,1024,256]{2,1,0:T(8,128)(2,1)S(1)} %get-tuple-element.17.s_ref, bf16[3,1024,256]{2,1,0:T(8,128)(2,1)} %get-tuple-element.18.weighted_ref, bf16[4,256,256]{2,1,0:T(8,128)(2,1)S(1)} %get-tuple-element.19.diagonal_ref, ...), custom_call_target="tpu_custom_call" | custom-call | tf_op jit(solution)/shard_map/cond/branch_1_fun/stage_c/pallas_call | solution.py:219
  28.1 0.1 collective-permute-start
  28.2 2.1 %collective-permute-done.arrived_ref = f32[5,256,128]{2,1,0:T(8,128)S(1)} collective-permute-done((f32[5,256,128]{2,1,0:T(8,128)S(1)}, f32[5,256,128]{2,1,0:T(8,128)S(1)}, u32[]{:S(2)}, u32[]{:S(2)}) %collective-permute-start) | collective-permute-done | bytes 655392 | tf_op jit(solution)/shard_map/cond/branch_1_fun/ppermute | solution.py:277
  30.3 0.2 combine_c.1
  30.5 1.3 %collective-permute-start.1 = (s16[528,128]{1,0:T(8,128)(2,1)S(1)}, s16[528,128]{1,0:T(8,128)(2,1)S(1)}, u32[]{:S(2)}, u32[]{:S(2)}) collective-permute-start(s16[528,128]{1,0:T(8,128)(2,1)S(1)} %get-tuple-element.26), channel_id=1, source_target_pairs={{0,8},{1,9},{3,11},{4,12},{5,13},{7,15},{8,0},{9,1},{10,2},{12,4},... | collective-permute-start | bytes 405512 | tf_op jit(solution)/shard_map/cond/branch_1_fun/ppermute | solution.py:254
  31.8 4.5 %collective-permute-start.2 = (s16[528,128]{1,0:T(8,128)(2,1)S(1)}, s16[528,128]{1,0:T(8,128)(2,1)S(1)}, u32[]{:S(2)}, u32[]{:S(2)}) collective-permute-start(s16[528,128]{1,0:T(8,128)(2,1)S(1)} %get-tuple-element.27), channel_id=1, source_target_pairs={{0,16},{2,18},{3,19},{4,20},{6,22},{7,23},{9,25},{10,26},{11,27},{... | collective-permute-start | bytes 405512 | tf_op jit(solution)/shard_map/cond/branch_1_fun/ppermute | solution.py:254
  36.3 1.9 %collective-permute-start.3 = (s16[528,128]{1,0:T(8,128)(2,1)S(1)}, s16[528,128]{1,0:T(8,128)(2,1)S(1)}, u32[]{:S(2)}, u32[]{:S(2)}) collective-permute-start(s16[528,128]{1,0:T(8,128)(2,1)S(1)} %get-tuple-element.28), channel_id=1, source_target_pairs={{1,25},{2,26},{3,27},{5,29},{6,30},{7,31},{8,16},{10,18},{11,19},{... | collective-permute-start | bytes 405512 | tf_op jit(solution)/shard_map/cond/branch_1_fun/ppermute | solution.py:254
  38.2 0.0 collective-permute-done.1.m1_ref
  38.3 1.7 %collective-permute-done.2.m2_ref = s16[528,128]{1,0:T(8,128)(2,1)S(1)} collective-permute-done((s16[528,128]{1,0:T(8,128)(2,1)S(1)}, s16[528,128]{1,0:T(8,128)(2,1)S(1)}, u32[]{:S(2)}, u32[]{:S(2)}) %collective-permute-start.2) | collective-permute-done | bytes 135200 | tf_op jit(solution)/shard_map/cond/branch_1_fun/ppermute | solution.py:254
  39.9 4.3 %collective-permute-done.3.m3_ref = s16[528,128]{1,0:T(8,128)(2,1)S(1)} collective-permute-done((s16[528,128]{1,0:T(8,128)(2,1)S(1)}, s16[528,128]{1,0:T(8,128)(2,1)S(1)}, u32[]{:S(2)}, u32[]{:S(2)}) %collective-permute-start.3) | collective-permute-done | bytes 135200 | tf_op jit(solution)/shard_map/cond/branch_1_fun/ppermute | solution.py:254
  44.2 0.8 %plane_c.1 = (f32[2,256,128]{2,1,0:T(8,128)S(1)}, s16[272,128]{1,0:T(8,128)(2,1)}) custom-call(f32[2,256,128]{2,1,0:T(8,128)S(1)} %get-tuple-element.25.total_ref, s16[528,128]{1,0:T(8,128)(2,1)S(1)} %collective-permute-done.1.m1_ref, s16[528,128]{1,0:T(8,128)(2,1)S(1)} %collective-permute-done.2.m2_ref, s16[528,128]{1,0:T(8,128)(2,1)S(1)} %collective-permute-done.3.m3_ref), custom_call_target="tpu_custom_call" | custom-call | tf_op jit(solution)/shard_map/cond/branch_1_fun/plane_c/pallas_call | solution.py:219
  45.0 0.0 collective-permute-done.5.s1b_ref
  45.0 0.0 collective-permute-done.6.s3_ref
  45.0 2.7 %stage_d.1 = (f32[6,256,128]{2,1,0:T(8,128)S(1)}, f32[6,256,128]{2,1,0:T(8,128)S(1)}) custom-call(bf16[3,1024,256]{2,1,0:T(8,128)(2,1)S(1)} %copy-done.2, bf16[3,1024,256]{2,1,0:T(8,128)(2,1)} %get-tuple-element.46.weighted_ref, bf16[4,256,256]{2,1,0:T(8,128)(2,1)S(1)} %get-tuple-element.47.diagonal_ref, ...), custom_call_target="tpu_custom_call" | custom-call | tf_op jit(solution)/shard_map/stage_d/pallas_call | solution.py:219
  47.7 0.0 copy-start.3
  47.8 0.1 collective-permute-start.8
  47.8 2.3 %collective-permute-done.8.arrived_ref = f32[6,256,128]{2,1,0:T(8,128)S(1)} collective-permute-done((f32[6,256,128]{2,1,0:T(8,128)S(1)}, f32[6,256,128]{2,1,0:T(8,128)S(1)}, u32[]{:S(2)}, u32[]{:S(2)}) %collective-permute-start.8) | collective-permute-done | bytes 786464 | tf_op jit(solution)/shard_map/ppermute | solution.py:277
  50.1 0.2 combine_d.1
  50.3 2.3 %collective-permute-start.10 = (s16[528,128]{1,0:T(8,128)(2,1)S(1)}, s16[528,128]{1,0:T(8,128)(2,1)S(1)}, u32[]{:S(2)}, u32[]{:S(2)}) collective-permute-start(s16[528,128]{1,0:T(8,128)(2,1)S(1)} %get-tuple-element.56), channel_id=1, source_target_pairs={{1,17},{2,18},{3,19},{5,21},{6,22},{7,23},{8,24},{10,26},{11,27},{... | collective-permute-start | bytes 405512 | tf_op jit(solution)/shard_map/ppermute | solution.py:254
  52.6 1.9 %collective-permute-start.11 = (s16[528,128]{1,0:T(8,128)(2,1)S(1)}, s16[528,128]{1,0:T(8,128)(2,1)S(1)}, u32[]{:S(2)}, u32[]{:S(2)}) collective-permute-start(s16[528,128]{1,0:T(8,128)(2,1)S(1)} %get-tuple-element.57), channel_id=1, source_target_pairs={{0,24},{2,26},{3,27},{4,28},{6,30},{7,31},{9,17},{10,18},{11,19},{... | collective-permute-start | bytes 405512 | tf_op jit(solution)/shard_map/ppermute | solution.py:254
  54.5 2.8 %collective-permute-start.9 = (s16[528,128]{1,0:T(8,128)(2,1)S(1)}, s16[528,128]{1,0:T(8,128)(2,1)S(1)}, u32[]{:S(2)}, u32[]{:S(2)}) collective-permute-start(s16[528,128]{1,0:T(8,128)(2,1)S(1)} %get-tuple-element.55), channel_id=1, source_target_pairs={{0,8},{1,9},{2,10},{4,12},{5,13},{6,14},{8,0},{9,1},{11,3},{12,4},... | collective-permute-start | bytes 405512 | tf_op jit(solution)/shard_map/ppermute | solution.py:254
  57.3 0.0 copy-done.3
  57.3 1.3 %collective-permute-start.13 = (s16[272,128]{1,0:T(8,128)(2,1)S(1)}, s16[272,128]{1,0:T(8,128)(2,1)S(1)}, u32[]{:S(2)}, u32[]{:S(2)}) collective-permute-start(s16[272,128]{1,0:T(8,128)(2,1)S(1)} %copy-done.3), channel_id=1, source_target_pairs={{0,2},{1,3},{4,6},{5,7},{8,10},{9,11},{12,14},{13,15},{18,16},{19,... | collective-permute-start | bytes 208904 | tf_op jit(solution)/shard_map/ppermute | solution.py:254
  58.6 0.1 collective-permute-done.10.m2_ref
  58.7 0.0 collective-permute-done.11.m3_ref
  58.7 1.9 %collective-permute-done.9.m1_ref = s16[528,128]{1,0:T(8,128)(2,1)S(1)} collective-permute-done((s16[528,128]{1,0:T(8,128)(2,1)S(1)}, s16[528,128]{1,0:T(8,128)(2,1)S(1)}, u32[]{:S(2)}, u32[]{:S(2)}) %collective-permute-start.9) | collective-permute-done | bytes 135200 | tf_op jit(solution)/shard_map/ppermute | solution.py:254
  60.5 0.2 plane_d.1
  60.7 4.0 %collective-permute-start.12 = (s16[272,128]{1,0:T(8,128)(2,1)S(1)}, s16[272,128]{1,0:T(8,128)(2,1)S(1)}, u32[]{:S(2)}, u32[]{:S(2)}) collective-permute-start(s16[272,128]{1,0:T(8,128)(2,1)S(1)} %get-tuple-element.60), channel_id=1, source_target_pairs={{0,1},{2,3},{3,2},{4,5},{6,7},{7,6},{9,8},{10,11},{11,10},{13,12},... | collective-permute-start | bytes 208904 | tf_op jit(solution)/shard_map/ppermute | solution.py:254
  64.7 1.3 %collective-permute-start.14 = (s16[272,128]{1,0:T(8,128)(2,1)S(1)}, s16[272,128]{1,0:T(8,128)(2,1)S(1)}, u32[]{:S(2)}, u32[]{:S(2)}) collective-permute-start(s16[272,128]{1,0:T(8,128)(2,1)S(1)} %get-tuple-element.62), channel_id=1, source_target_pairs={{0,3},{1,2},{4,7},{5,6},{8,11},{9,10},{12,15},{13,14},{18,17},{19,... | collective-permute-start | bytes 208904 | tf_op jit(solution)/shard_map/ppermute | solution.py:254
  66.0 0.0 collective-permute-done.13.m2_ref
  66.0 1.0 %collective-permute-done.12.m1_ref = s16[272,128]{1,0:T(8,128)(2,1)S(1)} collective-permute-done((s16[272,128]{1,0:T(8,128)(2,1)S(1)}, s16[272,128]{1,0:T(8,128)(2,1)S(1)}, u32[]{:S(2)}, u32[]{:S(2)}) %collective-permute-start.12) | collective-permute-done | bytes 69664 | tf_op jit(solution)/shard_map/ppermute | solution.py:254
  67.0 5.8 %collective-permute-done.14.m3_ref = s16[272,128]{1,0:T(8,128)(2,1)S(1)} collective-permute-done((s16[272,128]{1,0:T(8,128)(2,1)S(1)}, s16[272,128]{1,0:T(8,128)(2,1)S(1)}, u32[]{:S(2)}, u32[]{:S(2)}) %collective-permute-start.14) | collective-permute-done | bytes 69664 | tf_op jit(solution)/shard_map/ppermute | solution.py:254
  72.8 0.7 last.1
Async XLA Ops:
  0.0 8.4 %copy-start.2 = (bf16[3,1024,256]{2,1,0:T(8,128)(2,1)S(1)}, bf16[3,1024,256]{2,1,0:T(8,128)(2,1)}, u32[]{:S(2)}) copy-start(bf16[3,1024,256]{2,1,0:T(8,128)(2,1)} %s_ref.3) | copy-start | bytes 4718596
  0.0 8.4 %copy-start = (bf16[16,64,64]{2,1,0:T(8,128)(2,1)S(1)}, bf16[16,64,64]{2,1,0:T(8,128)(2,1)}, u32[]{:S(2)}) copy-start(bf16[16,64,64]{2,1,0:T(8,128)(2,1)} %mass_ref.1) | copy-start | bytes 393220
  0.0 8.4 %copy-start.1 = (s32[16]{0:T(128)S(1)}, s32[16]{0:T(128)}, u32[]{:S(2)}) copy-start(s32[16]{0:T(128)} %offsets_ref.1) | copy-start | bytes 196
  2.5 19.9 %collective-permute-start.4 = (bf16[3,256,256]{2,1,0:T(8,128)(2,1)}, bf16[3,256,256]{2,1,0:T(8,128)(2,1)S(1)}, u32[]{:S(2)}, u32[]{:S(2)}) collective-permute-start(bf16[3,256,256]{2,1,0:T(8,128)(2,1)} %get-tuple-element.65), channel_id=1, source_target_pairs={{0,1},{1,0},{2,3},{3,2},{4,5},{5,4},{6,7},{7,6},{8,9},{9,8},{10,11... | collective-permute-start | bytes 1179656 | tf_op jit(solution)/shard_map/ppermute | solution.py:242
  4.0 21.7 %collective-permute-start.7 = (bf16[3,256,256]{2,1,0:T(8,128)(2,1)}, bf16[3,256,256]{2,1,0:T(8,128)(2,1)}, u32[]{:S(2)}, u32[]{:S(2)}) collective-permute-start(bf16[3,256,256]{2,1,0:T(8,128)(2,1)} %get-tuple-element.63), channel_id=1, source_target_pairs={{0,2},{1,3},{2,0},{3,1},{4,6},{5,7},{6,4},{7,5},{8,10},{9,11},{10,... | collective-permute-start | bytes 1179656 | tf_op jit(solution)/shard_map/ppermute | solution.py:242
  6.6 38.4 %collective-permute-start.5 = (bf16[3,256,256]{2,1,0:T(8,128)(2,1)}, bf16[3,256,256]{2,1,0:T(8,128)(2,1)S(1)}, u32[]{:S(2)}, u32[]{:S(2)}) collective-permute-start(bf16[3,256,256]{2,1,0:T(8,128)(2,1)} %get-tuple-element.64), channel_id=1, source_target_pairs={{0,1},{1,0},{2,3},{3,2},{4,5},{5,4},{6,7},{7,6},{8,9},{9,8},{10,11... | collective-permute-start | bytes 1179656 | tf_op jit(solution)/shard_map/ppermute | solution.py:242
  7.1 37.9 %collective-permute-start.6 = (bf16[3,256,256]{2,1,0:T(8,128)(2,1)}, bf16[3,256,256]{2,1,0:T(8,128)(2,1)S(1)}, u32[]{:S(2)}, u32[]{:S(2)}) collective-permute-start(bf16[3,256,256]{2,1,0:T(8,128)(2,1)} %get-tuple-element.64), channel_id=1, source_target_pairs={{0,3},{1,2},{2,1},{3,0},{4,7},{5,6},{6,5},{7,4},{8,11},{9,10},{10,... | collective-permute-start | bytes 1179656 | tf_op jit(solution)/shard_map/ppermute | solution.py:242
  28.1 2.2 %collective-permute-start = (f32[5,256,128]{2,1,0:T(8,128)S(1)}, f32[5,256,128]{2,1,0:T(8,128)S(1)}, u32[]{:S(2)}, u32[]{:S(2)}) collective-permute-start(f32[5,256,128]{2,1,0:T(8,128)S(1)} %get-tuple-element.24), channel_id=1, source_target_pairs={{0,4},{4,0},{8,12},{12,8},{16,20},{20,16},{24,28},{28,24},{1,5},{5... | collective-permute-start | bytes 1966088 | tf_op jit(solution)/shard_map/cond/branch_1_fun/ppermute | solution.py:277
  30.5 7.8 %collective-permute-start.1 = (s16[528,128]{1,0:T(8,128)(2,1)S(1)}, s16[528,128]{1,0:T(8,128)(2,1)S(1)}, u32[]{:S(2)}, u32[]{:S(2)}) collective-permute-start(s16[528,128]{1,0:T(8,128)(2,1)S(1)} %get-tuple-element.26), channel_id=1, source_target_pairs={{0,8},{1,9},{3,11},{4,12},{5,13},{7,15},{8,0},{9,1},{10,2},{12,4},... | collective-permute-start | bytes 405512 | tf_op jit(solution)/shard_map/cond/branch_1_fun/ppermute | solution.py:254
  31.8 8.1 %collective-permute-start.2 = (s16[528,128]{1,0:T(8,128)(2,1)S(1)}, s16[528,128]{1,0:T(8,128)(2,1)S(1)}, u32[]{:S(2)}, u32[]{:S(2)}) collective-permute-start(s16[528,128]{1,0:T(8,128)(2,1)S(1)} %get-tuple-element.27), channel_id=1, source_target_pairs={{0,16},{2,18},{3,19},{4,20},{6,22},{7,23},{9,25},{10,26},{11,27},{... | collective-permute-start | bytes 405512 | tf_op jit(solution)/shard_map/cond/branch_1_fun/ppermute | solution.py:254
  36.3 7.9 %collective-permute-start.3 = (s16[528,128]{1,0:T(8,128)(2,1)S(1)}, s16[528,128]{1,0:T(8,128)(2,1)S(1)}, u32[]{:S(2)}, u32[]{:S(2)}) collective-permute-start(s16[528,128]{1,0:T(8,128)(2,1)S(1)} %get-tuple-element.28), channel_id=1, source_target_pairs={{1,25},{2,26},{3,27},{5,29},{6,30},{7,31},{8,16},{10,18},{11,19},{... | collective-permute-start | bytes 405512 | tf_op jit(solution)/shard_map/cond/branch_1_fun/ppermute | solution.py:254
  47.7 9.5 %copy-start.3 = (s16[272,128]{1,0:T(8,128)(2,1)S(1)}, s16[272,128]{1,0:T(8,128)(2,1)}, u32[]{:S(2)}) copy-start(s16[272,128]{1,0:T(8,128)(2,1)} %get-tuple-element.61) | copy-start | bytes 208900
  47.8 2.4 %collective-permute-start.8 = (f32[6,256,128]{2,1,0:T(8,128)S(1)}, f32[6,256,128]{2,1,0:T(8,128)S(1)}, u32[]{:S(2)}, u32[]{:S(2)}) collective-permute-start(f32[6,256,128]{2,1,0:T(8,128)S(1)} %get-tuple-element.53), channel_id=1, source_target_pairs={{0,4},{4,0},{8,12},{12,8},{16,20},{20,16},{24,28},{28,24},{1,5},{5... | collective-permute-start | bytes 2359304 | tf_op jit(solution)/shard_map/ppermute | solution.py:277
  50.3 8.3 %collective-permute-start.10 = (s16[528,128]{1,0:T(8,128)(2,1)S(1)}, s16[528,128]{1,0:T(8,128)(2,1)S(1)}, u32[]{:S(2)}, u32[]{:S(2)}) collective-permute-start(s16[528,128]{1,0:T(8,128)(2,1)S(1)} %get-tuple-element.56), channel_id=1, source_target_pairs={{1,17},{2,18},{3,19},{5,21},{6,22},{7,23},{8,24},{10,26},{11,27},{... | collective-permute-start | bytes 405512 | tf_op jit(solution)/shard_map/ppermute | solution.py:254
  52.6 6.1 %collective-permute-start.11 = (s16[528,128]{1,0:T(8,128)(2,1)S(1)}, s16[528,128]{1,0:T(8,128)(2,1)S(1)}, u32[]{:S(2)}, u32[]{:S(2)}) collective-permute-start(s16[528,128]{1,0:T(8,128)(2,1)S(1)} %get-tuple-element.57), channel_id=1, source_target_pairs={{0,24},{2,26},{3,27},{4,28},{6,30},{7,31},{9,17},{10,18},{11,19},{... | collective-permute-start | bytes 405512 | tf_op jit(solution)/shard_map/ppermute | solution.py:254
  54.5 6.0 %collective-permute-start.9 = (s16[528,128]{1,0:T(8,128)(2,1)S(1)}, s16[528,128]{1,0:T(8,128)(2,1)S(1)}, u32[]{:S(2)}, u32[]{:S(2)}) collective-permute-start(s16[528,128]{1,0:T(8,128)(2,1)S(1)} %get-tuple-element.55), channel_id=1, source_target_pairs={{0,8},{1,9},{2,10},{4,12},{5,13},{6,14},{8,0},{9,1},{11,3},{12,4},... | collective-permute-start | bytes 405512 | tf_op jit(solution)/shard_map/ppermute | solution.py:254
  57.3 8.7 %collective-permute-start.13 = (s16[272,128]{1,0:T(8,128)(2,1)S(1)}, s16[272,128]{1,0:T(8,128)(2,1)S(1)}, u32[]{:S(2)}, u32[]{:S(2)}) collective-permute-start(s16[272,128]{1,0:T(8,128)(2,1)S(1)} %copy-done.3), channel_id=1, source_target_pairs={{0,2},{1,3},{4,6},{5,7},{8,10},{9,11},{12,14},{13,15},{18,16},{19,... | collective-permute-start | bytes 208904 | tf_op jit(solution)/shard_map/ppermute | solution.py:254
  60.7 6.3 %collective-permute-start.12 = (s16[272,128]{1,0:T(8,128)(2,1)S(1)}, s16[272,128]{1,0:T(8,128)(2,1)S(1)}, u32[]{:S(2)}, u32[]{:S(2)}) collective-permute-start(s16[272,128]{1,0:T(8,128)(2,1)S(1)} %get-tuple-element.60), channel_id=1, source_target_pairs={{0,1},{2,3},{3,2},{4,5},{6,7},{7,6},{9,8},{10,11},{11,10},{13,12},... | collective-permute-start | bytes 208904 | tf_op jit(solution)/shard_map/ppermute | solution.py:254
  64.7 8.1 %collective-permute-start.14 = (s16[272,128]{1,0:T(8,128)(2,1)S(1)}, s16[272,128]{1,0:T(8,128)(2,1)S(1)}, u32[]{:S(2)}, u32[]{:S(2)}) collective-permute-start(s16[272,128]{1,0:T(8,128)(2,1)S(1)} %get-tuple-element.62), channel_id=1, source_target_pairs={{0,3},{1,2},{4,7},{5,6},{8,11},{9,10},{12,15},{13,14},{18,17},{19,... | collective-permute-start | bytes 208904 | tf_op jit(solution)/shard_map/ppermute | solution.py:254

commit v4 on v3

--- a/solution.py
+++ b/solution.py
@@ -35,10 +35,9 @@
     return result * factor
 
 
-STAGE_C = ((0, 0), (2, 0), (2, 1), (0, 2), (1, 2))
-START_C = (0, 2, 3, 3)
-STAGE_D = ((1, 0), (3, 0), (0, 1), (3, 1), (0, 3), (1, 3))
-START_D = (0, 2, 4, 4)
+STAGE_C = ((2, 0), (2, 1), (0, 2))
+STAGE_D = ((1, 0), (3, 0), (0, 1), (3, 1), (0, 3), (1, 3), (1, 2))
+START_D = (0, 2, 5, 4)
 
 
 def tdot(left, right):
@@ -59,19 +58,21 @@
     return piece.reshape(piece.shape[0] * piece.shape[1], piece.shape[2])
 
 
-def put(core, block, own_ref, other_ref, at):
+def halves(core, block):
     half = block.shape[1] // 2
     low, high = block[:, :half], block[:, half:]
     first = core == 0
-    own_ref[at] = jnp.where(first, low, high)
-    other_ref[at] = jnp.where(first, high, low)
-
-
-def early_kernel(offsets_ref, mass_ref, s_ref, diagonal_ref, weighted_ref, gram_ref, where_ref):
-    components, cell_rows, _ = s_ref.shape
+    return jnp.where(first, low, high), jnp.where(first, high, low)
+
+
+def early_kernel(
+    scale, offsets_ref, mass_ref, s_ref, diagonal_ref, weighted_ref, own_ref, other_ref, where_ref
+):
+    components = s_ref.shape[0]
     blocks, size, _ = mass_ref.shape
     quarters, rows, _ = diagonal_ref.shape
-    base = lax.axis_index("cells") * blocks
+    cells = lax.axis_index("cells")
+    base = cells * blocks
     for b in range(blocks):
         where_ref[offsets_ref[b] // size - base] = b
     diagonal_ref[...] = jnp.zeros_like(diagonal_ref)
@@ -90,11 +91,11 @@
     total = tdot(s_ref[0], weighted_ref[0])
     for c in range(1, components):
         total += tdot(s_ref[c], weighted_ref[c])
-    gram_ref[...] = total
+    own_ref[...], other_ref[...] = halves(cells % 2, total * scale)
 
 
 def stage_c_kernel(
-    scale, s_ref, weighted_ref, diagonal_ref, gram_ref, s1_ref, s2_ref, own_ref, other_ref
+    scale, s_ref, weighted_ref, diagonal_ref, s1_ref, s2_ref, own_ref, other_ref, later_ref
 ):
     z, core = lax.axis_index("snap"), lax.axis_index("cells") % 2
     rows = s2_ref.shape[1]
@@ -103,19 +104,26 @@
     s0, w0 = flat(s_ref[:, mine, :]), flat(weighted_ref[:, mine, :])
     s1, s2 = flat(s1_ref[...]), flat(s2_ref[...])
     w1, w2 = weigh(diagonal, s1_ref[...]), weigh(diagonal, s2_ref[...])
-    blocks = {
-        (0, 0): lambda: gram_ref[...],
-        (2, 0): lambda: tdot(s2, w0),
-        (2, 1): lambda: tdot(s2, w1),
-        (0, 2): lambda: tdot(s0, w2),
-        (1, 2): lambda: tdot(s1, w2),
-    }
+    blocks = {(2, 0): tdot(s2, w0), (2, 1): tdot(s2, w1), (0, 2): tdot(s0, w2)}
+    others = []
     for at, name in enumerate(STAGE_C):
-        put(core, blocks[name]() * scale, own_ref, other_ref, at)
+        own_ref[at], other = halves(core, blocks[name] * scale)
+        others.append(other)
+    encode(jnp.stack(others), other_ref)
+    later_ref[...] = tdot(s1, w2)
 
 
 def stage_d_kernel(
-    scale, s_ref, weighted_ref, diagonal_ref, s1_ref, s1b_ref, s3_ref, own_ref, other_ref
+    scale,
+    s_ref,
+    weighted_ref,
+    diagonal_ref,
+    later_ref,
+    s1_ref,
+    s1b_ref,
+    s3_ref,
+    own_ref,
+    other_ref,
 ):
     z, core = lax.axis_index("snap"), lax.axis_index("cells") % 2
     rows = s3_ref.shape[1]
@@ -129,19 +137,23 @@
     w1, w3 = weigh(diagonal, s1_ref[...]), weigh(diagonal, s3_ref[...])
     w1b = weigh(diagonal_ref[across], s1b_ref[...])
     blocks = {
-        (1, 0): lambda: tdot(s1, w0) + tdot(s1b, w0b),
-        (3, 0): lambda: tdot(s3, w0),
-        (0, 1): lambda: tdot(s0, w1) + tdot(s0b, w1b),
-        (3, 1): lambda: tdot(s3, w1),
-        (0, 3): lambda: tdot(s0, w3),
-        (1, 3): lambda: tdot(s1, w3),
+        (1, 0): tdot(s1, w0) + tdot(s1b, w0b),
+        (3, 0): tdot(s3, w0),
+        (0, 1): tdot(s0, w1) + tdot(s0b, w1b),
+        (3, 1): tdot(s3, w1),
+        (0, 3): tdot(s0, w3),
+        (1, 3): tdot(s1, w3),
+        (1, 2): later_ref[...],
     }
+    others = []
     for at, name in enumerate(STAGE_D):
-        put(core, blocks[name]() * scale, own_ref, other_ref, at)
+        own_ref[at], other = halves(core, blocks[name] * scale)
+        others.append(other)
+    encode(jnp.stack(others), other_ref)
 
 
 GROUP = 64
-TAIL = 16
+TAIL = 32
 STEPS = 256.0
 TOP = 32700.0
 
@@ -173,14 +185,28 @@
     return (lax.axis_index("cells") // 2) ^ lax.axis_index("snap")
 
 
-def combine_kernel(starts, own_ref, arrived_ref, total_ref, *message_refs):
+def combine_c_kernel(own_ref, arrived_ref, one_ref, other_ref, total_ref, *message_refs):
     q = place()
+    whole = own_ref[...] + decode(arrived_ref, len(STAGE_C))
+    square = one_ref[...] + other_ref[...]
     for m, ref in enumerate((total_ref, *message_refs)):
         to = q ^ m
-        start = jnp.where(
-            to == 0, starts[0], jnp.where(to == 1, starts[1], jnp.where(to == 2, starts[2], starts[3]))
-        )
-        value = own_ref[pl.ds(start, 2)] + arrived_ref[pl.ds(start, 2)]
+        first = jnp.where(to == 0, whole[0], jnp.where(to == 1, whole[1], whole[2]))
+        value = jnp.stack([first, square])
+        if m == 0:
+            ref[...] = value
+        else:
+            encode(value, ref)
+
+
+def combine_d_kernel(own_ref, arrived_ref, total_ref, *refs):
+    *message_refs, whole_ref = refs
+    q = place()
+    whole_ref[...] = own_ref[...] + decode(arrived_ref, len(STAGE_D))
+    for m, ref in enumerate((total_ref, *message_refs)):
+        to = q ^ m
+        start = jnp.where(to == 1, START_D[1], jnp.where(to == 2, START_D[2], START_D[3]))
+        value = whole_ref[pl.ds(jnp.where(to == 0, START_D[0], start), 2)]
         if m == 0:
             ref[...] = value
         else:
@@ -194,18 +220,18 @@
     return total
 
 
-def plane_c_kernel(total_ref, m1_ref, m2_ref, m3_ref, sum_ref, two_ref):
+def plane_c_kernel(total_ref, m1_ref, m2_ref, m3_ref, keep_ref, two_ref):
     total = plane_sum(total_ref, (m1_ref, m2_ref, m3_ref))
-    sum_ref[...] = total
-    encode(jnp.where(place() == 0, total[1:], total[:1]), two_ref)
-
-
-def plane_d_kernel(total_ref, m1_ref, m2_ref, m3_ref, sum_c_ref, keep_ref, one_ref, three_ref):
+    encode(total[:1], two_ref)
+    keep_ref[...] = jnp.where(place() == 0, total[1], total[0])
+
+
+def plane_d_kernel(total_ref, m1_ref, m2_ref, m3_ref, keep_c_ref, keep_ref, one_ref, three_ref):
     q = place()
     total = plane_sum(total_ref, (m1_ref, m2_ref, m3_ref))
-    encode(jnp.where(q == 0, total[:1], jnp.where(q == 2, sum_c_ref[1:], total[1:])), one_ref)
+    encode(jnp.where(q == 0, total[:1], total[1:]), one_ref)
     encode(total[1:], three_ref)
-    keep_ref[...] = jnp.where(q % 2 == 0, sum_c_ref[0], total[0])
+    keep_ref[...] = jnp.where(q % 2 == 0, keep_c_ref[...], total[0])
 
 
 def last_kernel(keep_ref, m1_ref, m2_ref, m3_ref, out_ref):
@@ -214,7 +240,7 @@
     )
 
 
-def call(kernel, outs, flops, name, *args, smem=(), scratch=()):
+def call(kernel, outs, name, *args, smem=(), scratch=()):
     vmem, scalar = pl.BlockSpec(memory_space=pltpu.VMEM), pl.BlockSpec(memory_space=pltpu.SMEM)
     return pl.pallas_call(
         kernel,
@@ -253,16 +279,20 @@
                     pairs.append((c * planes + i, to_c * planes + to_i))
         return lax.ppermute(array, ("cells", "snap"), pairs)
 
+    def swap(array):
+        return lax.ppermute(array, "cells", [(c, c ^ 1) for c in range(devices)])
+
+    def coded(slots):
+        return ((slots * columns + TAIL, half), jnp.int16)
+
+    def floats(*slots):
+        return ((*slots, columns, half), F32)
+
     out2, out1, out3 = rows_of(snapshots, 2), rows_of(snapshots, 1), rows_of(snapshots, 3)
     s2 = to_plane(out2, 2)
-    s1 = to_plane(out1, 1)
-    s3 = to_plane(out3, 3)
-    s1b = to_plane(out3, 1)
-
-    diagonal, weighted, gram = call(
-        early_kernel,
-        [((planes, rows, rows), BF16), (snapshots.shape, BF16), ((columns, columns), F32)],
-        2 * 2 * components * cell_rows * columns * columns,
+    diagonal, weighted, square, square_other = call(
+        functools.partial(early_kernel, scale),
+        [((planes, rows, rows), BF16), (snapshots.shape, BF16), floats(), floats()],
         "early",
         block_offsets,
         mass_blocks,
@@ -270,56 +300,63 @@
         smem=(0,),
         scratch=[pltpu.SMEM((mass_blocks.shape[0],), jnp.int32)],
     )
-
-    pair, single = ((2 * columns + TAIL, half), jnp.int16), ((columns + TAIL, half), jnp.int16)
-
-    def plane(own, other, starts, wanted, name):
-        arrived = lax.ppermute(other, "cells", [(c, c ^ 1) for c in range(devices)])
-        total, *out = call(
-            functools.partial(combine_kernel, starts),
-            [((2, columns, half), F32), pair, pair, pair],
-            0,
-            name,
-            own,
-            arrived,
-        )
-        return total, [send(out[m - 1], m, 0, wanted) for m in (1, 2, 3)]
-
-    def stage(kernel, blocks, name, *args):
-        shape = (len(blocks), columns, half)
-        return call(
-            functools.partial(kernel, scale),
-            [(shape, F32), (shape, F32)],
-            2 * len(blocks) * components * rows * columns * columns,
-            name,
-            *args,
-        )
-
-    def chain(weighted, diagonal, gram, s1, s2):
-        own, other = stage(
-            stage_c_kernel, STAGE_C, "stage_c", snapshots, weighted, diagonal, gram, s1, s2
-        )
-        total, arrived = plane(own, other, START_C, (0, 1, 2), "combine_c")
-        return tuple(
-            call(plane_c_kernel, [((2, columns, half), F32), single], 0, "plane_c", total, *arrived)
-        )
-
-    def never(weighted, diagonal, gram, s1, s2):
-        return jnp.zeros((2, columns, half), F32), jnp.zeros(*single)
-
-    sum_c, two = lax.cond(z < planes, chain, never, weighted, diagonal, gram, s1, s2)
+    out1, out3, weighted = lax.optimization_barrier((out1, out3, weighted))
+    s1 = to_plane(out1, 1)
+    s3 = to_plane(out3, 3)
+    s1b = to_plane(out3, 1)
+    square_arrived = swap(square_other)
+
+    own, other, later = call(
+        functools.partial(stage_c_kernel, scale),
+        [floats(len(STAGE_C)), coded(len(STAGE_C)), ((columns, columns), F32)],
+        "stage_c",
+        snapshots,
+        weighted,
+        diagonal,
+        s1,
+        s2,
+    )
+    total, *out = call(
+        combine_c_kernel,
+        [floats(2), coded(2), coded(2), coded(2)],
+        "combine_c",
+        own,
+        swap(other),
+        square,
+        square_arrived,
+    )
+    arrived = [send(out[m - 1], m, 0, (0, 1, 2)) for m in (1, 2, 3)]
+    keep, two = call(plane_c_kernel, [floats(), coded(1)], "plane_c", total, *arrived)
     from2 = send(two, 0, 2, (2, 3))
-    s1b, s3, sum_c = lax.optimization_barrier((s1b, s3, sum_c))
-    own, other = stage(
-        stage_d_kernel, STAGE_D, "stage_d", snapshots, weighted, diagonal, s1, s1b, s3
-    )
-    total, arrived = plane(own, other, START_D, (0, 1, 3), "combine_d")
+    s1b, s3, keep = lax.optimization_barrier((s1b, s3, keep))
+
+    own, other = call(
+        functools.partial(stage_d_kernel, scale),
+        [floats(len(STAGE_D)), coded(len(STAGE_D))],
+        "stage_d",
+        snapshots,
+        weighted,
+        diagonal,
+        later,
+        s1,
+        s1b,
+        s3,
+    )
+    total, *out = call(
+        combine_d_kernel,
+        [floats(2), coded(2), coded(2), coded(2)],
+        "combine_d",
+        own,
+        swap(other),
+        scratch=[pltpu.VMEM(own.shape, F32)],
+    )
+    arrived = [send(out[m - 1], m, 0, (0, 1, 2, 3)) for m in (1, 2, 3)]
     keep, one, three = call(
-        plane_d_kernel, [((columns, half), F32), single, single], 0, "plane_d", total, *arrived, sum_c
+        plane_d_kernel, [floats(), coded(1), coded(1)], "plane_d", total, *arrived, keep
     )
     from1 = send(one, 0, 1, (1, 2, 3))
     from3 = send(three, 0, 3, (2, 3))
-    return call(last_kernel, [((columns, half), F32)], 0, "last", keep, from1, from2, from3)[0]
+    return call(last_kernel, [floats()], "last", keep, from1, from2, from3)[0]
 
 
 def solution(mesh):

time: 74.5 us -> 75.8 us (1.017)
  waiting for transfers between devices: 33.1 us -> 45.2 us
  starting transfers between devices: 27.3 us -> 21.6 us
  Pallas kernels: 10.5 us -> 6.36 us
  local copies, waits for them, and re-layouts: 2.45 us -> 1.46 us
    ppermute x4, waiting for transfers between devices: 14.1 us -> 25.3 us  [to_plane(): return lax.ppermute(array, 'snap', [(i, i ^ m) for i in range(planes)])]
    ppermute x9, starting transfers between devices: 21.2 us -> 15.8 us  [send(): return lax.ppermute(array, ('cells', 'snap'), pairs)]
    pallas_call x8, Pallas kernels: 10.5 us -> 6.36 us  [call(): pl.pallas_call(kernel, out_shape=[jax.ShapeDtypeStruct(s, t) for s, t in...]
    ppermute x9, waiting for transfers between devices: 14.7 us -> 16.9 us  [send(): return lax.ppermute(array, ('cells', 'snap'), pairs)]
    ppermute x2 -> x3, waiting for transfers between devices: 4.36 us -> 2.95 us  [swap(): return lax.ppermute(array, 'cells', [(c, c ^ 1) for c in range(devices)])]
    dynamic_slice x1, local copies, waits for them, and re-layouts: 2.43 us -> 1.45 us  [rows_of(): return lax.dynamic_slice_in_dim(array, (z ^ m) * rows, rows, axis=1)]
    ppermute x4, starting transfers between devices: 5.96 us -> 5.2 us  [to_plane(): return lax.ppermute(array, 'snap', [(i, i ^ m) for i in range(planes)])]
  transfers between devices with their start and end apart: 15 -> 16, of which waited for: 10 -> 10; matrix products, arithmetic and copies ran while one was open for 0% -> 0% of each run, Pallas kernels for 9% -> 5%
where the time goes in v4:
time: 75.8 us; the launch traced here: 74.8 us
  waiting for transfers between devices  45.2 us (60%)
  starting transfers between devices  21.6 us (28%)
  Pallas kernels  6.36 us (8%)
  local copies, waits for them, and re-layouts  1.46 us (2%)
    ppermute x4, waiting for transfers between devices, to_plane(): return lax.ppermute(array, 'snap', [(i, i ^ m) for i in range(planes)])  25.3 us
    ppermute x9, waiting for transfers between devices, send(): return lax.ppermute(array, ('cells', 'snap'), pairs)  16.9 us
    ppermute x9, starting transfers between devices, send(): return lax.ppermute(array, ('cells', 'snap'), pairs)  15.8 us
    pallas_call x8, Pallas kernels, call(): pl.pallas_call(kernel, out_shape=[jax.ShapeDtypeStruct(s, t) for s, t in...  6.36 us
    ppermute x4, starting transfers between devices, to_plane(): return lax.ppermute(array, 'snap', [(i, i ^ m) for i in range(planes)])  5.2 us
    ppermute x3, waiting for transfers between devices, swap(): return lax.ppermute(array, 'cells', [(c, c ^ 1) for c in range(devices)])  2.95 us
  transfers between devices with their start and end apart: 16, of which 10 were waited for; matrix products, arithmetic and copies ran while one was open for 0% of the time, Pallas kernels for 5%

profile of v4, /device:TPU:4, one launch (start us, length us, event | category | flops | bytes accessed | tf_op | source)
XLA Modules:
  0.0 74.8 jit_solution(2420900054603663777)
XLA Ops:
  0.0 0.0 copy-start
  0.0 0.0 copy-start.2
  0.0 0.0 copy-start.1
  0.0 1.4 %constant_dynamic-slice_fusion = (bf16[3,256,256]{2,1,0:T(8,128)(2,1)S(1)}, bf16[3,256,256]{2,1,0:T(8,128)(2,1)S(1)}, bf16[3,256,256]{2,1,0:T(8,128)(2,1)S(1)}) fusion(bf16[3,1024,256]{2,1,0:T(8,128)(2,1)} %s_ref.5, s32[]{:T(128)S(6)} %select_n.11, s32[]{:T(128)S(6)} %select_n.10, s32[]{:T(128)S(6)} %select_n.9), kind=kLoop, calls=%fused_computation | loop fusion | bytes 2359308 | tf_op jit(solution)/shard_map/dynamic_slice | solution.py:271
  1.5 2.7 %collective-permute-start.1 = (bf16[3,256,256]{2,1,0:T(8,128)(2,1)S(1)}, bf16[3,256,256]{2,1,0:T(8,128)(2,1)S(1)}, u32[]{:S(2)}, u32[]{:S(2)}) collective-permute-start(bf16[3,256,256]{2,1,0:T(8,128)(2,1)S(1)} %get-tuple-element.61), channel_id=1, source_target_pairs={{0,2},{1,3},{2,0},{3,1},{4,6},{5,7},{6,4},{7,5},{8,10},{9,11},{10,... | collective-permute-start | bytes 1179656 | tf_op jit(solution)/shard_map/ppermute | solution.py:268
  4.1 0.0 copy-done
  4.1 0.0 copy-done.2
  4.1 0.0 copy-done.1
  4.1 2.3 %early.1 = (bf16[4,256,256]{2,1,0:T(8,128)(2,1)S(1)}, bf16[3,1024,256]{2,1,0:T(8,128)(2,1)S(1)}, f32[256,128]{1,0:T(8,128)S(1)}, f32[256,128]{1,0:T(8,128)S(1)}) custom-call(s32[16]{0:T(128)S(1)} %copy-done.2, bf16[16,64,64]{2,1,0:T(8,128)(2,1)S(1)} %copy-done.1, bf16[3,1024,256]{2,1,0:T(8,128)(2,1)S(1)} %copy-done), custom_call_target="tpu_custom_call" | custom-call | tf_op jit(solution)/shard_map/early/pallas_call | solution.py:245
  6.4 1.6 %collective-permute-start = (bf16[3,256,256]{2,1,0:T(8,128)(2,1)S(1)}, bf16[3,256,256]{2,1,0:T(8,128)(2,1)S(1)}, u32[]{:S(2)}, u32[]{:S(2)}) collective-permute-start(bf16[3,256,256]{2,1,0:T(8,128)(2,1)S(1)} %get-tuple-element.36), channel_id=1, source_target_pairs={{0,1},{1,0},{2,3},{3,2},{4,5},{5,4},{6,7},{7,6},{8,9},{9,8},{10,11... | collective-permute-start | bytes 1179656 | tf_op jit(solution)/shard_map/ppermute | solution.py:268
  8.1 0.2 collective-permute-start.3
  8.3 0.7 collective-permute-start.2
  9.0 21.3 %collective-permute-done.1.s2_ref = bf16[3,256,256]{2,1,0:T(8,128)(2,1)S(1)} collective-permute-done((bf16[3,256,256]{2,1,0:T(8,128)(2,1)S(1)}, bf16[3,256,256]{2,1,0:T(8,128)(2,1)S(1)}, u32[]{:S(2)}, u32[]{:S(2)}) %collective-permute-start.1) | collective-permute-done | bytes 393248 | tf_op jit(solution)/shard_map/ppermute | solution.py:268
  30.3 4.0 %collective-permute-done.s1_ref = bf16[3,256,256]{2,1,0:T(8,128)(2,1)S(1)} collective-permute-done((bf16[3,256,256]{2,1,0:T(8,128)(2,1)S(1)}, bf16[3,256,256]{2,1,0:T(8,128)(2,1)S(1)}, u32[]{:S(2)}, u32[]{:S(2)}) %collective-permute-start) | collective-permute-done | bytes 393248 | tf_op jit(solution)/shard_map/ppermute | solution.py:268
  34.3 0.8 %stage_c.1 = (f32[3,256,128]{2,1,0:T(8,128)S(1)}, s16[800,128]{1,0:T(8,128)(2,1)S(1)}, f32[256,256]{1,0:T(8,128)S(1)}) custom-call(bf16[3,1024,256]{2,1,0:T(8,128)(2,1)S(1)} %copy-done, bf16[3,1024,256]{2,1,0:T(8,128)(2,1)S(1)} %get-tuple-element.34.weighted_ref, bf16[4,256,256]{2,1,0:T(8,128)(2,1)S(1)} %get-tuple-element.35.diagonal_ref, ...), custom_call_target="tpu_custom_call" | custom-call | tf_op jit(solution)/shard_map/stage_c/pallas_call | solution.py:245
  35.1 0.1 collective-permute-start.4
  35.2 0.5 collective-permute-start.5
  35.7 1.1 %collective-permute-done.5.other_ref = f32[256,128]{1,0:T(8,128)S(1)} collective-permute-done((f32[256,128]{1,0:T(8,128)S(1)}, f32[256,128]{1,0:T(8,128)S(1)}, u32[]{:S(2)}, u32[]{:S(2)}) %collective-permute-start.5) | collective-permute-done | bytes 131104 | tf_op jit(solution)/shard_map/ppermute | solution.py:283
  36.8 0.0 collective-permute-done.4.arrived_ref
  36.9 0.2 combine_c.1
  37.1 1.3 %collective-permute-start.6 = (s16[544,128]{1,0:T(8,128)(2,1)S(1)}, s16[544,128]{1,0:T(8,128)(2,1)S(1)}, u32[]{:S(2)}, u32[]{:S(2)}) collective-permute-start(s16[544,128]{1,0:T(8,128)(2,1)S(1)} %get-tuple-element.44), channel_id=1, source_target_pairs={{0,8},{1,9},{3,11},{4,12},{5,13},{7,15},{8,0},{9,1},{10,2},{12,4},... | collective-permute-start | bytes 417800 | tf_op jit(solution)/shard_map/ppermute | solution.py:280
  38.4 4.5 %collective-permute-start.7 = (s16[544,128]{1,0:T(8,128)(2,1)S(1)}, s16[544,128]{1,0:T(8,128)(2,1)S(1)}, u32[]{:S(2)}, u32[]{:S(2)}) collective-permute-start(s16[544,128]{1,0:T(8,128)(2,1)S(1)} %get-tuple-element.45), channel_id=1, source_target_pairs={{0,16},{2,18},{3,19},{4,20},{6,22},{7,23},{9,25},{10,26},{11,27},{... | collective-permute-start | bytes 417800 | tf_op jit(solution)/shard_map/ppermute | solution.py:280
  42.9 1.9 %collective-permute-start.8 = (s16[544,128]{1,0:T(8,128)(2,1)S(1)}, s16[544,128]{1,0:T(8,128)(2,1)S(1)}, u32[]{:S(2)}, u32[]{:S(2)}) collective-permute-start(s16[544,128]{1,0:T(8,128)(2,1)S(1)} %get-tuple-element.46), channel_id=1, source_target_pairs={{1,25},{2,26},{3,27},{5,29},{6,30},{7,31},{8,16},{10,18},{11,19},{... | collective-permute-start | bytes 417800 | tf_op jit(solution)/shard_map/ppermute | solution.py:280
  44.9 0.0 collective-permute-done.6.m1_ref
  44.9 1.8 %collective-permute-done.7.m2_ref = s16[544,128]{1,0:T(8,128)(2,1)S(1)} collective-permute-done((s16[544,128]{1,0:T(8,128)(2,1)S(1)}, s16[544,128]{1,0:T(8,128)(2,1)S(1)}, u32[]{:S(2)}, u32[]{:S(2)}) %collective-permute-start.7) | collective-permute-done | bytes 139296 | tf_op jit(solution)/shard_map/ppermute | solution.py:280
  46.7 4.3 %collective-permute-done.8.m3_ref = s16[544,128]{1,0:T(8,128)(2,1)S(1)} collective-permute-done((s16[544,128]{1,0:T(8,128)(2,1)S(1)}, s16[544,128]{1,0:T(8,128)(2,1)S(1)}, u32[]{:S(2)}, u32[]{:S(2)}) %collective-permute-start.8) | collective-permute-done | bytes 139296 | tf_op jit(solution)/shard_map/ppermute | solution.py:280
  51.0 0.2 plane_c.1
  51.2 0.0 collective-permute-done.3.s3_ref
  51.2 0.0 collective-permute-done.2.s1b_ref
  51.2 1.4 %stage_d.1 = (f32[7,256,128]{2,1,0:T(8,128)S(1)}, s16[1824,128]{1,0:T(8,128)(2,1)S(1)}) custom-call(bf16[3,1024,256]{2,1,0:T(8,128)(2,1)S(1)} %copy-done, bf16[3,1024,256]{2,1,0:T(8,128)(2,1)S(1)} %get-tuple-element.34.weighted_ref, bf16[4,256,256]{2,1,0:T(8,128)(2,1)S(1)} %get-tuple-element.35.diagonal_ref, f32[256,256]{1,0:T(8,128)S(1)} %get-tuple-element.37.later_ref, ...), custom_call_target="tpu_custom_call" | custom-call | tf_op jit(solution)/shard_map/stage_d/pallas_call | solution.py:245
  52.6 0.1 collective-permute-start.9
  52.7 1.8 %collective-permute-done.9.arrived_ref = s16[1824,128]{1,0:T(8,128)(2,1)S(1)} collective-permute-done((s16[1824,128]{1,0:T(8,128)(2,1)S(1)}, s16[1824,128]{1,0:T(8,128)(2,1)S(1)}, u32[]{:S(2)}, u32[]{:S(2)}) %collective-permute-start.9) | collective-permute-done | bytes 466976 | tf_op jit(solution)/shard_map/ppermute | solution.py:283
  54.5 0.5 combine_d.1
  55.0 0.1 collective-permute-start.10
  55.0 0.9 %collective-permute-start.11 = (s16[544,128]{1,0:T(8,128)(2,1)S(1)}, s16[544,128]{1,0:T(8,128)(2,1)S(1)}, u32[]{:S(2)}, u32[]{:S(2)}) collective-permute-start(s16[544,128]{1,0:T(8,128)(2,1)S(1)} %get-tuple-element.54), channel_id=1, source_target_pairs={{0,16},{1,17},{2,18},{3,19},{4,20},{5,21},{6,22},{7,23},{8,24},{9,... | collective-permute-start | bytes 417800 | tf_op jit(solution)/shard_map/ppermute | solution.py:280
  55.9 2.6 %collective-permute-start.12 = (s16[544,128]{1,0:T(8,128)(2,1)S(1)}, s16[544,128]{1,0:T(8,128)(2,1)S(1)}, u32[]{:S(2)}, u32[]{:S(2)}) collective-permute-start(s16[544,128]{1,0:T(8,128)(2,1)S(1)} %get-tuple-element.55), channel_id=1, source_target_pairs={{0,24},{1,25},{2,26},{3,27},{4,28},{5,29},{6,30},{7,31},{8,16},{9,... | collective-permute-start | bytes 417800 | tf_op jit(solution)/shard_map/ppermute | solution.py:280
  58.5 1.3 %collective-permute-start.14 = (s16[288,128]{1,0:T(8,128)(2,1)S(1)}, s16[288,128]{1,0:T(8,128)(2,1)S(1)}, u32[]{:S(2)}, u32[]{:S(2)}) collective-permute-start(s16[288,128]{1,0:T(8,128)(2,1)S(1)} %get-tuple-element.59), channel_id=1, source_target_pairs={{0,2},{1,3},{4,6},{5,7},{8,10},{9,11},{12,14},{13,15},{18,16},{19,... | collective-permute-start | bytes 221192 | tf_op jit(solution)/shard_map/ppermute | solution.py:280
  59.8 1.7 %collective-permute-done.10.m1_ref = s16[544,128]{1,0:T(8,128)(2,1)S(1)} collective-permute-done((s16[544,128]{1,0:T(8,128)(2,1)S(1)}, s16[544,128]{1,0:T(8,128)(2,1)S(1)}, u32[]{:S(2)}, u32[]{:S(2)}) %collective-permute-start.10) | collective-permute-done | bytes 139296 | tf_op jit(solution)/shard_map/ppermute | solution.py:280
  61.6 2.3 %collective-permute-done.11.m2_ref = s16[544,128]{1,0:T(8,128)(2,1)S(1)} collective-permute-done((s16[544,128]{1,0:T(8,128)(2,1)S(1)}, s16[544,128]{1,0:T(8,128)(2,1)S(1)}, u32[]{:S(2)}, u32[]{:S(2)}) %collective-permute-start.11) | collective-permute-done | bytes 139296 | tf_op jit(solution)/shard_map/ppermute | solution.py:280
  63.8 0.0 collective-permute-done.12.m3_ref
  63.8 0.2 plane_d.1
  64.0 1.9 %collective-permute-start.13 = (s16[288,128]{1,0:T(8,128)(2,1)S(1)}, s16[288,128]{1,0:T(8,128)(2,1)S(1)}, u32[]{:S(2)}, u32[]{:S(2)}) collective-permute-start(s16[288,128]{1,0:T(8,128)(2,1)S(1)} %get-tuple-element.58), channel_id=1, source_target_pairs={{0,1},{2,3},{3,2},{4,5},{6,7},{7,6},{9,8},{10,11},{11,10},{13,12},... | collective-permute-start | bytes 221192 | tf_op jit(solution)/shard_map/ppermute | solution.py:280
  65.9 1.3 %collective-permute-start.15 = (s16[288,128]{1,0:T(8,128)(2,1)S(1)}, s16[288,128]{1,0:T(8,128)(2,1)S(1)}, u32[]{:S(2)}, u32[]{:S(2)}) collective-permute-start(s16[288,128]{1,0:T(8,128)(2,1)S(1)} %get-tuple-element.60), channel_id=1, source_target_pairs={{0,3},{1,2},{4,7},{5,6},{8,11},{9,10},{12,15},{13,14},{18,17},{19,... | collective-permute-start | bytes 221192 | tf_op jit(solution)/shard_map/ppermute | solution.py:280
  67.2 0.0 collective-permute-done.14.m2_ref
  67.3 3.0 %collective-permute-done.13.m1_ref = s16[288,128]{1,0:T(8,128)(2,1)S(1)} collective-permute-done((s16[288,128]{1,0:T(8,128)(2,1)S(1)}, s16[288,128]{1,0:T(8,128)(2,1)S(1)}, u32[]{:S(2)}, u32[]{:S(2)}) %collective-permute-start.13) | collective-permute-done | bytes 73760 | tf_op jit(solution)/shard_map/ppermute | solution.py:280
  70.3 3.8 %collective-permute-done.15.m3_ref = s16[288,128]{1,0:T(8,128)(2,1)S(1)} collective-permute-done((s16[288,128]{1,0:T(8,128)(2,1)S(1)}, s16[288,128]{1,0:T(8,128)(2,1)S(1)}, u32[]{:S(2)}, u32[]{:S(2)}) %collective-permute-start.15) | collective-permute-done | bytes 73760 | tf_op jit(solution)/shard_map/ppermute | solution.py:280
  74.1 0.7 last.1
Async XLA Ops:
  0.0 4.1 %copy-start = (bf16[3,1024,256]{2,1,0:T(8,128)(2,1)S(1)}, bf16[3,1024,256]{2,1,0:T(8,128)(2,1)}, u32[]{:S(2)}) copy-start(bf16[3,1024,256]{2,1,0:T(8,128)(2,1)} %s_ref.5) | copy-start | bytes 4718596
  0.0 4.1 %copy-start.2 = (s32[16]{0:T(128)S(1)}, s32[16]{0:T(128)}, u32[]{:S(2)}) copy-start(s32[16]{0:T(128)} %offsets_ref.1) | copy-start | bytes 196
  0.0 4.1 %copy-start.1 = (bf16[16,64,64]{2,1,0:T(8,128)(2,1)S(1)}, bf16[16,64,64]{2,1,0:T(8,128)(2,1)}, u32[]{:S(2)}) copy-start(bf16[16,64,64]{2,1,0:T(8,128)(2,1)} %mass_ref.1) | copy-start | bytes 393220
  1.5 28.9 %collective-permute-start.1 = (bf16[3,256,256]{2,1,0:T(8,128)(2,1)S(1)}, bf16[3,256,256]{2,1,0:T(8,128)(2,1)S(1)}, u32[]{:S(2)}, u32[]{:S(2)}) collective-permute-start(bf16[3,256,256]{2,1,0:T(8,128)(2,1)S(1)} %get-tuple-element.61), channel_id=1, source_target_pairs={{0,2},{1,3},{2,0},{3,1},{4,6},{5,7},{6,4},{7,5},{8,10},{9,11},{10,... | collective-permute-start | bytes 1179656 | tf_op jit(solution)/shard_map/ppermute | solution.py:268
  6.4 27.8 %collective-permute-start = (bf16[3,256,256]{2,1,0:T(8,128)(2,1)S(1)}, bf16[3,256,256]{2,1,0:T(8,128)(2,1)S(1)}, u32[]{:S(2)}, u32[]{:S(2)}) collective-permute-start(bf16[3,256,256]{2,1,0:T(8,128)(2,1)S(1)} %get-tuple-element.36), channel_id=1, source_target_pairs={{0,1},{1,0},{2,3},{3,2},{4,5},{5,4},{6,7},{7,6},{8,9},{9,8},{10,11... | collective-permute-start | bytes 1179656 | tf_op jit(solution)/shard_map/ppermute | solution.py:268
  8.1 43.1 %collective-permute-start.3 = (bf16[3,256,256]{2,1,0:T(8,128)(2,1)S(1)}, bf16[3,256,256]{2,1,0:T(8,128)(2,1)S(1)}, u32[]{:S(2)}, u32[]{:S(2)}) collective-permute-start(bf16[3,256,256]{2,1,0:T(8,128)(2,1)S(1)} %get-tuple-element.38), channel_id=1, source_target_pairs={{0,3},{1,2},{2,1},{3,0},{4,7},{5,6},{6,5},{7,4},{8,11},{9,10},{10,... | collective-permute-start | bytes 1179656 | tf_op jit(solution)/shard_map/ppermute | solution.py:268
  8.3 42.9 %collective-permute-start.2 = (bf16[3,256,256]{2,1,0:T(8,128)(2,1)S(1)}, bf16[3,256,256]{2,1,0:T(8,128)(2,1)S(1)}, u32[]{:S(2)}, u32[]{:S(2)}) collective-permute-start(bf16[3,256,256]{2,1,0:T(8,128)(2,1)S(1)} %get-tuple-element.38), channel_id=1, source_target_pairs={{0,1},{1,0},{2,3},{3,2},{4,5},{5,4},{6,7},{7,6},{8,9},{9,8},{10,11... | collective-permute-start | bytes 1179656 | tf_op jit(solution)/shard_map/ppermute | solution.py:268
  35.1 1.7 %collective-permute-start.4 = (s16[800,128]{1,0:T(8,128)(2,1)S(1)}, s16[800,128]{1,0:T(8,128)(2,1)S(1)}, u32[]{:S(2)}, u32[]{:S(2)}) collective-permute-start(s16[800,128]{1,0:T(8,128)(2,1)S(1)} %get-tuple-element.40), channel_id=1, source_target_pairs={{0,4},{4,0},{8,12},{12,8},{16,20},{20,16},{24,28},{28,24},{1,5},{5... | collective-permute-start | bytes 614408 | tf_op jit(solution)/shard_map/ppermute | solution.py:283
  35.2 1.6 %collective-permute-start.5 = (f32[256,128]{1,0:T(8,128)S(1)}, f32[256,128]{1,0:T(8,128)S(1)}, u32[]{:S(2)}, u32[]{:S(2)}) collective-permute-start(f32[256,128]{1,0:T(8,128)S(1)} %get-tuple-element.42), channel_id=1, source_target_pairs={{0,4},{4,0},{8,12},{12,8},{16,20},{20,16},{24,28},{28,24},{1,5},{5... | collective-permute-start | bytes 393224 | tf_op jit(solution)/shard_map/ppermute | solution.py:283
  37.1 7.8 %collective-permute-start.6 = (s16[544,128]{1,0:T(8,128)(2,1)S(1)}, s16[544,128]{1,0:T(8,128)(2,1)S(1)}, u32[]{:S(2)}, u32[]{:S(2)}) collective-permute-start(s16[544,128]{1,0:T(8,128)(2,1)S(1)} %get-tuple-element.44), channel_id=1, source_target_pairs={{0,8},{1,9},{3,11},{4,12},{5,13},{7,15},{8,0},{9,1},{10,2},{12,4},... | collective-permute-start | bytes 417800 | tf_op jit(solution)/shard_map/ppermute | solution.py:280
  38.4 8.3 %collective-permute-start.7 = (s16[544,128]{1,0:T(8,128)(2,1)S(1)}, s16[544,128]{1,0:T(8,128)(2,1)S(1)}, u32[]{:S(2)}, u32[]{:S(2)}) collective-permute-start(s16[544,128]{1,0:T(8,128)(2,1)S(1)} %get-tuple-element.45), channel_id=1, source_target_pairs={{0,16},{2,18},{3,19},{4,20},{6,22},{7,23},{9,25},{10,26},{11,27},{... | collective-permute-start | bytes 417800 | tf_op jit(solution)/shard_map/ppermute | solution.py:280
  42.9 8.0 %collective-permute-start.8 = (s16[544,128]{1,0:T(8,128)(2,1)S(1)}, s16[544,128]{1,0:T(8,128)(2,1)S(1)}, u32[]{:S(2)}, u32[]{:S(2)}) collective-permute-start(s16[544,128]{1,0:T(8,128)(2,1)S(1)} %get-tuple-element.46), channel_id=1, source_target_pairs={{1,25},{2,26},{3,27},{5,29},{6,30},{7,31},{8,16},{10,18},{11,19},{... | collective-permute-start | bytes 417800 | tf_op jit(solution)/shard_map/ppermute | solution.py:280
  52.6 1.9 %collective-permute-start.9 = (s16[1824,128]{1,0:T(8,128)(2,1)S(1)}, s16[1824,128]{1,0:T(8,128)(2,1)S(1)}, u32[]{:S(2)}, u32[]{:S(2)}) collective-permute-start(s16[1824,128]{1,0:T(8,128)(2,1)S(1)} %get-tuple-element.51), channel_id=1, source_target_pairs={{0,4},{4,0},{8,12},{12,8},{16,20},{20,16},{24,28},{28,24},{1,5},{5... | collective-permute-start | bytes 1400840 | tf_op jit(solution)/shard_map/ppermute | solution.py:283
  55.0 6.6 %collective-permute-start.10 = (s16[544,128]{1,0:T(8,128)(2,1)S(1)}, s16[544,128]{1,0:T(8,128)(2,1)S(1)}, u32[]{:S(2)}, u32[]{:S(2)}) collective-permute-start(s16[544,128]{1,0:T(8,128)(2,1)S(1)} %get-tuple-element.53), channel_id=1, source_target_pairs={{0,8},{1,9},{2,10},{3,11},{4,12},{5,13},{6,14},{7,15},{8,0},{9,1},... | collective-permute-start | bytes 417800 | tf_op jit(solution)/shard_map/ppermute | solution.py:280
  55.0 8.8 %collective-permute-start.11 = (s16[544,128]{1,0:T(8,128)(2,1)S(1)}, s16[544,128]{1,0:T(8,128)(2,1)S(1)}, u32[]{:S(2)}, u32[]{:S(2)}) collective-permute-start(s16[544,128]{1,0:T(8,128)(2,1)S(1)} %get-tuple-element.54), channel_id=1, source_target_pairs={{0,16},{1,17},{2,18},{3,19},{4,20},{5,21},{6,22},{7,23},{8,24},{9,... | collective-permute-start | bytes 417800 | tf_op jit(solution)/shard_map/ppermute | solution.py:280
  55.9 7.9 %collective-permute-start.12 = (s16[544,128]{1,0:T(8,128)(2,1)S(1)}, s16[544,128]{1,0:T(8,128)(2,1)S(1)}, u32[]{:S(2)}, u32[]{:S(2)}) collective-permute-start(s16[544,128]{1,0:T(8,128)(2,1)S(1)} %get-tuple-element.55), channel_id=1, source_target_pairs={{0,24},{1,25},{2,26},{3,27},{4,28},{5,29},{6,30},{7,31},{8,16},{9,... | collective-permute-start | bytes 417800 | tf_op jit(solution)/shard_map/ppermute | solution.py:280
  58.5 8.7 %collective-permute-start.14 = (s16[288,128]{1,0:T(8,128)(2,1)S(1)}, s16[288,128]{1,0:T(8,128)(2,1)S(1)}, u32[]{:S(2)}, u32[]{:S(2)}) collective-permute-start(s16[288,128]{1,0:T(8,128)(2,1)S(1)} %get-tuple-element.59), channel_id=1, source_target_pairs={{0,2},{1,3},{4,6},{5,7},{8,10},{9,11},{12,14},{13,15},{18,16},{19,... | collective-permute-start | bytes 221192 | tf_op jit(solution)/shard_map/ppermute | solution.py:280
  64.0 6.2 %collective-permute-start.13 = (s16[288,128]{1,0:T(8,128)(2,1)S(1)}, s16[288,128]{1,0:T(8,128)(2,1)S(1)}, u32[]{:S(2)}, u32[]{:S(2)}) collective-permute-start(s16[288,128]{1,0:T(8,128)(2,1)S(1)} %get-tuple-element.58), channel_id=1, source_target_pairs={{0,1},{2,3},{3,2},{4,5},{6,7},{7,6},{9,8},{10,11},{11,10},{13,12},... | collective-permute-start | bytes 221192 | tf_op jit(solution)/shard_map/ppermute | solution.py:280
  65.9 8.2 %collective-permute-start.15 = (s16[288,128]{1,0:T(8,128)(2,1)S(1)}, s16[288,128]{1,0:T(8,128)(2,1)S(1)}, u32[]{:S(2)}, u32[]{:S(2)}) collective-permute-start(s16[288,128]{1,0:T(8,128)(2,1)S(1)} %get-tuple-element.60), channel_id=1, source_target_pairs={{0,3},{1,2},{4,7},{5,6},{8,11},{9,10},{12,15},{13,14},{18,17},{19,... | collective-permute-start | bytes 221192 | tf_op jit(solution)/shard_map/ppermute | solution.py:280

commit v5 on v4

--- a/solution.py
+++ b/solution.py
@@ -300,11 +300,12 @@
         smem=(0,),
         scratch=[pltpu.SMEM((mass_blocks.shape[0],), jnp.int32)],
     )
-    out1, out3, weighted = lax.optimization_barrier((out1, out3, weighted))
+    out1, weighted = lax.optimization_barrier((out1, weighted))
     s1 = to_plane(out1, 1)
+    square_arrived = swap(square_other)
+    out3, square_arrived = lax.optimization_barrier((out3, square_arrived))
     s3 = to_plane(out3, 3)
     s1b = to_plane(out3, 1)
-    square_arrived = swap(square_other)
 
     own, other, later = call(
         functools.partial(stage_c_kernel, scale),

time: 75.8 us -> 75.5 us (level)
    ppermute x3, waiting for transfers between devices: 2.95 us -> 4.6 us  [swap(): return lax.ppermute(array, 'cells', [(c, c ^ 1) for c in range(devices)])]
    ppermute x4, waiting for transfers between devices: 25.3 us -> 24 us  [to_plane(): return lax.ppermute(array, 'snap', [(i, i ^ m) for i in range(planes)])]
  transfers between devices with their start and end apart: 16 -> 16, of which waited for: 10 -> 11; matrix products, arithmetic and copies ran while one was open for 0% -> 0% of each run, Pallas kernels for 5% -> 5%
where the time goes in v5:
time: 75.5 us; the launch traced here: 74.5 us
  waiting for transfers between devices  45.4 us (60%)
  starting transfers between devices  21.1 us (28%)
  Pallas kernels  6.36 us (8%)
  local copies, waits for them, and re-layouts  1.46 us (2%)
    ppermute x4, waiting for transfers between devices, to_plane(): return lax.ppermute(array, 'snap', [(i, i ^ m) for i in range(planes)])  24 us
    ppermute x9, waiting for transfers between devices, send(): return lax.ppermute(array, ('cells', 'snap'), pairs)  16.9 us
    ppermute x9, starting transfers between devices, send(): return lax.ppermute(array, ('cells', 'snap'), pairs)  15.8 us
    pallas_call x8, Pallas kernels, call(): pl.pallas_call(kernel, out_shape=[jax.ShapeDtypeStruct(s, t) for s, t in...  6.36 us
    ppermute x4, starting transfers between devices, to_plane(): return lax.ppermute(array, 'snap', [(i, i ^ m) for i in range(planes)])  5.2 us
    ppermute x3, waiting for transfers between devices, swap(): return lax.ppermute(array, 'cells', [(c, c ^ 1) for c in range(devices)])  4.6 us
  transfers between devices with their start and end apart: 16, of which 11 were waited for; matrix products, arithmetic and copies ran while one was open for 0% of the time, Pallas kernels for 5%

profile of v5, /device:TPU:4, one launch (start us, length us, event | category | flops | bytes accessed | tf_op | source)
XLA Modules:
  0.0 74.5 jit_solution(9751740598154414572)
XLA Ops:
  0.0 0.0 copy-start
  0.0 0.0 copy-start.2
  0.0 0.0 copy-start.1
  0.0 1.4 %constant_dynamic-slice_fusion = (bf16[3,256,256]{2,1,0:T(8,128)(2,1)S(1)}, bf16[3,256,256]{2,1,0:T(8,128)(2,1)S(1)}, bf16[3,256,256]{2,1,0:T(8,128)(2,1)S(1)}) fusion(bf16[3,1024,256]{2,1,0:T(8,128)(2,1)} %s_ref.5, s32[]{:T(128)S(6)} %select_n.11, s32[]{:T(128)S(6)} %select_n.10, s32[]{:T(128)S(6)} %select_n.9), kind=kLoop, calls=%fused_computation | loop fusion | bytes 2359308 | tf_op jit(solution)/shard_map/dynamic_slice | solution.py:271
  1.5 2.7 %collective-permute-start.1 = (bf16[3,256,256]{2,1,0:T(8,128)(2,1)S(1)}, bf16[3,256,256]{2,1,0:T(8,128)(2,1)S(1)}, u32[]{:S(2)}, u32[]{:S(2)}) collective-permute-start(bf16[3,256,256]{2,1,0:T(8,128)(2,1)S(1)} %get-tuple-element.64), channel_id=1, source_target_pairs={{0,2},{1,3},{2,0},{3,1},{4,6},{5,7},{6,4},{7,5},{8,10},{9,11},{10,... | collective-permute-start | bytes 1179656 | tf_op jit(solution)/shard_map/ppermute | solution.py:268
  4.1 0.0 copy-done
  4.1 0.0 copy-done.2
  4.1 0.0 copy-done.1
  4.1 2.3 %early.1 = (bf16[4,256,256]{2,1,0:T(8,128)(2,1)S(1)}, bf16[3,1024,256]{2,1,0:T(8,128)(2,1)S(1)}, f32[256,128]{1,0:T(8,128)S(1)}, f32[256,128]{1,0:T(8,128)S(1)}) custom-call(s32[16]{0:T(128)S(1)} %copy-done.2, bf16[16,64,64]{2,1,0:T(8,128)(2,1)S(1)} %copy-done.1, bf16[3,1024,256]{2,1,0:T(8,128)(2,1)S(1)} %copy-done), custom_call_target="tpu_custom_call" | custom-call | tf_op jit(solution)/shard_map/early/pallas_call | solution.py:245
  6.4 1.6 %collective-permute-start = (bf16[3,256,256]{2,1,0:T(8,128)(2,1)S(1)}, bf16[3,256,256]{2,1,0:T(8,128)(2,1)S(1)}, u32[]{:S(2)}, u32[]{:S(2)}) collective-permute-start(bf16[3,256,256]{2,1,0:T(8,128)(2,1)S(1)} %get-tuple-element.37), channel_id=1, source_target_pairs={{0,1},{1,0},{2,3},{3,2},{4,5},{5,4},{6,7},{7,6},{8,9},{9,8},{10,11... | collective-permute-start | bytes 1179656 | tf_op jit(solution)/shard_map/ppermute | solution.py:268
  8.1 0.0 collective-permute-start.2
  8.1 1.3 %collective-permute-done.2.other_ref = f32[256,128]{1,0:T(8,128)S(1)} collective-permute-done((f32[256,128]{1,0:T(8,128)S(1)}, f32[256,128]{1,0:T(8,128)S(1)}, u32[]{:S(2)}, u32[]{:S(2)}) %collective-permute-start.2) | collective-permute-done | bytes 131104 | tf_op jit(solution)/shard_map/ppermute | solution.py:283
  9.4 0.2 collective-permute-start.4
  9.7 0.7 collective-permute-start.3
  10.3 20.0 %collective-permute-done.1.s2_ref = bf16[3,256,256]{2,1,0:T(8,128)(2,1)S(1)} collective-permute-done((bf16[3,256,256]{2,1,0:T(8,128)(2,1)S(1)}, bf16[3,256,256]{2,1,0:T(8,128)(2,1)S(1)}, u32[]{:S(2)}, u32[]{:S(2)}) %collective-permute-start.1) | collective-permute-done | bytes 393248 | tf_op jit(solution)/shard_map/ppermute | solution.py:268
  30.3 4.0 %collective-permute-done.s1_ref = bf16[3,256,256]{2,1,0:T(8,128)(2,1)S(1)} collective-permute-done((bf16[3,256,256]{2,1,0:T(8,128)(2,1)S(1)}, bf16[3,256,256]{2,1,0:T(8,128)(2,1)S(1)}, u32[]{:S(2)}, u32[]{:S(2)}) %collective-permute-start) | collective-permute-done | bytes 393248 | tf_op jit(solution)/shard_map/ppermute | solution.py:268
  34.3 0.8 %stage_c.1 = (f32[3,256,128]{2,1,0:T(8,128)S(1)}, s16[800,128]{1,0:T(8,128)(2,1)S(1)}, f32[256,256]{1,0:T(8,128)S(1)}) custom-call(bf16[3,1024,256]{2,1,0:T(8,128)(2,1)S(1)} %copy-done, bf16[3,1024,256]{2,1,0:T(8,128)(2,1)S(1)} %get-tuple-element.35.weighted_ref, bf16[4,256,256]{2,1,0:T(8,128)(2,1)S(1)} %get-tuple-element.36.diagonal_ref, ...), custom_call_target="tpu_custom_call" | custom-call | tf_op jit(solution)/shard_map/stage_c/pallas_call | solution.py:245
  35.1 0.1 collective-permute-start.5
  35.2 1.4 %collective-permute-done.5.arrived_ref = s16[800,128]{1,0:T(8,128)(2,1)S(1)} collective-permute-done((s16[800,128]{1,0:T(8,128)(2,1)S(1)}, s16[800,128]{1,0:T(8,128)(2,1)S(1)}, u32[]{:S(2)}, u32[]{:S(2)}) %collective-permute-start.5) | collective-permute-done | bytes 204832 | tf_op jit(solution)/shard_map/ppermute | solution.py:283
  36.7 0.2 combine_c.1
  36.9 1.3 %collective-permute-start.6 = (s16[544,128]{1,0:T(8,128)(2,1)S(1)}, s16[544,128]{1,0:T(8,128)(2,1)S(1)}, u32[]{:S(2)}, u32[]{:S(2)}) collective-permute-start(s16[544,128]{1,0:T(8,128)(2,1)S(1)} %get-tuple-element.46), channel_id=1, source_target_pairs={{0,8},{1,9},{3,11},{4,12},{5,13},{7,15},{8,0},{9,1},{10,2},{12,4},... | collective-permute-start | bytes 417800 | tf_op jit(solution)/shard_map/ppermute | solution.py:280
  38.2 4.5 %collective-permute-start.7 = (s16[544,128]{1,0:T(8,128)(2,1)S(1)}, s16[544,128]{1,0:T(8,128)(2,1)S(1)}, u32[]{:S(2)}, u32[]{:S(2)}) collective-permute-start(s16[544,128]{1,0:T(8,128)(2,1)S(1)} %get-tuple-element.47), channel_id=1, source_target_pairs={{0,16},{2,18},{3,19},{4,20},{6,22},{7,23},{9,25},{10,26},{11,27},{... | collective-permute-start | bytes 417800 | tf_op jit(solution)/shard_map/ppermute | solution.py:280
  42.7 1.9 %collective-permute-start.8 = (s16[544,128]{1,0:T(8,128)(2,1)S(1)}, s16[544,128]{1,0:T(8,128)(2,1)S(1)}, u32[]{:S(2)}, u32[]{:S(2)}) collective-permute-start(s16[544,128]{1,0:T(8,128)(2,1)S(1)} %get-tuple-element.48), channel_id=1, source_target_pairs={{1,25},{2,26},{3,27},{5,29},{6,30},{7,31},{8,16},{10,18},{11,19},{... | collective-permute-start | bytes 417800 | tf_op jit(solution)/shard_map/ppermute | solution.py:280
  44.7 0.0 collective-permute-done.6.m1_ref
  44.7 1.7 %collective-permute-done.7.m2_ref = s16[544,128]{1,0:T(8,128)(2,1)S(1)} collective-permute-done((s16[544,128]{1,0:T(8,128)(2,1)S(1)}, s16[544,128]{1,0:T(8,128)(2,1)S(1)}, u32[]{:S(2)}, u32[]{:S(2)}) %collective-permute-start.7) | collective-permute-done | bytes 139296 | tf_op jit(solution)/shard_map/ppermute | solution.py:280
  46.4 4.3 %collective-permute-done.8.m3_ref = s16[544,128]{1,0:T(8,128)(2,1)S(1)} collective-permute-done((s16[544,128]{1,0:T(8,128)(2,1)S(1)}, s16[544,128]{1,0:T(8,128)(2,1)S(1)}, u32[]{:S(2)}, u32[]{:S(2)}) %collective-permute-start.8) | collective-permute-done | bytes 139296 | tf_op jit(solution)/shard_map/ppermute | solution.py:280
  50.7 0.2 plane_c.1
  50.9 0.0 collective-permute-done.4.s3_ref
  50.9 0.0 collective-permute-done.3.s1b_ref
  50.9 1.4 %stage_d.1 = (f32[7,256,128]{2,1,0:T(8,128)S(1)}, s16[1824,128]{1,0:T(8,128)(2,1)S(1)}) custom-call(bf16[3,1024,256]{2,1,0:T(8,128)(2,1)S(1)} %copy-done, bf16[3,1024,256]{2,1,0:T(8,128)(2,1)S(1)} %get-tuple-element.35.weighted_ref, bf16[4,256,256]{2,1,0:T(8,128)(2,1)S(1)} %get-tuple-element.36.diagonal_ref, f32[256,256]{1,0:T(8,128)S(1)} %get-tuple-element.38.later_ref, ...), custom_call_target="tpu_custom_call" | custom-call | tf_op jit(solution)/shard_map/stage_d/pallas_call | solution.py:245
  52.3 0.1 collective-permute-start.9
  52.4 1.8 %collective-permute-done.9.arrived_ref = s16[1824,128]{1,0:T(8,128)(2,1)S(1)} collective-permute-done((s16[1824,128]{1,0:T(8,128)(2,1)S(1)}, s16[1824,128]{1,0:T(8,128)(2,1)S(1)}, u32[]{:S(2)}, u32[]{:S(2)}) %collective-permute-start.9) | collective-permute-done | bytes 466976 | tf_op jit(solution)/shard_map/ppermute | solution.py:283
  54.2 0.5 combine_d.1
  54.7 0.1 collective-permute-start.10
  54.8 0.9 %collective-permute-start.11 = (s16[544,128]{1,0:T(8,128)(2,1)S(1)}, s16[544,128]{1,0:T(8,128)(2,1)S(1)}, u32[]{:S(2)}, u32[]{:S(2)}) collective-permute-start(s16[544,128]{1,0:T(8,128)(2,1)S(1)} %get-tuple-element.56), channel_id=1, source_target_pairs={{0,16},{1,17},{2,18},{3,19},{4,20},{5,21},{6,22},{7,23},{8,24},{9,... | collective-permute-start | bytes 417800 | tf_op jit(solution)/shard_map/ppermute | solution.py:280
  55.7 2.6 %collective-permute-start.12 = (s16[544,128]{1,0:T(8,128)(2,1)S(1)}, s16[544,128]{1,0:T(8,128)(2,1)S(1)}, u32[]{:S(2)}, u32[]{:S(2)}) collective-permute-start(s16[544,128]{1,0:T(8,128)(2,1)S(1)} %get-tuple-element.57), channel_id=1, source_target_pairs={{0,24},{1,25},{2,26},{3,27},{4,28},{5,29},{6,30},{7,31},{8,16},{9,... | collective-permute-start | bytes 417800 | tf_op jit(solution)/shard_map/ppermute | solution.py:280
  58.2 1.3 %collective-permute-start.14 = (s16[288,128]{1,0:T(8,128)(2,1)S(1)}, s16[288,128]{1,0:T(8,128)(2,1)S(1)}, u32[]{:S(2)}, u32[]{:S(2)}) collective-permute-start(s16[288,128]{1,0:T(8,128)(2,1)S(1)} %get-tuple-element.61), channel_id=1, source_target_pairs={{0,2},{1,3},{4,6},{5,7},{8,10},{9,11},{12,14},{13,15},{18,16},{19,... | collective-permute-start | bytes 221192 | tf_op jit(solution)/shard_map/ppermute | solution.py:280
  59.5 1.7 %collective-permute-done.10.m1_ref = s16[544,128]{1,0:T(8,128)(2,1)S(1)} collective-permute-done((s16[544,128]{1,0:T(8,128)(2,1)S(1)}, s16[544,128]{1,0:T(8,128)(2,1)S(1)}, u32[]{:S(2)}, u32[]{:S(2)}) %collective-permute-start.10) | collective-permute-done | bytes 139296 | tf_op jit(solution)/shard_map/ppermute | solution.py:280
  61.3 2.3 %collective-permute-done.11.m2_ref = s16[544,128]{1,0:T(8,128)(2,1)S(1)} collective-permute-done((s16[544,128]{1,0:T(8,128)(2,1)S(1)}, s16[544,128]{1,0:T(8,128)(2,1)S(1)}, u32[]{:S(2)}, u32[]{:S(2)}) %collective-permute-start.11) | collective-permute-done | bytes 139296 | tf_op jit(solution)/shard_map/ppermute | solution.py:280
  63.5 0.0 collective-permute-done.12.m3_ref
  63.5 0.2 plane_d.1
  63.7 1.9 %collective-permute-start.13 = (s16[288,128]{1,0:T(8,128)(2,1)S(1)}, s16[288,128]{1,0:T(8,128)(2,1)S(1)}, u32[]{:S(2)}, u32[]{:S(2)}) collective-permute-start(s16[288,128]{1,0:T(8,128)(2,1)S(1)} %get-tuple-element.60), channel_id=1, source_target_pairs={{0,1},{2,3},{3,2},{4,5},{6,7},{7,6},{9,8},{10,11},{11,10},{13,12},... | collective-permute-start | bytes 221192 | tf_op jit(solution)/shard_map/ppermute | solution.py:280
  65.7 1.3 %collective-permute-start.15 = (s16[288,128]{1,0:T(8,128)(2,1)S(1)}, s16[288,128]{1,0:T(8,128)(2,1)S(1)}, u32[]{:S(2)}, u32[]{:S(2)}) collective-permute-start(s16[288,128]{1,0:T(8,128)(2,1)S(1)} %get-tuple-element.62), channel_id=1, source_target_pairs={{0,3},{1,2},{4,7},{5,6},{8,11},{9,10},{12,15},{13,14},{18,17},{19,... | collective-permute-start | bytes 221192 | tf_op jit(solution)/shard_map/ppermute | solution.py:280
  67.0 0.0 collective-permute-done.14.m2_ref
  67.0 3.0 %collective-permute-done.13.m1_ref = s16[288,128]{1,0:T(8,128)(2,1)S(1)} collective-permute-done((s16[288,128]{1,0:T(8,128)(2,1)S(1)}, s16[288,128]{1,0:T(8,128)(2,1)S(1)}, u32[]{:S(2)}, u32[]{:S(2)}) %collective-permute-start.13) | collective-permute-done | bytes 73760 | tf_op jit(solution)/shard_map/ppermute | solution.py:280
  70.0 3.8 %collective-permute-done.15.m3_ref = s16[288,128]{1,0:T(8,128)(2,1)S(1)} collective-permute-done((s16[288,128]{1,0:T(8,128)(2,1)S(1)}, s16[288,128]{1,0:T(8,128)(2,1)S(1)}, u32[]{:S(2)}, u32[]{:S(2)}) %collective-permute-start.15) | collective-permute-done | bytes 73760 | tf_op jit(solution)/shard_map/ppermute | solution.py:280
  73.8 0.7 last.1
Async XLA Ops:
  0.0 4.1 %copy-start = (bf16[3,1024,256]{2,1,0:T(8,128)(2,1)S(1)}, bf16[3,1024,256]{2,1,0:T(8,128)(2,1)}, u32[]{:S(2)}) copy-start(bf16[3,1024,256]{2,1,0:T(8,128)(2,1)} %s_ref.5) | copy-start | bytes 4718596
  0.0 4.1 %copy-start.2 = (s32[16]{0:T(128)S(1)}, s32[16]{0:T(128)}, u32[]{:S(2)}) copy-start(s32[16]{0:T(128)} %offsets_ref.1) | copy-start | bytes 196
  0.0 4.1 %copy-start.1 = (bf16[16,64,64]{2,1,0:T(8,128)(2,1)S(1)}, bf16[16,64,64]{2,1,0:T(8,128)(2,1)}, u32[]{:S(2)}) copy-start(bf16[16,64,64]{2,1,0:T(8,128)(2,1)} %mass_ref.1) | copy-start | bytes 393220
  1.5 28.9 %collective-permute-start.1 = (bf16[3,256,256]{2,1,0:T(8,128)(2,1)S(1)}, bf16[3,256,256]{2,1,0:T(8,128)(2,1)S(1)}, u32[]{:S(2)}, u32[]{:S(2)}) collective-permute-start(bf16[3,256,256]{2,1,0:T(8,128)(2,1)S(1)} %get-tuple-element.64), channel_id=1, source_target_pairs={{0,2},{1,3},{2,0},{3,1},{4,6},{5,7},{6,4},{7,5},{8,10},{9,11},{10,... | collective-permute-start | bytes 1179656 | tf_op jit(solution)/shard_map/ppermute | solution.py:268
  6.4 27.8 %collective-permute-start = (bf16[3,256,256]{2,1,0:T(8,128)(2,1)S(1)}, bf16[3,256,256]{2,1,0:T(8,128)(2,1)S(1)}, u32[]{:S(2)}, u32[]{:S(2)}) collective-permute-start(bf16[3,256,256]{2,1,0:T(8,128)(2,1)S(1)} %get-tuple-element.37), channel_id=1, source_target_pairs={{0,1},{1,0},{2,3},{3,2},{4,5},{5,4},{6,7},{7,6},{8,9},{9,8},{10,11... | collective-permute-start | bytes 1179656 | tf_op jit(solution)/shard_map/ppermute | solution.py:268
  8.1 1.3 %collective-permute-start.2 = (f32[256,128]{1,0:T(8,128)S(1)}, f32[256,128]{1,0:T(8,128)S(1)}, u32[]{:S(2)}, u32[]{:S(2)}) collective-permute-start(f32[256,128]{1,0:T(8,128)S(1)} %get-tuple-element.39), channel_id=1, source_target_pairs={{0,4},{4,0},{8,12},{12,8},{16,20},{20,16},{24,28},{28,24},{1,5},{5... | collective-permute-start | bytes 393224 | tf_op jit(solution)/shard_map/ppermute | solution.py:283
  9.4 41.5 %collective-permute-start.4 = (bf16[3,256,256]{2,1,0:T(8,128)(2,1)S(1)}, bf16[3,256,256]{2,1,0:T(8,128)(2,1)S(1)}, u32[]{:S(2)}, u32[]{:S(2)}) collective-permute-start(bf16[3,256,256]{2,1,0:T(8,128)(2,1)S(1)} %get-tuple-element.40), channel_id=1, source_target_pairs={{0,3},{1,2},{2,1},{3,0},{4,7},{5,6},{6,5},{7,4},{8,11},{9,10},{10,... | collective-permute-start | bytes 1179656 | tf_op jit(solution)/shard_map/ppermute | solution.py:268
  9.7 41.2 %collective-permute-start.3 = (bf16[3,256,256]{2,1,0:T(8,128)(2,1)S(1)}, bf16[3,256,256]{2,1,0:T(8,128)(2,1)S(1)}, u32[]{:S(2)}, u32[]{:S(2)}) collective-permute-start(bf16[3,256,256]{2,1,0:T(8,128)(2,1)S(1)} %get-tuple-element.40), channel_id=1, source_target_pairs={{0,1},{1,0},{2,3},{3,2},{4,5},{5,4},{6,7},{7,6},{8,9},{9,8},{10,11... | collective-permute-start | bytes 1179656 | tf_op jit(solution)/shard_map/ppermute | solution.py:268
  35.1 1.5 %collective-permute-start.5 = (s16[800,128]{1,0:T(8,128)(2,1)S(1)}, s16[800,128]{1,0:T(8,128)(2,1)S(1)}, u32[]{:S(2)}, u32[]{:S(2)}) collective-permute-start(s16[800,128]{1,0:T(8,128)(2,1)S(1)} %get-tuple-element.42), channel_id=1, source_target_pairs={{0,4},{4,0},{8,12},{12,8},{16,20},{20,16},{24,28},{28,24},{1,5},{5... | collective-permute-start | bytes 614408 | tf_op jit(solution)/shard_map/ppermute | solution.py:283
  36.9 7.8 %collective-permute-start.6 = (s16[544,128]{1,0:T(8,128)(2,1)S(1)}, s16[544,128]{1,0:T(8,128)(2,1)S(1)}, u32[]{:S(2)}, u32[]{:S(2)}) collective-permute-start(s16[544,128]{1,0:T(8,128)(2,1)S(1)} %get-tuple-element.46), channel_id=1, source_target_pairs={{0,8},{1,9},{3,11},{4,12},{5,13},{7,15},{8,0},{9,1},{10,2},{12,4},... | collective-permute-start | bytes 417800 | tf_op jit(solution)/shard_map/ppermute | solution.py:280
  38.2 8.2 %collective-permute-start.7 = (s16[544,128]{1,0:T(8,128)(2,1)S(1)}, s16[544,128]{1,0:T(8,128)(2,1)S(1)}, u32[]{:S(2)}, u32[]{:S(2)}) collective-permute-start(s16[544,128]{1,0:T(8,128)(2,1)S(1)} %get-tuple-element.47), channel_id=1, source_target_pairs={{0,16},{2,18},{3,19},{4,20},{6,22},{7,23},{9,25},{10,26},{11,27},{... | collective-permute-start | bytes 417800 | tf_op jit(solution)/shard_map/ppermute | solution.py:280
  42.7 7.9 %collective-permute-start.8 = (s16[544,128]{1,0:T(8,128)(2,1)S(1)}, s16[544,128]{1,0:T(8,128)(2,1)S(1)}, u32[]{:S(2)}, u32[]{:S(2)}) collective-permute-start(s16[544,128]{1,0:T(8,128)(2,1)S(1)} %get-tuple-element.48), channel_id=1, source_target_pairs={{1,25},{2,26},{3,27},{5,29},{6,30},{7,31},{8,16},{10,18},{11,19},{... | collective-permute-start | bytes 417800 | tf_op jit(solution)/shard_map/ppermute | solution.py:280
  52.3 1.9 %collective-permute-start.9 = (s16[1824,128]{1,0:T(8,128)(2,1)S(1)}, s16[1824,128]{1,0:T(8,128)(2,1)S(1)}, u32[]{:S(2)}, u32[]{:S(2)}) collective-permute-start(s16[1824,128]{1,0:T(8,128)(2,1)S(1)} %get-tuple-element.53), channel_id=1, source_target_pairs={{0,4},{4,0},{8,12},{12,8},{16,20},{20,16},{24,28},{28,24},{1,5},{5... | collective-permute-start | bytes 1400840 | tf_op jit(solution)/shard_map/ppermute | solution.py:283
  54.7 6.6 %collective-permute-start.10 = (s16[544,128]{1,0:T(8,128)(2,1)S(1)}, s16[544,128]{1,0:T(8,128)(2,1)S(1)}, u32[]{:S(2)}, u32[]{:S(2)}) collective-permute-start(s16[544,128]{1,0:T(8,128)(2,1)S(1)} %get-tuple-element.55), channel_id=1, source_target_pairs={{0,8},{1,9},{2,10},{3,11},{4,12},{5,13},{6,14},{7,15},{8,0},{9,1},... | collective-permute-start | bytes 417800 | tf_op jit(solution)/shard_map/ppermute | solution.py:280
  54.8 8.8 %collective-permute-start.11 = (s16[544,128]{1,0:T(8,128)(2,1)S(1)}, s16[544,128]{1,0:T(8,128)(2,1)S(1)}, u32[]{:S(2)}, u32[]{:S(2)}) collective-permute-start(s16[544,128]{1,0:T(8,128)(2,1)S(1)} %get-tuple-element.56), channel_id=1, source_target_pairs={{0,16},{1,17},{2,18},{3,19},{4,20},{5,21},{6,22},{7,23},{8,24},{9,... | collective-permute-start | bytes 417800 | tf_op jit(solution)/shard_map/ppermute | solution.py:280
  55.7 7.9 %collective-permute-start.12 = (s16[544,128]{1,0:T(8,128)(2,1)S(1)}, s16[544,128]{1,0:T(8,128)(2,1)S(1)}, u32[]{:S(2)}, u32[]{:S(2)}) collective-permute-start(s16[544,128]{1,0:T(8,128)(2,1)S(1)} %get-tuple-element.57), channel_id=1, source_target_pairs={{0,24},{1,25},{2,26},{3,27},{4,28},{5,29},{6,30},{7,31},{8,16},{9,... | collective-permute-start | bytes 417800 | tf_op jit(solution)/shard_map/ppermute | solution.py:280
  58.2 8.7 %collective-permute-start.14 = (s16[288,128]{1,0:T(8,128)(2,1)S(1)}, s16[288,128]{1,0:T(8,128)(2,1)S(1)}, u32[]{:S(2)}, u32[]{:S(2)}) collective-permute-start(s16[288,128]{1,0:T(8,128)(2,1)S(1)} %get-tuple-element.61), channel_id=1, source_target_pairs={{0,2},{1,3},{4,6},{5,7},{8,10},{9,11},{12,14},{13,15},{18,16},{19,... | collective-permute-start | bytes 221192 | tf_op jit(solution)/shard_map/ppermute | solution.py:280
  63.7 6.2 %collective-permute-start.13 = (s16[288,128]{1,0:T(8,128)(2,1)S(1)}, s16[288,128]{1,0:T(8,128)(2,1)S(1)}, u32[]{:S(2)}, u32[]{:S(2)}) collective-permute-start(s16[288,128]{1,0:T(8,128)(2,1)S(1)} %get-tuple-element.60), channel_id=1, source_target_pairs={{0,1},{2,3},{3,2},{4,5},{6,7},{7,6},{9,8},{10,11},{11,10},{13,12},... | collective-permute-start | bytes 221192 | tf_op jit(solution)/shard_map/ppermute | solution.py:280
  65.7 8.2 %collective-permute-start.15 = (s16[288,128]{1,0:T(8,128)(2,1)S(1)}, s16[288,128]{1,0:T(8,128)(2,1)S(1)}, u32[]{:S(2)}, u32[]{:S(2)}) collective-permute-start(s16[288,128]{1,0:T(8,128)(2,1)S(1)} %get-tuple-element.62), channel_id=1, source_target_pairs={{0,3},{1,2},{4,7},{5,6},{8,11},{9,10},{12,15},{13,14},{18,17},{19,... | collective-permute-start | bytes 221192 | tf_op jit(solution)/shard_map/ppermute | solution.py:280

commit v6 on v5

--- a/solution.py
+++ b/solution.py
@@ -300,12 +300,11 @@
         smem=(0,),
         scratch=[pltpu.SMEM((mass_blocks.shape[0],), jnp.int32)],
     )
-    out1, weighted = lax.optimization_barrier((out1, weighted))
     s1 = to_plane(out1, 1)
+    s1b = to_plane(out3, 1)
     square_arrived = swap(square_other)
     out3, square_arrived = lax.optimization_barrier((out3, square_arrived))
     s3 = to_plane(out3, 3)
-    s1b = to_plane(out3, 1)
 
     own, other, later = call(
         functools.partial(stage_c_kernel, scale),

time: 75.5 us -> 65.2 us (0.86)
  waiting for transfers between devices: 45.4 us -> 35 us
  starting transfers between devices: 21.1 us -> 21.9 us
    ppermute x4, waiting for transfers between devices: 24 us -> 13.5 us  [to_plane(): return lax.ppermute(array, 'snap', [(i, i ^ m) for i in range(planes)])]
  transfers between devices with their start and end apart: 16 -> 16, of which waited for: 11 -> 11; matrix products, arithmetic and copies ran while one was open for 0% -> 0% of each run, Pallas kernels for 5% -> 6%
where the time goes in v6:
time: 65.2 us; the launch traced here: 64.9 us
  waiting for transfers between devices  35 us (54%)
  starting transfers between devices  21.9 us (34%)
  Pallas kernels  6.35 us (10%)
  local copies, waits for them, and re-layouts  1.46 us (2%)
    ppermute x9, waiting for transfers between devices, send(): return lax.ppermute(array, ('cells', 'snap'), pairs)  17.4 us
    ppermute x9, starting transfers between devices, send(): return lax.ppermute(array, ('cells', 'snap'), pairs)  16.4 us
    ppermute x4, waiting for transfers between devices, to_plane(): return lax.ppermute(array, 'snap', [(i, i ^ m) for i in range(planes)])  13.5 us
    pallas_call x8, Pallas kernels, call(): pl.pallas_call(kernel, out_shape=[jax.ShapeDtypeStruct(s, t) for s, t in...  6.35 us
    ppermute x4, starting transfers between devices, to_plane(): return lax.ppermute(array, 'snap', [(i, i ^ m) for i in range(planes)])  5.28 us
    ppermute x3, waiting for transfers between devices, swap(): return lax.ppermute(array, 'cells', [(c, c ^ 1) for c in range(devices)])  4.07 us
    dynamic_slice x1, local copies, waits for them, and re-layouts, rows_of(): return lax.dynamic_slice_in_dim(array, (z ^ m) * rows, rows, axis=1)  1.45 us
  transfers between devices with their start and end apart: 16, of which 11 were waited for; matrix products, arithmetic and copies ran while one was open for 0% of the time, Pallas kernels for 6%

profile of v6, /device:TPU:4, one launch (start us, length us, event | category | flops | bytes accessed | tf_op | source)
XLA Modules:
  0.0 64.9 jit_solution(11924699319038429819)
XLA Ops:
  0.0 0.0 copy-start
  0.0 0.0 copy-start.2
  0.0 0.0 copy-start.1
  0.0 1.4 %constant_dynamic-slice_fusion = (bf16[3,256,256]{2,1,0:T(8,128)(2,1)S(1)}, bf16[3,256,256]{2,1,0:T(8,128)(2,1)S(1)}, bf16[3,256,256]{2,1,0:T(8,128)(2,1)S(1)}) fusion(bf16[3,1024,256]{2,1,0:T(8,128)(2,1)} %s_ref.5, s32[]{:T(128)S(6)} %select_n.11, s32[]{:T(128)S(6)} %select_n.10, s32[]{:T(128)S(6)} %select_n.9), kind=kLoop, calls=%fused_computation | loop fusion | bytes 2359308 | tf_op jit(solution)/shard_map/dynamic_slice | solution.py:271
  1.5 2.7 %collective-permute-start.1 = (bf16[3,256,256]{2,1,0:T(8,128)(2,1)S(1)}, bf16[3,256,256]{2,1,0:T(8,128)(2,1)S(1)}, u32[]{:S(2)}, u32[]{:S(2)}) collective-permute-start(bf16[3,256,256]{2,1,0:T(8,128)(2,1)S(1)} %get-tuple-element.60), channel_id=1, source_target_pairs={{0,2},{1,3},{2,0},{3,1},{4,6},{5,7},{6,4},{7,5},{8,10},{9,11},{10,... | collective-permute-start | bytes 1179656 | tf_op jit(solution)/shard_map/ppermute | solution.py:268
  4.1 1.6 %collective-permute-start = (bf16[3,256,256]{2,1,0:T(8,128)(2,1)S(1)}, bf16[3,256,256]{2,1,0:T(8,128)(2,1)S(1)}, u32[]{:S(2)}, u32[]{:S(2)}) collective-permute-start(bf16[3,256,256]{2,1,0:T(8,128)(2,1)S(1)} %get-tuple-element.61), channel_id=1, source_target_pairs={{0,1},{1,0},{2,3},{3,2},{4,5},{5,4},{6,7},{7,6},{8,9},{9,8},{10,11... | collective-permute-start | bytes 1179656 | tf_op jit(solution)/shard_map/ppermute | solution.py:268
  5.7 0.0 copy-done
  5.7 0.0 copy-done.2
  5.7 0.0 copy-done.1
  5.7 2.3 %early.1 = (bf16[4,256,256]{2,1,0:T(8,128)(2,1)S(1)}, bf16[3,1024,256]{2,1,0:T(8,128)(2,1)S(1)}, f32[256,128]{1,0:T(8,128)S(1)}, f32[256,128]{1,0:T(8,128)S(1)}) custom-call(s32[16]{0:T(128)S(1)} %copy-done.2, bf16[16,64,64]{2,1,0:T(8,128)(2,1)S(1)} %copy-done.1, bf16[3,1024,256]{2,1,0:T(8,128)(2,1)S(1)} %copy-done), custom_call_target="tpu_custom_call" | custom-call | tf_op jit(solution)/shard_map/early/pallas_call | solution.py:245
  8.0 0.1 collective-permute-start.3
  8.1 0.5 collective-permute-start.2
  8.6 0.8 %collective-permute-done.3.other_ref = f32[256,128]{1,0:T(8,128)S(1)} collective-permute-done((f32[256,128]{1,0:T(8,128)S(1)}, f32[256,128]{1,0:T(8,128)S(1)}, u32[]{:S(2)}, u32[]{:S(2)}) %collective-permute-start.3) | collective-permute-done | bytes 131104 | tf_op jit(solution)/shard_map/ppermute | solution.py:283
  9.4 0.5 collective-permute-start.4
  10.0 12.9 %collective-permute-done.1.s2_ref = bf16[3,256,256]{2,1,0:T(8,128)(2,1)S(1)} collective-permute-done((bf16[3,256,256]{2,1,0:T(8,128)(2,1)S(1)}, bf16[3,256,256]{2,1,0:T(8,128)(2,1)S(1)}, u32[]{:S(2)}, u32[]{:S(2)}) %collective-permute-start.1) | collective-permute-done | bytes 393248 | tf_op jit(solution)/shard_map/ppermute | solution.py:268
  22.9 0.6 collective-permute-done.s1_ref
  23.5 0.8 %stage_c.1 = (f32[3,256,128]{2,1,0:T(8,128)S(1)}, s16[800,128]{1,0:T(8,128)(2,1)S(1)}, f32[256,256]{1,0:T(8,128)S(1)}) custom-call(bf16[3,1024,256]{2,1,0:T(8,128)(2,1)S(1)} %copy-done, bf16[3,1024,256]{2,1,0:T(8,128)(2,1)S(1)} %get-tuple-element.32.weighted_ref, bf16[4,256,256]{2,1,0:T(8,128)(2,1)S(1)} %get-tuple-element.33.diagonal_ref, ...), custom_call_target="tpu_custom_call" | custom-call | tf_op jit(solution)/shard_map/stage_c/pallas_call | solution.py:245
  24.3 0.1 collective-permute-start.5
  24.4 1.4 %collective-permute-done.5.arrived_ref = s16[800,128]{1,0:T(8,128)(2,1)S(1)} collective-permute-done((s16[800,128]{1,0:T(8,128)(2,1)S(1)}, s16[800,128]{1,0:T(8,128)(2,1)S(1)}, u32[]{:S(2)}, u32[]{:S(2)}) %collective-permute-start.5) | collective-permute-done | bytes 204832 | tf_op jit(solution)/shard_map/ppermute | solution.py:283
  25.9 0.2 combine_c.1
  26.1 1.3 %collective-permute-start.6 = (s16[544,128]{1,0:T(8,128)(2,1)S(1)}, s16[544,128]{1,0:T(8,128)(2,1)S(1)}, u32[]{:S(2)}, u32[]{:S(2)}) collective-permute-start(s16[544,128]{1,0:T(8,128)(2,1)S(1)} %get-tuple-element.42), channel_id=1, source_target_pairs={{0,8},{1,9},{3,11},{4,12},{5,13},{7,15},{8,0},{9,1},{10,2},{12,4},... | collective-permute-start | bytes 417800 | tf_op jit(solution)/shard_map/ppermute | solution.py:280
  27.4 4.5 %collective-permute-start.7 = (s16[544,128]{1,0:T(8,128)(2,1)S(1)}, s16[544,128]{1,0:T(8,128)(2,1)S(1)}, u32[]{:S(2)}, u32[]{:S(2)}) collective-permute-start(s16[544,128]{1,0:T(8,128)(2,1)S(1)} %get-tuple-element.43), channel_id=1, source_target_pairs={{0,16},{2,18},{3,19},{4,20},{6,22},{7,23},{9,25},{10,26},{11,27},{... | collective-permute-start | bytes 417800 | tf_op jit(solution)/shard_map/ppermute | solution.py:280
  31.9 1.9 %collective-permute-start.8 = (s16[544,128]{1,0:T(8,128)(2,1)S(1)}, s16[544,128]{1,0:T(8,128)(2,1)S(1)}, u32[]{:S(2)}, u32[]{:S(2)}) collective-permute-start(s16[544,128]{1,0:T(8,128)(2,1)S(1)} %get-tuple-element.44), channel_id=1, source_target_pairs={{1,25},{2,26},{3,27},{5,29},{6,30},{7,31},{8,16},{10,18},{11,19},{... | collective-permute-start | bytes 417800 | tf_op jit(solution)/shard_map/ppermute | solution.py:280
  33.9 0.0 collective-permute-done.6.m1_ref
  33.9 1.7 %collective-permute-done.7.m2_ref = s16[544,128]{1,0:T(8,128)(2,1)S(1)} collective-permute-done((s16[544,128]{1,0:T(8,128)(2,1)S(1)}, s16[544,128]{1,0:T(8,128)(2,1)S(1)}, u32[]{:S(2)}, u32[]{:S(2)}) %collective-permute-start.7) | collective-permute-done | bytes 139296 | tf_op jit(solution)/shard_map/ppermute | solution.py:280
  35.6 4.3 %collective-permute-done.8.m3_ref = s16[544,128]{1,0:T(8,128)(2,1)S(1)} collective-permute-done((s16[544,128]{1,0:T(8,128)(2,1)S(1)}, s16[544,128]{1,0:T(8,128)(2,1)S(1)}, u32[]{:S(2)}, u32[]{:S(2)}) %collective-permute-start.8) | collective-permute-done | bytes 139296 | tf_op jit(solution)/shard_map/ppermute | solution.py:280
  39.9 0.2 plane_c.1
  40.1 0.0 collective-permute-done.2.s1b_ref
  40.1 0.0 collective-permute-done.4.s3_ref
  40.1 1.4 %stage_d.1 = (f32[7,256,128]{2,1,0:T(8,128)S(1)}, s16[1824,128]{1,0:T(8,128)(2,1)S(1)}) custom-call(bf16[3,1024,256]{2,1,0:T(8,128)(2,1)S(1)} %copy-done, bf16[3,1024,256]{2,1,0:T(8,128)(2,1)S(1)} %get-tuple-element.32.weighted_ref, bf16[4,256,256]{2,1,0:T(8,128)(2,1)S(1)} %get-tuple-element.33.diagonal_ref, f32[256,256]{1,0:T(8,128)S(1)} %get-tuple-element.34.later_ref, ...), custom_call_target="tpu_custom_call" | custom-call | tf_op jit(solution)/shard_map/stage_d/pallas_call | solution.py:245
  41.5 0.1 collective-permute-start.9
  41.6 1.8 %collective-permute-done.9.arrived_ref = s16[1824,128]{1,0:T(8,128)(2,1)S(1)} collective-permute-done((s16[1824,128]{1,0:T(8,128)(2,1)S(1)}, s16[1824,128]{1,0:T(8,128)(2,1)S(1)}, u32[]{:S(2)}, u32[]{:S(2)}) %collective-permute-start.9) | collective-permute-done | bytes 466976 | tf_op jit(solution)/shard_map/ppermute | solution.py:283
  43.4 0.5 combine_d.1
  43.9 1.1 %collective-permute-start.10 = (s16[544,128]{1,0:T(8,128)(2,1)S(1)}, s16[544,128]{1,0:T(8,128)(2,1)S(1)}, u32[]{:S(2)}, u32[]{:S(2)}) collective-permute-start(s16[544,128]{1,0:T(8,128)(2,1)S(1)} %get-tuple-element.51), channel_id=1, source_target_pairs={{0,8},{1,9},{2,10},{3,11},{4,12},{5,13},{6,14},{7,15},{8,0},{9,1},... | collective-permute-start | bytes 417800 | tf_op jit(solution)/shard_map/ppermute | solution.py:280
  45.0 0.5 collective-permute-start.11
  45.4 2.0 %collective-permute-start.12 = (s16[544,128]{1,0:T(8,128)(2,1)S(1)}, s16[544,128]{1,0:T(8,128)(2,1)S(1)}, u32[]{:S(2)}, u32[]{:S(2)}) collective-permute-start(s16[544,128]{1,0:T(8,128)(2,1)S(1)} %get-tuple-element.53), channel_id=1, source_target_pairs={{0,24},{1,25},{2,26},{3,27},{4,28},{5,29},{6,30},{7,31},{8,16},{9,... | collective-permute-start | bytes 417800 | tf_op jit(solution)/shard_map/ppermute | solution.py:280
  47.4 1.3 %collective-permute-start.14 = (s16[288,128]{1,0:T(8,128)(2,1)S(1)}, s16[288,128]{1,0:T(8,128)(2,1)S(1)}, u32[]{:S(2)}, u32[]{:S(2)}) collective-permute-start(s16[288,128]{1,0:T(8,128)(2,1)S(1)} %get-tuple-element.57), channel_id=1, source_target_pairs={{0,2},{1,3},{4,6},{5,7},{8,10},{9,11},{12,14},{13,15},{18,16},{19,... | collective-permute-start | bytes 221192 | tf_op jit(solution)/shard_map/ppermute | solution.py:280
  48.7 1.7 %collective-permute-done.10.m1_ref = s16[544,128]{1,0:T(8,128)(2,1)S(1)} collective-permute-done((s16[544,128]{1,0:T(8,128)(2,1)S(1)}, s16[544,128]{1,0:T(8,128)(2,1)S(1)}, u32[]{:S(2)}, u32[]{:S(2)}) %collective-permute-start.10) | collective-permute-done | bytes 139296 | tf_op jit(solution)/shard_map/ppermute | solution.py:280
  50.5 2.9 %collective-permute-done.11.m2_ref = s16[544,128]{1,0:T(8,128)(2,1)S(1)} collective-permute-done((s16[544,128]{1,0:T(8,128)(2,1)S(1)}, s16[544,128]{1,0:T(8,128)(2,1)S(1)}, u32[]{:S(2)}, u32[]{:S(2)}) %collective-permute-start.11) | collective-permute-done | bytes 139296 | tf_op jit(solution)/shard_map/ppermute | solution.py:280
  53.4 0.0 collective-permute-done.12.m3_ref
  53.4 0.2 plane_d.1
  53.6 2.5 %collective-permute-start.13 = (s16[288,128]{1,0:T(8,128)(2,1)S(1)}, s16[288,128]{1,0:T(8,128)(2,1)S(1)}, u32[]{:S(2)}, u32[]{:S(2)}) collective-permute-start(s16[288,128]{1,0:T(8,128)(2,1)S(1)} %get-tuple-element.56), channel_id=1, source_target_pairs={{0,1},{2,3},{3,2},{4,5},{6,7},{7,6},{9,8},{10,11},{11,10},{13,12},... | collective-permute-start | bytes 221192 | tf_op jit(solution)/shard_map/ppermute | solution.py:280
  56.1 1.3 %collective-permute-start.15 = (s16[288,128]{1,0:T(8,128)(2,1)S(1)}, s16[288,128]{1,0:T(8,128)(2,1)S(1)}, u32[]{:S(2)}, u32[]{:S(2)}) collective-permute-start(s16[288,128]{1,0:T(8,128)(2,1)S(1)} %get-tuple-element.58), channel_id=1, source_target_pairs={{0,3},{1,2},{4,7},{5,6},{8,11},{9,10},{12,15},{13,14},{18,17},{19,... | collective-permute-start | bytes 221192 | tf_op jit(solution)/shard_map/ppermute | solution.py:280
  57.4 0.0 collective-permute-done.14.m2_ref
  57.4 2.4 %collective-permute-done.13.m1_ref = s16[288,128]{1,0:T(8,128)(2,1)S(1)} collective-permute-done((s16[288,128]{1,0:T(8,128)(2,1)S(1)}, s16[288,128]{1,0:T(8,128)(2,1)S(1)}, u32[]{:S(2)}, u32[]{:S(2)}) %collective-permute-start.13) | collective-permute-done | bytes 73760 | tf_op jit(solution)/shard_map/ppermute | solution.py:280
  59.8 4.4 %collective-permute-done.15.m3_ref = s16[288,128]{1,0:T(8,128)(2,1)S(1)} collective-permute-done((s16[288,128]{1,0:T(8,128)(2,1)S(1)}, s16[288,128]{1,0:T(8,128)(2,1)S(1)}, u32[]{:S(2)}, u32[]{:S(2)}) %collective-permute-start.15) | collective-permute-done | bytes 73760 | tf_op jit(solution)/shard_map/ppermute | solution.py:280
  64.2 0.7 %last.1 = f32[256,128]{1,0:T(8,128)} custom-call(f32[256,128]{1,0:T(8,128)S(1)} %get-tuple-element.55.keep_ref, s16[288,128]{1,0:T(8,128)(2,1)S(1)} %collective-permute-done.13.m1_ref, s16[288,128]{1,0:T(8,128)(2,1)S(1)} %collective-permute-done.14.m2_ref, s16[288,128]{1,0:T(8,128)(2,1)S(1)} %collective-permute-done.15.m3_ref), custom_call_target="tpu_custom_call" | custom-call | tf_op jit(solution)/shard_map/last/pallas_call | solution.py:245
Async XLA Ops:
  0.0 5.7 %copy-start = (bf16[3,1024,256]{2,1,0:T(8,128)(2,1)S(1)}, bf16[3,1024,256]{2,1,0:T(8,128)(2,1)}, u32[]{:S(2)}) copy-start(bf16[3,1024,256]{2,1,0:T(8,128)(2,1)} %s_ref.5) | copy-start | bytes 4718596
  0.0 5.7 %copy-start.2 = (s32[16]{0:T(128)S(1)}, s32[16]{0:T(128)}, u32[]{:S(2)}) copy-start(s32[16]{0:T(128)} %offsets_ref.1) | copy-start | bytes 196
  0.0 5.7 %copy-start.1 = (bf16[16,64,64]{2,1,0:T(8,128)(2,1)S(1)}, bf16[16,64,64]{2,1,0:T(8,128)(2,1)}, u32[]{:S(2)}) copy-start(bf16[16,64,64]{2,1,0:T(8,128)(2,1)} %mass_ref.1) | copy-start | bytes 393220
  1.5 21.4 %collective-permute-start.1 = (bf16[3,256,256]{2,1,0:T(8,128)(2,1)S(1)}, bf16[3,256,256]{2,1,0:T(8,128)(2,1)S(1)}, u32[]{:S(2)}, u32[]{:S(2)}) collective-permute-start(bf16[3,256,256]{2,1,0:T(8,128)(2,1)S(1)} %get-tuple-element.60), channel_id=1, source_target_pairs={{0,2},{1,3},{2,0},{3,1},{4,6},{5,7},{6,4},{7,5},{8,10},{9,11},{10,... | collective-permute-start | bytes 1179656 | tf_op jit(solution)/shard_map/ppermute | solution.py:268
  4.1 19.4 %collective-permute-start = (bf16[3,256,256]{2,1,0:T(8,128)(2,1)S(1)}, bf16[3,256,256]{2,1,0:T(8,128)(2,1)S(1)}, u32[]{:S(2)}, u32[]{:S(2)}) collective-permute-start(bf16[3,256,256]{2,1,0:T(8,128)(2,1)S(1)} %get-tuple-element.61), channel_id=1, source_target_pairs={{0,1},{1,0},{2,3},{3,2},{4,5},{5,4},{6,7},{7,6},{8,9},{9,8},{10,11... | collective-permute-start | bytes 1179656 | tf_op jit(solution)/shard_map/ppermute | solution.py:268
  8.0 1.4 %collective-permute-start.3 = (f32[256,128]{1,0:T(8,128)S(1)}, f32[256,128]{1,0:T(8,128)S(1)}, u32[]{:S(2)}, u32[]{:S(2)}) collective-permute-start(f32[256,128]{1,0:T(8,128)S(1)} %get-tuple-element.35), channel_id=1, source_target_pairs={{0,4},{4,0},{8,12},{12,8},{16,20},{20,16},{24,28},{28,24},{1,5},{5... | collective-permute-start | bytes 393224 | tf_op jit(solution)/shard_map/ppermute | solution.py:283
  8.1 32.0 %collective-permute-start.2 = (bf16[3,256,256]{2,1,0:T(8,128)(2,1)S(1)}, bf16[3,256,256]{2,1,0:T(8,128)(2,1)S(1)}, u32[]{:S(2)}, u32[]{:S(2)}) collective-permute-start(bf16[3,256,256]{2,1,0:T(8,128)(2,1)S(1)} %get-tuple-element.36), channel_id=1, source_target_pairs={{0,1},{1,0},{2,3},{3,2},{4,5},{5,4},{6,7},{7,6},{8,9},{9,8},{10,11... | collective-permute-start | bytes 1179656 | tf_op jit(solution)/shard_map/ppermute | solution.py:268
  9.4 30.7 %collective-permute-start.4 = (bf16[3,256,256]{2,1,0:T(8,128)(2,1)S(1)}, bf16[3,256,256]{2,1,0:T(8,128)(2,1)S(1)}, u32[]{:S(2)}, u32[]{:S(2)}) collective-permute-start(bf16[3,256,256]{2,1,0:T(8,128)(2,1)S(1)} %get-tuple-element.36), channel_id=1, source_target_pairs={{0,3},{1,2},{2,1},{3,0},{4,7},{5,6},{6,5},{7,4},{8,11},{9,10},{10,... | collective-permute-start | bytes 1179656 | tf_op jit(solution)/shard_map/ppermute | solution.py:268
  24.3 1.5 %collective-permute-start.5 = (s16[800,128]{1,0:T(8,128)(2,1)S(1)}, s16[800,128]{1,0:T(8,128)(2,1)S(1)}, u32[]{:S(2)}, u32[]{:S(2)}) collective-permute-start(s16[800,128]{1,0:T(8,128)(2,1)S(1)} %get-tuple-element.38), channel_id=1, source_target_pairs={{0,4},{4,0},{8,12},{12,8},{16,20},{20,16},{24,28},{28,24},{1,5},{5... | collective-permute-start | bytes 614408 | tf_op jit(solution)/shard_map/ppermute | solution.py:283
  26.1 7.8 %collective-permute-start.6 = (s16[544,128]{1,0:T(8,128)(2,1)S(1)}, s16[544,128]{1,0:T(8,128)(2,1)S(1)}, u32[]{:S(2)}, u32[]{:S(2)}) collective-permute-start(s16[544,128]{1,0:T(8,128)(2,1)S(1)} %get-tuple-element.42), channel_id=1, source_target_pairs={{0,8},{1,9},{3,11},{4,12},{5,13},{7,15},{8,0},{9,1},{10,2},{12,4},... | collective-permute-start | bytes 417800 | tf_op jit(solution)/shard_map/ppermute | solution.py:280
  27.4 8.2 %collective-permute-start.7 = (s16[544,128]{1,0:T(8,128)(2,1)S(1)}, s16[544,128]{1,0:T(8,128)(2,1)S(1)}, u32[]{:S(2)}, u32[]{:S(2)}) collective-permute-start(s16[544,128]{1,0:T(8,128)(2,1)S(1)} %get-tuple-element.43), channel_id=1, source_target_pairs={{0,16},{2,18},{3,19},{4,20},{6,22},{7,23},{9,25},{10,26},{11,27},{... | collective-permute-start | bytes 417800 | tf_op jit(solution)/shard_map/ppermute | solution.py:280
  31.9 7.9 %collective-permute-start.8 = (s16[544,128]{1,0:T(8,128)(2,1)S(1)}, s16[544,128]{1,0:T(8,128)(2,1)S(1)}, u32[]{:S(2)}, u32[]{:S(2)}) collective-permute-start(s16[544,128]{1,0:T(8,128)(2,1)S(1)} %get-tuple-element.44), channel_id=1, source_target_pairs={{1,25},{2,26},{3,27},{5,29},{6,30},{7,31},{8,16},{10,18},{11,19},{... | collective-permute-start | bytes 417800 | tf_op jit(solution)/shard_map/ppermute | solution.py:280
  41.5 1.9 %collective-permute-start.9 = (s16[1824,128]{1,0:T(8,128)(2,1)S(1)}, s16[1824,128]{1,0:T(8,128)(2,1)S(1)}, u32[]{:S(2)}, u32[]{:S(2)}) collective-permute-start(s16[1824,128]{1,0:T(8,128)(2,1)S(1)} %get-tuple-element.49), channel_id=1, source_target_pairs={{0,4},{4,0},{8,12},{12,8},{16,20},{20,16},{24,28},{28,24},{1,5},{5... | collective-permute-start | bytes 1400840 | tf_op jit(solution)/shard_map/ppermute | solution.py:283
  43.9 6.6 %collective-permute-start.10 = (s16[544,128]{1,0:T(8,128)(2,1)S(1)}, s16[544,128]{1,0:T(8,128)(2,1)S(1)}, u32[]{:S(2)}, u32[]{:S(2)}) collective-permute-start(s16[544,128]{1,0:T(8,128)(2,1)S(1)} %get-tuple-element.51), channel_id=1, source_target_pairs={{0,8},{1,9},{2,10},{3,11},{4,12},{5,13},{6,14},{7,15},{8,0},{9,1},... | collective-permute-start | bytes 417800 | tf_op jit(solution)/shard_map/ppermute | solution.py:280
  45.0 8.4 %collective-permute-start.11 = (s16[544,128]{1,0:T(8,128)(2,1)S(1)}, s16[544,128]{1,0:T(8,128)(2,1)S(1)}, u32[]{:S(2)}, u32[]{:S(2)}) collective-permute-start(s16[544,128]{1,0:T(8,128)(2,1)S(1)} %get-tuple-element.52), channel_id=1, source_target_pairs={{0,16},{1,17},{2,18},{3,19},{4,20},{5,21},{6,22},{7,23},{8,24},{9,... | collective-permute-start | bytes 417800 | tf_op jit(solution)/shard_map/ppermute | solution.py:280
  45.4 7.9 %collective-permute-start.12 = (s16[544,128]{1,0:T(8,128)(2,1)S(1)}, s16[544,128]{1,0:T(8,128)(2,1)S(1)}, u32[]{:S(2)}, u32[]{:S(2)}) collective-permute-start(s16[544,128]{1,0:T(8,128)(2,1)S(1)} %get-tuple-element.53), channel_id=1, source_target_pairs={{0,24},{1,25},{2,26},{3,27},{4,28},{5,29},{6,30},{7,31},{8,16},{9,... | collective-permute-start | bytes 417800 | tf_op jit(solution)/shard_map/ppermute | solution.py:280
  47.4 10.0 %collective-permute-start.14 = (s16[288,128]{1,0:T(8,128)(2,1)S(1)}, s16[288,128]{1,0:T(8,128)(2,1)S(1)}, u32[]{:S(2)}, u32[]{:S(2)}) collective-permute-start(s16[288,128]{1,0:T(8,128)(2,1)S(1)} %get-tuple-element.57), channel_id=1, source_target_pairs={{0,2},{1,3},{4,6},{5,7},{8,10},{9,11},{12,14},{13,15},{18,16},{19,... | collective-permute-start | bytes 221192 | tf_op jit(solution)/shard_map/ppermute | solution.py:280
  53.6 6.2 %collective-permute-start.13 = (s16[288,128]{1,0:T(8,128)(2,1)S(1)}, s16[288,128]{1,0:T(8,128)(2,1)S(1)}, u32[]{:S(2)}, u32[]{:S(2)}) collective-permute-start(s16[288,128]{1,0:T(8,128)(2,1)S(1)} %get-tuple-element.56), channel_id=1, source_target_pairs={{0,1},{2,3},{3,2},{4,5},{6,7},{7,6},{9,8},{10,11},{11,10},{13,12},... | collective-permute-start | bytes 221192 | tf_op jit(solution)/shard_map/ppermute | solution.py:280
  56.1 8.0 %collective-permute-start.15 = (s16[288,128]{1,0:T(8,128)(2,1)S(1)}, s16[288,128]{1,0:T(8,128)(2,1)S(1)}, u32[]{:S(2)}, u32[]{:S(2)}) collective-permute-start(s16[288,128]{1,0:T(8,128)(2,1)S(1)} %get-tuple-element.58), channel_id=1, source_target_pairs={{0,3},{1,2},{4,7},{5,6},{8,11},{9,10},{12,15},{13,14},{18,17},{19,... | collective-permute-start | bytes 221192 | tf_op jit(solution)/shard_map/ppermute | solution.py:280

commit v7 on v6

--- a/solution.py
+++ b/solution.py
@@ -35,9 +35,12 @@
     return result * factor
 
 
-STAGE_C = ((2, 0), (2, 1), (0, 2))
-STAGE_D = ((1, 0), (3, 0), (0, 1), (3, 1), (0, 3), (1, 3), (1, 2))
-START_D = (0, 2, 5, 4)
+STAGE_C = ((1, 3), (3, 0), (3, 1), (0, 3))
+STAGE_D = ((2, 0), (1, 0), (0, 2), (2, 1))
+STAGE_B = ((0, 1), (1, 2))
+GO_EARLY = {1: (3, 0), 2: (3, 1)}
+GO_FIRST = {0: (2, 0), 1: (1, 0), 3: (2, 1)}
+GO_LAST = {0: (1, 3), 2: (1, 2)}
 
 
 def tdot(left, right):
@@ -94,68 +97,61 @@
     own_ref[...], other_ref[...] = halves(cells % 2, total * scale)
 
 
-def stage_c_kernel(
-    scale, s_ref, weighted_ref, diagonal_ref, s1_ref, s2_ref, own_ref, other_ref, later_ref
-):
-    z, core = lax.axis_index("snap"), lax.axis_index("cells") % 2
-    rows = s2_ref.shape[1]
-    mine = pl.ds(pl.multiple_of(z * rows, rows), rows)
-    diagonal = diagonal_ref[z]
-    s0, w0 = flat(s_ref[:, mine, :]), flat(weighted_ref[:, mine, :])
-    s1, s2 = flat(s1_ref[...]), flat(s2_ref[...])
-    w1, w2 = weigh(diagonal, s1_ref[...]), weigh(diagonal, s2_ref[...])
-    blocks = {(2, 0): tdot(s2, w0), (2, 1): tdot(s2, w1), (0, 2): tdot(s0, w2)}
+def emit(scale, blocks, own_ref, other_ref):
+    core = lax.axis_index("cells") % 2
     others = []
-    for at, name in enumerate(STAGE_C):
-        own_ref[at], other = halves(core, blocks[name] * scale)
+    for at, block in enumerate(blocks):
+        own_ref[at], other = halves(core, block * scale)
         others.append(other)
     encode(jnp.stack(others), other_ref)
-    later_ref[...] = tdot(s1, w2)
+
+
+def quarter(z, ref):
+    rows = ref.shape[1] // lax.axis_size("snap")
+    return flat(ref[:, pl.ds(pl.multiple_of(z * rows, rows), rows), :])
+
+
+def stage_c_kernel(
+    scale, s_ref, weighted_ref, diagonal_ref, s1_ref, s3_ref, own_ref, other_ref, w1_ref
+):
+    z = lax.axis_index("snap")
+    diagonal = diagonal_ref[z]
+    s0, w0 = quarter(z, s_ref), quarter(z, weighted_ref)
+    s1, s3 = flat(s1_ref[...]), flat(s3_ref[...])
+    w1, w3 = weigh(diagonal, s1_ref[...]), weigh(diagonal, s3_ref[...])
+    w1_ref[...] = w1
+    blocks = {(3, 0): (s3, w0), (3, 1): (s3, w1), (0, 3): (s0, w3), (1, 3): (s1, w3)}
+    emit(scale, [tdot(*blocks[name]) for name in STAGE_C], own_ref, other_ref)
 
 
 def stage_d_kernel(
-    scale,
-    s_ref,
-    weighted_ref,
-    diagonal_ref,
-    later_ref,
-    s1_ref,
-    s1b_ref,
-    s3_ref,
-    own_ref,
-    other_ref,
+    scale, s_ref, weighted_ref, diagonal_ref, s1_ref, w1_ref, s1b_ref, s2_ref, own_ref, other_ref
 ):
-    z, core = lax.axis_index("snap"), lax.axis_index("cells") % 2
-    rows = s3_ref.shape[1]
+    z = lax.axis_index("snap")
     across = z ^ 2
-    mine = pl.ds(pl.multiple_of(z * rows, rows), rows)
-    more = pl.ds(pl.multiple_of(across * rows, rows), rows)
-    diagonal = diagonal_ref[z]
-    s0, w0 = flat(s_ref[:, mine, :]), flat(weighted_ref[:, mine, :])
-    s0b, w0b = flat(s_ref[:, more, :]), flat(weighted_ref[:, more, :])
-    s1, s1b, s3 = flat(s1_ref[...]), flat(s1b_ref[...]), flat(s3_ref[...])
-    w1, w3 = weigh(diagonal, s1_ref[...]), weigh(diagonal, s3_ref[...])
+    s0, w0 = quarter(z, s_ref), quarter(z, weighted_ref)
+    s0b, w0b = quarter(across, s_ref), quarter(across, weighted_ref)
+    s1, s1b, s2, w1 = flat(s1_ref[...]), flat(s1b_ref[...]), flat(s2_ref[...]), w1_ref[...]
     w1b = weigh(diagonal_ref[across], s1b_ref[...])
+    w2 = weigh(diagonal_ref[z], s2_ref[...])
     blocks = {
+        (0, 1): tdot(s0, w1) + tdot(s0b, w1b),
         (1, 0): tdot(s1, w0) + tdot(s1b, w0b),
-        (3, 0): tdot(s3, w0),
-        (0, 1): tdot(s0, w1) + tdot(s0b, w1b),
-        (3, 1): tdot(s3, w1),
-        (0, 3): tdot(s0, w3),
-        (1, 3): tdot(s1, w3),
-        (1, 2): later_ref[...],
+        (2, 0): tdot(s2, w0),
+        (2, 1): tdot(s2, w1),
+        (1, 2): tdot(s1, w2),
+        (0, 2): tdot(s0, w2),
     }
-    others = []
-    for at, name in enumerate(STAGE_D):
-        own_ref[at], other = halves(core, blocks[name] * scale)
-        others.append(other)
-    encode(jnp.stack(others), other_ref)
+    emit(scale, [blocks[name] for name in STAGE_D + STAGE_B], own_ref, other_ref)
 
 
 GROUP = 64
-TAIL = 32
 STEPS = 256.0
 TOP = 32700.0
+
+
+def tail(slots, rows):
+    return -(-slots * rows // (GROUP * 16)) * 16
 
 
 def encode(value, message_ref):
@@ -167,13 +163,14 @@
     code = jnp.round(value * (TOP * jnp.exp2(step * (-1.0 / STEPS)))[:, None, :])
     codes = code.reshape(slots * rows, columns).astype(jnp.int32).astype(jnp.int16)
     message_ref[: slots * rows] = codes
-    step = jnp.concatenate([step, jnp.zeros((TAIL - groups, columns), F32)], axis=0)
+    more = tail(slots, rows) - groups
+    if more:
+        step = jnp.concatenate([step, jnp.zeros((more, columns), F32)], axis=0)
     message_ref[slots * rows :] = step.astype(jnp.int32).astype(jnp.int16)
 
 
-def decode(message_ref, slots):
-    total, columns = message_ref.shape
-    rows = (total - TAIL) // slots
+def decode(message_ref, slots, rows):
+    columns = message_ref.shape[1]
     groups = slots * rows // GROUP
     step = message_ref[slots * rows :].astype(jnp.int32).astype(F32)[:groups]
     code = message_ref[: slots * rows].astype(jnp.int32).astype(F32)
@@ -185,59 +182,57 @@
     return (lax.axis_index("cells") // 2) ^ lax.axis_index("snap")
 
 
-def combine_c_kernel(own_ref, arrived_ref, one_ref, other_ref, total_ref, *message_refs):
+def combine_kernel(own_ref, arrived_ref, total_ref, *refs):
+    *message_refs, whole_ref = refs
     q = place()
-    whole = own_ref[...] + decode(arrived_ref, len(STAGE_C))
-    square = one_ref[...] + other_ref[...]
+    whole_ref[...] = own_ref[...] + decode(arrived_ref, *own_ref.shape[:2])
+    total_ref[...] = whole_ref[pl.ds(q, 1)]
+    for m, ref in enumerate(message_refs, 1):
+        encode(whole_ref[pl.ds(q ^ m, 1)], ref)
+
+
+def combine_d_kernel(own_ref, arrived_ref, square_ref, other_ref, total_ref, *refs):
+    *message_refs, whole_ref = refs
+    q = place()
+    whole_ref[...] = own_ref[...] + decode(arrived_ref, *own_ref.shape[:2])
+    square = square_ref[...] + other_ref[...]
     for m, ref in enumerate((total_ref, *message_refs)):
         to = q ^ m
-        first = jnp.where(to == 0, whole[0], jnp.where(to == 1, whole[1], whole[2]))
-        value = jnp.stack([first, square])
+        second = jnp.where(to == 0, square, jnp.where(to == 1, whole_ref[4], whole_ref[5]))
+        value = jnp.stack([whole_ref[to], second])
         if m == 0:
             ref[...] = value
         else:
             encode(value, ref)
 
 
-def combine_d_kernel(own_ref, arrived_ref, total_ref, *refs):
-    *message_refs, whole_ref = refs
-    q = place()
-    whole_ref[...] = own_ref[...] + decode(arrived_ref, len(STAGE_D))
-    for m, ref in enumerate((total_ref, *message_refs)):
-        to = q ^ m
-        start = jnp.where(to == 1, START_D[1], jnp.where(to == 2, START_D[2], START_D[3]))
-        value = whole_ref[pl.ds(jnp.where(to == 0, START_D[0], start), 2)]
-        if m == 0:
-            ref[...] = value
-        else:
-            encode(value, ref)
-
-
 def plane_sum(total_ref, message_refs):
     total = total_ref[...]
     for ref in message_refs:
-        total += decode(ref, 2)
+        total += decode(ref, *total.shape[:2])
     return total
 
 
-def plane_c_kernel(total_ref, m1_ref, m2_ref, m3_ref, keep_ref, two_ref):
+def plane_c_kernel(total_ref, m1_ref, m2_ref, m3_ref, sum_ref, three_ref):
     total = plane_sum(total_ref, (m1_ref, m2_ref, m3_ref))
-    encode(total[:1], two_ref)
-    keep_ref[...] = jnp.where(place() == 0, total[1], total[0])
-
-
-def plane_d_kernel(total_ref, m1_ref, m2_ref, m3_ref, keep_c_ref, keep_ref, one_ref, three_ref):
+    sum_ref[...] = total
+    encode(total, three_ref)
+
+
+def plane_d_kernel(total_ref, m1_ref, m2_ref, m3_ref, sum_c_ref, keep_ref, first_ref, last_ref):
     q = place()
     total = plane_sum(total_ref, (m1_ref, m2_ref, m3_ref))
-    encode(jnp.where(q == 0, total[:1], total[1:]), one_ref)
-    encode(total[1:], three_ref)
-    keep_ref[...] = jnp.where(q % 2 == 0, keep_c_ref[...], total[0])
+    sum_c = sum_c_ref[...]
+    encode(total[:1], first_ref)
+    encode(jnp.where(q == 0, sum_c, total[1:]), last_ref)
+    keep_ref[...] = jnp.where(q < 2, total[1], jnp.where(q == 3, sum_c[0], total[0]))
 
 
 def last_kernel(keep_ref, m1_ref, m2_ref, m3_ref, out_ref):
-    out_ref[...] = (
-        keep_ref[...] + decode(m1_ref, 1)[0] + decode(m2_ref, 1)[0] + decode(m3_ref, 1)[0]
-    )
+    total = keep_ref[...]
+    for ref in (m1_ref, m2_ref, m3_ref):
+        total += decode(ref, 1, total.shape[0])[0]
+    out_ref[...] = total
 
 
 def call(kernel, outs, name, *args, smem=(), scratch=()):
@@ -279,17 +274,27 @@
                     pairs.append((c * planes + i, to_c * planes + to_i))
         return lax.ppermute(array, ("cells", "snap"), pairs)
 
+    def reach(array, blocks):
+        pairs = []
+        for c in range(devices):
+            for i in range(planes):
+                if (c // 2) ^ i in blocks:
+                    row, column = blocks[(c // 2) ^ i]
+                    to_c = 2 * (i ^ column) + c % 2
+                    pairs.append((c * planes + i, to_c * planes + (i ^ row)))
+        return lax.ppermute(array, ("cells", "snap"), pairs)
+
     def swap(array):
         return lax.ppermute(array, "cells", [(c, c ^ 1) for c in range(devices)])
 
     def coded(slots):
-        return ((slots * columns + TAIL, half), jnp.int16)
+        return ((slots * columns + tail(slots, columns), half), jnp.int16)
 
     def floats(*slots):
         return ((*slots, columns, half), F32)
 
     out2, out1, out3 = rows_of(snapshots, 2), rows_of(snapshots, 1), rows_of(snapshots, 3)
-    s2 = to_plane(out2, 2)
+    s3 = to_plane(out3, 3)
     diagonal, weighted, square, square_other = call(
         functools.partial(early_kernel, scale),
         [((planes, rows, rows), BF16), (snapshots.shape, BF16), floats(), floats()],
@@ -303,44 +308,44 @@
     s1 = to_plane(out1, 1)
     s1b = to_plane(out3, 1)
     square_arrived = swap(square_other)
-    out3, square_arrived = lax.optimization_barrier((out3, square_arrived))
-    s3 = to_plane(out3, 3)
-
-    own, other, later = call(
+    out2, weighted = lax.optimization_barrier((out2, weighted))
+    s2 = to_plane(out2, 2)
+
+    stage_c, w1 = [floats(4), coded(4)], ((components * rows, columns), BF16)
+    own, other, w1 = call(
         functools.partial(stage_c_kernel, scale),
-        [floats(len(STAGE_C)), coded(len(STAGE_C)), ((columns, columns), F32)],
+        [*stage_c, w1],
         "stage_c",
         snapshots,
         weighted,
         diagonal,
         s1,
-        s2,
+        s3,
     )
     total, *out = call(
-        combine_c_kernel,
-        [floats(2), coded(2), coded(2), coded(2)],
+        combine_kernel,
+        [floats(1), coded(1), coded(1), coded(1)],
         "combine_c",
         own,
         swap(other),
-        square,
-        square_arrived,
-    )
-    arrived = [send(out[m - 1], m, 0, (0, 1, 2)) for m in (1, 2, 3)]
-    keep, two = call(plane_c_kernel, [floats(), coded(1)], "plane_c", total, *arrived)
-    from2 = send(two, 0, 2, (2, 3))
-    s1b, s3, keep = lax.optimization_barrier((s1b, s3, keep))
+        scratch=[pltpu.VMEM(own.shape, F32)],
+    )
+    arrived = [send(out[m - 1], m, 0, (0, 1, 2, 3)) for m in (1, 2, 3)]
+    sum_c, early = call(plane_c_kernel, [floats(1), coded(1)], "plane_c", total, *arrived)
+    from3 = reach(early, GO_EARLY)
+    s1b, s2, sum_c = lax.optimization_barrier((s1b, s2, sum_c))
 
     own, other = call(
         functools.partial(stage_d_kernel, scale),
-        [floats(len(STAGE_D)), coded(len(STAGE_D))],
+        [floats(6), coded(6)],
         "stage_d",
         snapshots,
         weighted,
         diagonal,
-        later,
         s1,
+        w1,
         s1b,
-        s3,
+        s2,
     )
     total, *out = call(
         combine_d_kernel,
@@ -348,15 +353,16 @@
         "combine_d",
         own,
         swap(other),
+        square,
+        square_arrived,
         scratch=[pltpu.VMEM(own.shape, F32)],
     )
     arrived = [send(out[m - 1], m, 0, (0, 1, 2, 3)) for m in (1, 2, 3)]
-    keep, one, three = call(
-        plane_d_kernel, [floats(), coded(1), coded(1)], "plane_d", total, *arrived, keep
-    )
-    from1 = send(one, 0, 1, (1, 2, 3))
-    from3 = send(three, 0, 3, (2, 3))
-    return call(last_kernel, [floats()], "last", keep, from1, from2, from3)[0]
+    keep, first, last = call(
+        plane_d_kernel, [floats(), coded(1), coded(1)], "plane_d", total, *arrived, sum_c
+    )
+    arrived = [reach(first, GO_FIRST), reach(last, GO_LAST), from3]
+    return call(last_kernel, [floats()], "last", keep, *arrived)[0]
 
 
 def solution(mesh):

time: 65.2 us -> 64.2 us (0.985)
  waiting for transfers between devices: 35 us -> 26.6 us
  starting transfers between devices: 21.9 us -> 29.2 us
    ppermute x0 -> x3, starting transfers between devices: none -> 15.3 us  [reach(): return lax.ppermute(array, ('cells', 'snap'), pairs)]
    ppermute x9 -> x6, waiting for transfers between devices: 17.4 us -> 3.81 us  [send(): return lax.ppermute(array, ('cells', 'snap'), pairs)]
    ppermute x9 -> x6, starting transfers between devices: 16.4 us -> 7.11 us  [send(): return lax.ppermute(array, ('cells', 'snap'), pairs)]
    ppermute x4, waiting for transfers between devices: 13.5 us -> 17.6 us  [to_plane(): return lax.ppermute(array, 'snap', [(i, i ^ m) for i in range(planes)])]
    ppermute x0 -> x3, waiting for transfers between devices: none -> 2.3 us  [reach(): return lax.ppermute(array, ('cells', 'snap'), pairs)]
    ppermute x3, waiting for transfers between devices: 4.07 us -> 2.94 us  [swap(): return lax.ppermute(array, 'cells', [(c, c ^ 1) for c in range(devices)])]
    ppermute x4, starting transfers between devices: 5.28 us -> 6.09 us  [to_plane(): return lax.ppermute(array, 'snap', [(i, i ^ m) for i in range(planes)])]
  transfers between devices with their start and end apart: 16 -> 16, of which waited for: 11 -> 9; matrix products, arithmetic and copies ran while one was open for 0% -> 0% of each run, Pallas kernels for 6% -> 6%
where the time goes in v7:
time: 64.2 us; the launch traced here: 63.6 us
  starting transfers between devices  29.2 us (45%)
  waiting for transfers between devices  26.6 us (41%)
  Pallas kernels  6.19 us (10%)
  local copies, waits for them, and re-layouts  1.46 us (2%)
    ppermute x4, waiting for transfers between devices, to_plane(): return lax.ppermute(array, 'snap', [(i, i ^ m) for i in range(planes)])  17.6 us
    ppermute x3, starting transfers between devices, reach(): return lax.ppermute(array, ('cells', 'snap'), pairs)  15.3 us
    ppermute x6, starting transfers between devices, send(): return lax.ppermute(array, ('cells', 'snap'), pairs)  7.11 us
    pallas_call x8, Pallas kernels, call(): pl.pallas_call(kernel, out_shape=[jax.ShapeDtypeStruct(s, t) for s, t in...  6.19 us
    ppermute x4, starting transfers between devices, to_plane(): return lax.ppermute(array, 'snap', [(i, i ^ m) for i in range(planes)])  6.09 us
    ppermute x6, waiting for transfers between devices, send(): return lax.ppermute(array, ('cells', 'snap'), pairs)  3.81 us
    ppermute x3, waiting for transfers between devices, swap(): return lax.ppermute(array, 'cells', [(c, c ^ 1) for c in range(devices)])  2.94 us
    ppermute x3, waiting for transfers between devices, reach(): return lax.ppermute(array, ('cells', 'snap'), pairs)  2.3 us
  transfers between devices with their start and end apart: 16, of which 9 were waited for; matrix products, arithmetic and copies ran while one was open for 0% of the time, Pallas kernels for 6%

profile of v7, /device:TPU:4, one launch (start us, length us, event | category | flops | bytes accessed | tf_op | source)
XLA Modules:
  0.0 63.6 jit_solution(10447510850240506317)
XLA Ops:
  0.0 0.0 copy-start
  0.0 0.0 copy-start.2
  0.0 0.0 copy-start.1
  0.0 1.4 %constant_dynamic-slice_fusion = (bf16[3,256,256]{2,1,0:T(8,128)(2,1)S(1)}, bf16[3,256,256]{2,1,0:T(8,128)(2,1)S(1)}, bf16[3,256,256]{2,1,0:T(8,128)(2,1)S(1)}) fusion(bf16[3,1024,256]{2,1,0:T(8,128)(2,1)} %s_ref.5, s32[]{:T(128)S(6)} %select_n.11, s32[]{:T(128)S(6)} %select_n.10, s32[]{:T(128)S(6)} %select_n.9), kind=kLoop, calls=%fused_computation | loop fusion | bytes 2359308 | tf_op jit(solution)/shard_map/dynamic_slice | solution.py:266
  1.5 1.6 %collective-permute-start = (bf16[3,256,256]{2,1,0:T(8,128)(2,1)S(1)}, bf16[3,256,256]{2,1,0:T(8,128)(2,1)S(1)}, u32[]{:S(2)}, u32[]{:S(2)}) collective-permute-start(bf16[3,256,256]{2,1,0:T(8,128)(2,1)S(1)} %get-tuple-element.60), channel_id=1, source_target_pairs={{0,1},{1,0},{2,3},{3,2},{4,5},{5,4},{6,7},{7,6},{8,9},{9,8},{10,11... | collective-permute-start | bytes 1179656 | tf_op jit(solution)/shard_map/ppermute | solution.py:263
  3.1 2.5 %collective-permute-start.1 = (bf16[3,256,256]{2,1,0:T(8,128)(2,1)S(1)}, bf16[3,256,256]{2,1,0:T(8,128)(2,1)S(1)}, u32[]{:S(2)}, u32[]{:S(2)}) collective-permute-start(bf16[3,256,256]{2,1,0:T(8,128)(2,1)S(1)} %get-tuple-element.59), channel_id=1, source_target_pairs={{0,3},{1,2},{2,1},{3,0},{4,7},{5,6},{6,5},{7,4},{8,11},{9,10},{10,... | collective-permute-start | bytes 1179656 | tf_op jit(solution)/shard_map/ppermute | solution.py:263
  5.6 0.7 %collective-permute-start.2 = (bf16[3,256,256]{2,1,0:T(8,128)(2,1)S(1)}, bf16[3,256,256]{2,1,0:T(8,128)(2,1)S(1)}, u32[]{:S(2)}, u32[]{:S(2)}) collective-permute-start(bf16[3,256,256]{2,1,0:T(8,128)(2,1)S(1)} %get-tuple-element.59), channel_id=1, source_target_pairs={{0,1},{1,0},{2,3},{3,2},{4,5},{5,4},{6,7},{7,6},{8,9},{9,8},{10,11... | collective-permute-start | bytes 1179656 | tf_op jit(solution)/shard_map/ppermute | solution.py:263
  6.3 0.0 copy-done
  6.3 0.0 copy-done.2
  6.3 0.0 copy-done.1
  6.3 2.3 %early.1 = (bf16[4,256,256]{2,1,0:T(8,128)(2,1)S(1)}, bf16[3,1024,256]{2,1,0:T(8,128)(2,1)S(1)}, f32[256,128]{1,0:T(8,128)S(1)}, f32[256,128]{1,0:T(8,128)S(1)}) custom-call(s32[16]{0:T(128)S(1)} %copy-done.2, bf16[16,64,64]{2,1,0:T(8,128)(2,1)S(1)} %copy-done.1, bf16[3,1024,256]{2,1,0:T(8,128)(2,1)S(1)} %copy-done), custom_call_target="tpu_custom_call" | custom-call | tf_op jit(solution)/shard_map/early/pallas_call | solution.py:240
  8.6 1.3 %collective-permute-start.3 = (bf16[3,256,256]{2,1,0:T(8,128)(2,1)S(1)}, bf16[3,256,256]{2,1,0:T(8,128)(2,1)S(1)}, u32[]{:S(2)}, u32[]{:S(2)}) collective-permute-start(bf16[3,256,256]{2,1,0:T(8,128)(2,1)S(1)} %get-tuple-element.36), channel_id=1, source_target_pairs={{0,2},{1,3},{2,0},{3,1},{4,6},{5,7},{6,4},{7,5},{8,10},{9,11},{10,... | collective-permute-start | bytes 1179656 | tf_op jit(solution)/shard_map/ppermute | solution.py:263
  9.9 4.2 %collective-permute-done.s1_ref = bf16[3,256,256]{2,1,0:T(8,128)(2,1)S(1)} collective-permute-done((bf16[3,256,256]{2,1,0:T(8,128)(2,1)S(1)}, bf16[3,256,256]{2,1,0:T(8,128)(2,1)S(1)}, u32[]{:S(2)}, u32[]{:S(2)}) %collective-permute-start) | collective-permute-done | bytes 393248 | tf_op jit(solution)/shard_map/ppermute | solution.py:263
  14.1 9.9 %collective-permute-done.1.s3_ref = bf16[3,256,256]{2,1,0:T(8,128)(2,1)S(1)} collective-permute-done((bf16[3,256,256]{2,1,0:T(8,128)(2,1)S(1)}, bf16[3,256,256]{2,1,0:T(8,128)(2,1)S(1)}, u32[]{:S(2)}, u32[]{:S(2)}) %collective-permute-start.1) | collective-permute-done | bytes 393248 | tf_op jit(solution)/shard_map/ppermute | solution.py:263
  24.0 0.9 %stage_c.1 = (f32[4,256,128]{2,1,0:T(8,128)S(1)}, s16[1040,128]{1,0:T(8,128)(2,1)S(1)}, bf16[768,256]{1,0:T(8,128)(2,1)S(1)}) custom-call(bf16[3,1024,256]{2,1,0:T(8,128)(2,1)S(1)} %copy-done, bf16[3,1024,256]{2,1,0:T(8,128)(2,1)S(1)} %get-tuple-element.33.weighted_ref, bf16[4,256,256]{2,1,0:T(8,128)(2,1)S(1)} %get-tuple-element.34.diagonal_ref, ...), custom_call_target="tpu_custom_call" | custom-call | tf_op jit(solution)/shard_map/stage_c/pallas_call | solution.py:240
  24.9 0.1 collective-permute-start.4
  25.0 1.5 %collective-permute-done.4.arrived_ref = s16[1040,128]{1,0:T(8,128)(2,1)S(1)} collective-permute-done((s16[1040,128]{1,0:T(8,128)(2,1)S(1)}, s16[1040,128]{1,0:T(8,128)(2,1)S(1)}, u32[]{:S(2)}, u32[]{:S(2)}) %collective-permute-start.4) | collective-permute-done | bytes 266272 | tf_op jit(solution)/shard_map/ppermute | solution.py:288
  26.5 0.2 combine_c.1
  26.8 1.6 %collective-permute-start.5 = (s16[272,128]{1,0:T(8,128)(2,1)S(1)}, s16[272,128]{1,0:T(8,128)(2,1)S(1)}, u32[]{:S(2)}, u32[]{:S(2)}) collective-permute-start(s16[272,128]{1,0:T(8,128)(2,1)S(1)} %get-tuple-element.40), channel_id=1, source_target_pairs={{0,8},{1,9},{2,10},{3,11},{4,12},{5,13},{6,14},{7,15},{8,0},{9,1},... | collective-permute-start | bytes 208904 | tf_op jit(solution)/shard_map/ppermute | solution.py:275
  28.3 0.5 collective-permute-start.6
  28.8 1.5 %collective-permute-start.7 = (s16[272,128]{1,0:T(8,128)(2,1)S(1)}, s16[272,128]{1,0:T(8,128)(2,1)S(1)}, u32[]{:S(2)}, u32[]{:S(2)}) collective-permute-start(s16[272,128]{1,0:T(8,128)(2,1)S(1)} %get-tuple-element.42), channel_id=1, source_target_pairs={{0,24},{1,25},{2,26},{3,27},{4,28},{5,29},{6,30},{7,31},{8,16},{9,... | collective-permute-start | bytes 208904 | tf_op jit(solution)/shard_map/ppermute | solution.py:275
  30.3 0.8 %collective-permute-done.5.m1_ref = s16[272,128]{1,0:T(8,128)(2,1)S(1)} collective-permute-done((s16[272,128]{1,0:T(8,128)(2,1)S(1)}, s16[272,128]{1,0:T(8,128)(2,1)S(1)}, u32[]{:S(2)}, u32[]{:S(2)}) %collective-permute-start.5) | collective-permute-done | bytes 69664 | tf_op jit(solution)/shard_map/ppermute | solution.py:275
  31.2 2.2 %collective-permute-done.6.m2_ref = s16[272,128]{1,0:T(8,128)(2,1)S(1)} collective-permute-done((s16[272,128]{1,0:T(8,128)(2,1)S(1)}, s16[272,128]{1,0:T(8,128)(2,1)S(1)}, u32[]{:S(2)}, u32[]{:S(2)}) %collective-permute-start.6) | collective-permute-done | bytes 69664 | tf_op jit(solution)/shard_map/ppermute | solution.py:275
  33.4 0.7 %collective-permute-done.7.m3_ref = s16[272,128]{1,0:T(8,128)(2,1)S(1)} collective-permute-done((s16[272,128]{1,0:T(8,128)(2,1)S(1)}, s16[272,128]{1,0:T(8,128)(2,1)S(1)}, u32[]{:S(2)}, u32[]{:S(2)}) %collective-permute-start.7) | collective-permute-done | bytes 69664 | tf_op jit(solution)/shard_map/ppermute | solution.py:275
  34.1 0.1 plane_c.1
  34.2 3.4 %collective-permute-done.2.s1b_ref = bf16[3,256,256]{2,1,0:T(8,128)(2,1)S(1)} collective-permute-done((bf16[3,256,256]{2,1,0:T(8,128)(2,1)S(1)}, bf16[3,256,256]{2,1,0:T(8,128)(2,1)S(1)}, u32[]{:S(2)}, u32[]{:S(2)}) %collective-permute-start.2) | collective-permute-done | bytes 393248 | tf_op jit(solution)/shard_map/ppermute | solution.py:263
  37.7 0.0 collective-permute-done.3.s2_ref
  37.7 1.3 %stage_d.1 = (f32[6,256,128]{2,1,0:T(8,128)S(1)}, s16[1568,128]{1,0:T(8,128)(2,1)S(1)}) custom-call(bf16[3,1024,256]{2,1,0:T(8,128)(2,1)S(1)} %copy-done, bf16[3,1024,256]{2,1,0:T(8,128)(2,1)S(1)} %get-tuple-element.33.weighted_ref, bf16[4,256,256]{2,1,0:T(8,128)(2,1)S(1)} %get-tuple-element.34.diagonal_ref, ...), custom_call_target="tpu_custom_call" | custom-call | tf_op jit(solution)/shard_map/stage_d/pallas_call | solution.py:240
  39.0 0.1 collective-permute-start.8
  39.1 0.5 collective-permute-start.9
  39.6 1.4 %collective-permute-done.9.other_ref = f32[256,128]{1,0:T(8,128)S(1)} collective-permute-done((f32[256,128]{1,0:T(8,128)S(1)}, f32[256,128]{1,0:T(8,128)S(1)}, u32[]{:S(2)}, u32[]{:S(2)}) %collective-permute-start.9) | collective-permute-done | bytes 131104 | tf_op jit(solution)/shard_map/ppermute | solution.py:288
  41.0 0.0 collective-permute-done.8.arrived_ref
  41.0 0.4 combine_d.1
  41.4 1.6 %collective-permute-start.10 = (s16[528,128]{1,0:T(8,128)(2,1)S(1)}, s16[528,128]{1,0:T(8,128)(2,1)S(1)}, u32[]{:S(2)}, u32[]{:S(2)}) collective-permute-start(s16[528,128]{1,0:T(8,128)(2,1)S(1)} %get-tuple-element.51), channel_id=1, source_target_pairs={{0,8},{1,9},{2,10},{3,11},{4,12},{5,13},{6,14},{7,15},{8,0},{9,1},... | collective-permute-start | bytes 405512 | tf_op jit(solution)/shard_map/ppermute | solution.py:275
  43.0 0.5 collective-permute-start.11
  43.5 1.5 %collective-permute-start.12 = (s16[528,128]{1,0:T(8,128)(2,1)S(1)}, s16[528,128]{1,0:T(8,128)(2,1)S(1)}, u32[]{:S(2)}, u32[]{:S(2)}) collective-permute-start(s16[528,128]{1,0:T(8,128)(2,1)S(1)} %get-tuple-element.53), channel_id=1, source_target_pairs={{0,24},{1,25},{2,26},{3,27},{4,28},{5,29},{6,30},{7,31},{8,16},{9,... | collective-permute-start | bytes 405512 | tf_op jit(solution)/shard_map/ppermute | solution.py:275
  45.0 7.5 %collective-permute-start.15 = (s16[272,128]{1,0:T(8,128)(2,1)S(1)}, s16[272,128]{1,0:T(8,128)(2,1)S(1)}, u32[]{:S(2)}, u32[]{:S(2)}) collective-permute-start(s16[272,128]{1,0:T(8,128)(2,1)S(1)} %get-tuple-element.58), channel_id=1, source_target_pairs={{1,10},{2,25},{5,14},{6,29},{8,3},{11,16},{12,7},{15,20},{16,11},{... | collective-permute-start | bytes 208904 | tf_op jit(solution)/shard_map/ppermute | solution.py:285
  52.6 0.0 collective-permute-done.10.m1_ref
  52.6 0.0 collective-permute-done.11.m2_ref
  52.6 0.0 collective-permute-done.12.m3_ref
  52.6 0.2 plane_d.1
  52.8 1.3 %collective-permute-start.13 = (s16[272,128]{1,0:T(8,128)(2,1)S(1)}, s16[272,128]{1,0:T(8,128)(2,1)S(1)}, u32[]{:S(2)}, u32[]{:S(2)}) collective-permute-start(s16[272,128]{1,0:T(8,128)(2,1)S(1)} %get-tuple-element.56), channel_id=1, source_target_pairs={{0,2},{1,8},{3,17},{4,6},{5,12},{7,21},{8,1},{9,11},{10,24},{12,5}... | collective-permute-start | bytes 208904 | tf_op jit(solution)/shard_map/ppermute | solution.py:285
  54.1 6.5 %collective-permute-start.14 = (s16[272,128]{1,0:T(8,128)(2,1)S(1)}, s16[272,128]{1,0:T(8,128)(2,1)S(1)}, u32[]{:S(2)}, u32[]{:S(2)}) collective-permute-start(s16[272,128]{1,0:T(8,128)(2,1)S(1)} %get-tuple-element.57), channel_id=1, source_target_pairs={{0,25},{2,3},{4,29},{6,7},{9,16},{11,10},{13,20},{15,14},{16,17},{... | collective-permute-start | bytes 208904 | tf_op jit(solution)/shard_map/ppermute | solution.py:285
  60.6 0.0 collective-permute-done.15.m3_ref
  60.6 0.0 collective-permute-done.13.m1_ref
  60.6 2.3 %collective-permute-done.14.m2_ref = s16[272,128]{1,0:T(8,128)(2,1)S(1)} collective-permute-done((s16[272,128]{1,0:T(8,128)(2,1)S(1)}, s16[272,128]{1,0:T(8,128)(2,1)S(1)}, u32[]{:S(2)}, u32[]{:S(2)}) %collective-permute-start.14) | collective-permute-done | bytes 69664 | tf_op jit(solution)/shard_map/ppermute | solution.py:285
  62.9 0.7 %last.1 = f32[256,128]{1,0:T(8,128)} custom-call(f32[256,128]{1,0:T(8,128)S(1)} %get-tuple-element.55.keep_ref, s16[272,128]{1,0:T(8,128)(2,1)S(1)} %collective-permute-done.13.m1_ref, s16[272,128]{1,0:T(8,128)(2,1)S(1)} %collective-permute-done.14.m2_ref, s16[272,128]{1,0:T(8,128)(2,1)S(1)} %collective-permute-done.15.m3_ref), custom_call_target="tpu_custom_call" | custom-call | tf_op jit(solution)/shard_map/last/pallas_call | solution.py:240
Async XLA Ops:
  0.0 6.3 %copy-start = (bf16[3,1024,256]{2,1,0:T(8,128)(2,1)S(1)}, bf16[3,1024,256]{2,1,0:T(8,128)(2,1)}, u32[]{:S(2)}) copy-start(bf16[3,1024,256]{2,1,0:T(8,128)(2,1)} %s_ref.5) | copy-start | bytes 4718596
  0.0 6.3 %copy-start.2 = (s32[16]{0:T(128)S(1)}, s32[16]{0:T(128)}, u32[]{:S(2)}) copy-start(s32[16]{0:T(128)} %offsets_ref.1) | copy-start | bytes 196
  0.0 6.3 %copy-start.1 = (bf16[16,64,64]{2,1,0:T(8,128)(2,1)S(1)}, bf16[16,64,64]{2,1,0:T(8,128)(2,1)}, u32[]{:S(2)}) copy-start(bf16[16,64,64]{2,1,0:T(8,128)(2,1)} %mass_ref.1) | copy-start | bytes 393220
  1.5 12.6 %collective-permute-start = (bf16[3,256,256]{2,1,0:T(8,128)(2,1)S(1)}, bf16[3,256,256]{2,1,0:T(8,128)(2,1)S(1)}, u32[]{:S(2)}, u32[]{:S(2)}) collective-permute-start(bf16[3,256,256]{2,1,0:T(8,128)(2,1)S(1)} %get-tuple-element.60), channel_id=1, source_target_pairs={{0,1},{1,0},{2,3},{3,2},{4,5},{5,4},{6,7},{7,6},{8,9},{9,8},{10,11... | collective-permute-start | bytes 1179656 | tf_op jit(solution)/shard_map/ppermute | solution.py:263
  3.1 20.9 %collective-permute-start.1 = (bf16[3,256,256]{2,1,0:T(8,128)(2,1)S(1)}, bf16[3,256,256]{2,1,0:T(8,128)(2,1)S(1)}, u32[]{:S(2)}, u32[]{:S(2)}) collective-permute-start(bf16[3,256,256]{2,1,0:T(8,128)(2,1)S(1)} %get-tuple-element.59), channel_id=1, source_target_pairs={{0,3},{1,2},{2,1},{3,0},{4,7},{5,6},{6,5},{7,4},{8,11},{9,10},{10,... | collective-permute-start | bytes 1179656 | tf_op jit(solution)/shard_map/ppermute | solution.py:263
  5.6 32.1 %collective-permute-start.2 = (bf16[3,256,256]{2,1,0:T(8,128)(2,1)S(1)}, bf16[3,256,256]{2,1,0:T(8,128)(2,1)S(1)}, u32[]{:S(2)}, u32[]{:S(2)}) collective-permute-start(bf16[3,256,256]{2,1,0:T(8,128)(2,1)S(1)} %get-tuple-element.59), channel_id=1, source_target_pairs={{0,1},{1,0},{2,3},{3,2},{4,5},{5,4},{6,7},{7,6},{8,9},{9,8},{10,11... | collective-permute-start | bytes 1179656 | tf_op jit(solution)/shard_map/ppermute | solution.py:263
  8.6 29.1 %collective-permute-start.3 = (bf16[3,256,256]{2,1,0:T(8,128)(2,1)S(1)}, bf16[3,256,256]{2,1,0:T(8,128)(2,1)S(1)}, u32[]{:S(2)}, u32[]{:S(2)}) collective-permute-start(bf16[3,256,256]{2,1,0:T(8,128)(2,1)S(1)} %get-tuple-element.36), channel_id=1, source_target_pairs={{0,2},{1,3},{2,0},{3,1},{4,6},{5,7},{6,4},{7,5},{8,10},{9,11},{10,... | collective-permute-start | bytes 1179656 | tf_op jit(solution)/shard_map/ppermute | solution.py:263
  24.9 1.6 %collective-permute-start.4 = (s16[1040,128]{1,0:T(8,128)(2,1)S(1)}, s16[1040,128]{1,0:T(8,128)(2,1)S(1)}, u32[]{:S(2)}, u32[]{:S(2)}) collective-permute-start(s16[1040,128]{1,0:T(8,128)(2,1)S(1)} %get-tuple-element.38), channel_id=1, source_target_pairs={{0,4},{4,0},{8,12},{12,8},{16,20},{20,16},{24,28},{28,24},{1,5},{5... | collective-permute-start | bytes 798728 | tf_op jit(solution)/shard_map/ppermute | solution.py:288
  26.8 4.4 %collective-permute-start.5 = (s16[272,128]{1,0:T(8,128)(2,1)S(1)}, s16[272,128]{1,0:T(8,128)(2,1)S(1)}, u32[]{:S(2)}, u32[]{:S(2)}) collective-permute-start(s16[272,128]{1,0:T(8,128)(2,1)S(1)} %get-tuple-element.40), channel_id=1, source_target_pairs={{0,8},{1,9},{2,10},{3,11},{4,12},{5,13},{6,14},{7,15},{8,0},{9,1},... | collective-permute-start | bytes 208904 | tf_op jit(solution)/shard_map/ppermute | solution.py:275
  28.3 5.1 %collective-permute-start.6 = (s16[272,128]{1,0:T(8,128)(2,1)S(1)}, s16[272,128]{1,0:T(8,128)(2,1)S(1)}, u32[]{:S(2)}, u32[]{:S(2)}) collective-permute-start(s16[272,128]{1,0:T(8,128)(2,1)S(1)} %get-tuple-element.41), channel_id=1, source_target_pairs={{0,16},{1,17},{2,18},{3,19},{4,20},{5,21},{6,22},{7,23},{8,24},{9,... | collective-permute-start | bytes 208904 | tf_op jit(solution)/shard_map/ppermute | solution.py:275
  28.8 5.3 %collective-permute-start.7 = (s16[272,128]{1,0:T(8,128)(2,1)S(1)}, s16[272,128]{1,0:T(8,128)(2,1)S(1)}, u32[]{:S(2)}, u32[]{:S(2)}) collective-permute-start(s16[272,128]{1,0:T(8,128)(2,1)S(1)} %get-tuple-element.42), channel_id=1, source_target_pairs={{0,24},{1,25},{2,26},{3,27},{4,28},{5,29},{6,30},{7,31},{8,16},{9,... | collective-permute-start | bytes 208904 | tf_op jit(solution)/shard_map/ppermute | solution.py:275
  39.0 2.0 %collective-permute-start.8 = (s16[1568,128]{1,0:T(8,128)(2,1)S(1)}, s16[1568,128]{1,0:T(8,128)(2,1)S(1)}, u32[]{:S(2)}, u32[]{:S(2)}) collective-permute-start(s16[1568,128]{1,0:T(8,128)(2,1)S(1)} %get-tuple-element.47), channel_id=1, source_target_pairs={{0,4},{4,0},{8,12},{12,8},{16,20},{20,16},{24,28},{28,24},{1,5},{5... | collective-permute-start | bytes 1204232 | tf_op jit(solution)/shard_map/ppermute | solution.py:288
  39.1 1.9 %collective-permute-start.9 = (f32[256,128]{1,0:T(8,128)S(1)}, f32[256,128]{1,0:T(8,128)S(1)}, u32[]{:S(2)}, u32[]{:S(2)}) collective-permute-start(f32[256,128]{1,0:T(8,128)S(1)} %get-tuple-element.49), channel_id=1, source_target_pairs={{0,4},{4,0},{8,12},{12,8},{16,20},{20,16},{24,28},{28,24},{1,5},{5... | collective-permute-start | bytes 393224 | tf_op jit(solution)/shard_map/ppermute | solution.py:288
  41.4 11.1 %collective-permute-start.10 = (s16[528,128]{1,0:T(8,128)(2,1)S(1)}, s16[528,128]{1,0:T(8,128)(2,1)S(1)}, u32[]{:S(2)}, u32[]{:S(2)}) collective-permute-start(s16[528,128]{1,0:T(8,128)(2,1)S(1)} %get-tuple-element.51), channel_id=1, source_target_pairs={{0,8},{1,9},{2,10},{3,11},{4,12},{5,13},{6,14},{7,15},{8,0},{9,1},... | collective-permute-start | bytes 405512 | tf_op jit(solution)/shard_map/ppermute | solution.py:275
  43.0 9.6 %collective-permute-start.11 = (s16[528,128]{1,0:T(8,128)(2,1)S(1)}, s16[528,128]{1,0:T(8,128)(2,1)S(1)}, u32[]{:S(2)}, u32[]{:S(2)}) collective-permute-start(s16[528,128]{1,0:T(8,128)(2,1)S(1)} %get-tuple-element.52), channel_id=1, source_target_pairs={{0,16},{1,17},{2,18},{3,19},{4,20},{5,21},{6,22},{7,23},{8,24},{9,... | collective-permute-start | bytes 405512 | tf_op jit(solution)/shard_map/ppermute | solution.py:275
  43.5 9.1 %collective-permute-start.12 = (s16[528,128]{1,0:T(8,128)(2,1)S(1)}, s16[528,128]{1,0:T(8,128)(2,1)S(1)}, u32[]{:S(2)}, u32[]{:S(2)}) collective-permute-start(s16[528,128]{1,0:T(8,128)(2,1)S(1)} %get-tuple-element.53), channel_id=1, source_target_pairs={{0,24},{1,25},{2,26},{3,27},{4,28},{5,29},{6,30},{7,31},{8,16},{9,... | collective-permute-start | bytes 405512 | tf_op jit(solution)/shard_map/ppermute | solution.py:275
  45.0 15.6 %collective-permute-start.15 = (s16[272,128]{1,0:T(8,128)(2,1)S(1)}, s16[272,128]{1,0:T(8,128)(2,1)S(1)}, u32[]{:S(2)}, u32[]{:S(2)}) collective-permute-start(s16[272,128]{1,0:T(8,128)(2,1)S(1)} %get-tuple-element.58), channel_id=1, source_target_pairs={{1,10},{2,25},{5,14},{6,29},{8,3},{11,16},{12,7},{15,20},{16,11},{... | collective-permute-start | bytes 208904 | tf_op jit(solution)/shard_map/ppermute | solution.py:285
  52.8 7.8 %collective-permute-start.13 = (s16[272,128]{1,0:T(8,128)(2,1)S(1)}, s16[272,128]{1,0:T(8,128)(2,1)S(1)}, u32[]{:S(2)}, u32[]{:S(2)}) collective-permute-start(s16[272,128]{1,0:T(8,128)(2,1)S(1)} %get-tuple-element.56), channel_id=1, source_target_pairs={{0,2},{1,8},{3,17},{4,6},{5,12},{7,21},{8,1},{9,11},{10,24},{12,5}... | collective-permute-start | bytes 208904 | tf_op jit(solution)/shard_map/ppermute | solution.py:285
  54.1 8.8 %collective-permute-start.14 = (s16[272,128]{1,0:T(8,128)(2,1)S(1)}, s16[272,128]{1,0:T(8,128)(2,1)S(1)}, u32[]{:S(2)}, u32[]{:S(2)}) collective-permute-start(s16[272,128]{1,0:T(8,128)(2,1)S(1)} %get-tuple-element.57), channel_id=1, source_target_pairs={{0,25},{2,3},{4,29},{6,7},{9,16},{11,10},{13,20},{15,14},{16,17},{... | collective-permute-start | bytes 208904 | tf_op jit(solution)/shard_map/ppermute | solution.py:285

commit v8 on v7

--- a/solution.py
+++ b/solution.py
@@ -112,35 +112,64 @@
 
 
 def stage_c_kernel(
-    scale, s_ref, weighted_ref, diagonal_ref, s1_ref, s3_ref, own_ref, other_ref, w1_ref
+    scale,
+    s_ref,
+    weighted_ref,
+    diagonal_ref,
+    s1_ref,
+    s3_ref,
+    own_ref,
+    other_ref,
+    w1_ref,
+    left_ref,
+    pair_ref,
 ):
     z = lax.axis_index("snap")
     diagonal = diagonal_ref[z]
     s0, w0 = quarter(z, s_ref), quarter(z, weighted_ref)
     s1, s3 = flat(s1_ref[...]), flat(s3_ref[...])
     w1, w3 = weigh(diagonal, s1_ref[...]), weigh(diagonal, s3_ref[...])
+    s0t, s1t = s0.T, s1.T
+    blocks = {
+        (3, 0): tdot(s3, w0),
+        (3, 1): tdot(s3, w1),
+        (0, 3): jnp.dot(s0t, w3, preferred_element_type=F32),
+        (1, 3): jnp.dot(s1t, w3, preferred_element_type=F32),
+    }
+    emit(scale, [blocks[name] for name in STAGE_C], own_ref, other_ref)
     w1_ref[...] = w1
-    blocks = {(3, 0): (s3, w0), (3, 1): (s3, w1), (0, 3): (s0, w3), (1, 3): (s1, w3)}
-    emit(scale, [tdot(*blocks[name]) for name in STAGE_C], own_ref, other_ref)
+    left_ref[0], left_ref[1] = s0t, s1t
+    pair_ref[0] = jnp.dot(s0t, w1, preferred_element_type=F32)
+    pair_ref[1] = jnp.dot(s1t, w0, preferred_element_type=F32)
 
 
 def stage_d_kernel(
-    scale, s_ref, weighted_ref, diagonal_ref, s1_ref, w1_ref, s1b_ref, s2_ref, own_ref, other_ref
+    scale,
+    s_ref,
+    weighted_ref,
+    diagonal_ref,
+    left_ref,
+    pair_ref,
+    w1_ref,
+    s1b_ref,
+    s2_ref,
+    own_ref,
+    other_ref,
 ):
     z = lax.axis_index("snap")
     across = z ^ 2
-    s0, w0 = quarter(z, s_ref), quarter(z, weighted_ref)
+    w0, w1 = quarter(z, weighted_ref), w1_ref[...]
     s0b, w0b = quarter(across, s_ref), quarter(across, weighted_ref)
-    s1, s1b, s2, w1 = flat(s1_ref[...]), flat(s1b_ref[...]), flat(s2_ref[...]), w1_ref[...]
+    s1b, s2 = flat(s1b_ref[...]), flat(s2_ref[...])
     w1b = weigh(diagonal_ref[across], s1b_ref[...])
     w2 = weigh(diagonal_ref[z], s2_ref[...])
     blocks = {
-        (0, 1): tdot(s0, w1) + tdot(s0b, w1b),
-        (1, 0): tdot(s1, w0) + tdot(s1b, w0b),
+        (0, 1): pair_ref[0] + tdot(s0b, w1b),
+        (1, 0): pair_ref[1] + tdot(s1b, w0b),
         (2, 0): tdot(s2, w0),
         (2, 1): tdot(s2, w1),
-        (1, 2): tdot(s1, w2),
-        (0, 2): tdot(s0, w2),
+        (0, 2): jnp.dot(left_ref[0], w2, preferred_element_type=F32),
+        (1, 2): jnp.dot(left_ref[1], w2, preferred_element_type=F32),
     }
     emit(scale, [blocks[name] for name in STAGE_D + STAGE_B], own_ref, other_ref)
 
@@ -148,6 +177,7 @@
 GROUP = 64
 STEPS = 256.0
 TOP = 32700.0
+LEAST = 1e-33
 
 
 def tail(slots, rows):
@@ -158,7 +188,7 @@
     slots, rows, columns = value.shape
     groups = slots * rows // GROUP
     value = value.reshape(groups, GROUP, columns)
-    most = jnp.maximum(jnp.max(jnp.abs(value), axis=1), 1e-36)
+    most = jnp.maximum(jnp.max(jnp.abs(value), axis=1), LEAST)
     step = jnp.ceil(jnp.log2(most) * STEPS)
     code = jnp.round(value * (TOP * jnp.exp2(step * (-1.0 / STEPS)))[:, None, :])
     codes = code.reshape(slots * rows, columns).astype(jnp.int32).astype(jnp.int16)
@@ -308,13 +338,19 @@
     s1 = to_plane(out1, 1)
     s1b = to_plane(out3, 1)
     square_arrived = swap(square_other)
-    out2, weighted = lax.optimization_barrier((out2, weighted))
+    out2, square_arrived = lax.optimization_barrier((out2, square_arrived))
     s2 = to_plane(out2, 2)
 
-    stage_c, w1 = [floats(4), coded(4)], ((components * rows, columns), BF16)
-    own, other, w1 = call(
+    held = components * rows
+    own, other, w1, left, pair = call(
         functools.partial(stage_c_kernel, scale),
-        [*stage_c, w1],
+        [
+            floats(4),
+            coded(4),
+            ((held, columns), BF16),
+            ((2, columns, held), BF16),
+            ((2, columns, columns), F32),
+        ],
         "stage_c",
         snapshots,
         weighted,
@@ -342,7 +378,8 @@
         snapshots,
         weighted,
         diagonal,
-        s1,
+        left,
+        pair,
         w1,
         s1b,
         s2,

time: 64.2 us -> 63.8 us (level)
  starting transfers between devices: 29.2 us -> 28.1 us
  waiting for transfers between devices: 26.6 us -> 27.3 us
    ppermute x3, waiting for transfers between devices: 2.94 us -> 3.84 us  [swap(): return lax.ppermute(array, 'cells', [(c, c ^ 1) for c in range(devices)])]
  transfers between devices with their start and end apart: 16 -> 16, of which waited for: 9 -> 10; matrix products, arithmetic and copies ran while one was open for 0% -> 0% of each run, Pallas kernels for 6% -> 6%
where the time goes in v8:
time: 63.8 us; the launch traced here: 63.2 us
  starting transfers between devices  28.1 us (44%)
  waiting for transfers between devices  27.3 us (43%)
  Pallas kernels  6.12 us (10%)
  local copies, waits for them, and re-layouts  1.46 us (2%)
    ppermute x4, waiting for transfers between devices, to_plane(): return lax.ppermute(array, 'snap', [(i, i ^ m) for i in range(planes)])  17.4 us
    ppermute x3, starting transfers between devices, reach(): return lax.ppermute(array, ('cells', 'snap'), pairs)  15.3 us
    ppermute x6, starting transfers between devices, send(): return lax.ppermute(array, ('cells', 'snap'), pairs)  7.11 us
    pallas_call x8, Pallas kernels, call(): pl.pallas_call(kernel, out_shape=[jax.ShapeDtypeStruct(s, t) for s, t in...  6.12 us
    ppermute x4, starting transfers between devices, to_plane(): return lax.ppermute(array, 'snap', [(i, i ^ m) for i in range(planes)])  5.51 us
    ppermute x3, waiting for transfers between devices, swap(): return lax.ppermute(array, 'cells', [(c, c ^ 1) for c in range(devices)])  3.84 us
    ppermute x6, waiting for transfers between devices, send(): return lax.ppermute(array, ('cells', 'snap'), pairs)  3.81 us
    ppermute x3, waiting for transfers between devices, reach(): return lax.ppermute(array, ('cells', 'snap'), pairs)  2.3 us
  transfers between devices with their start and end apart: 16, of which 10 were waited for; matrix products, arithmetic and copies ran while one was open for 0% of the time, Pallas kernels for 6%

profile of v8, /device:TPU:4, one launch (start us, length us, event | category | flops | bytes accessed | tf_op | source)
XLA Modules:
  0.0 63.2 jit_solution(1387390692873289465)
XLA Ops:
  0.0 0.0 copy-start
  0.0 0.0 copy-start.2
  0.0 0.0 copy-start.1
  0.0 1.4 %constant_dynamic-slice_fusion = (bf16[3,256,256]{2,1,0:T(8,128)(2,1)S(1)}, bf16[3,256,256]{2,1,0:T(8,128)(2,1)S(1)}, bf16[3,256,256]{2,1,0:T(8,128)(2,1)S(1)}) fusion(bf16[3,1024,256]{2,1,0:T(8,128)(2,1)} %s_ref.5, s32[]{:T(128)S(6)} %select_n.11, s32[]{:T(128)S(6)} %select_n.10, s32[]{:T(128)S(6)} %select_n.9), kind=kLoop, calls=%fused_computation | loop fusion | bytes 2359308 | tf_op jit(solution)/shard_map/dynamic_slice | solution.py:296
  1.5 1.6 %collective-permute-start = (bf16[3,256,256]{2,1,0:T(8,128)(2,1)S(1)}, bf16[3,256,256]{2,1,0:T(8,128)(2,1)S(1)}, u32[]{:S(2)}, u32[]{:S(2)}) collective-permute-start(bf16[3,256,256]{2,1,0:T(8,128)(2,1)S(1)} %get-tuple-element.65), channel_id=1, source_target_pairs={{0,1},{1,0},{2,3},{3,2},{4,5},{5,4},{6,7},{7,6},{8,9},{9,8},{10,11... | collective-permute-start | bytes 1179656 | tf_op jit(solution)/shard_map/ppermute | solution.py:293
  3.1 2.5 %collective-permute-start.1 = (bf16[3,256,256]{2,1,0:T(8,128)(2,1)S(1)}, bf16[3,256,256]{2,1,0:T(8,128)(2,1)S(1)}, u32[]{:S(2)}, u32[]{:S(2)}) collective-permute-start(bf16[3,256,256]{2,1,0:T(8,128)(2,1)S(1)} %get-tuple-element.64), channel_id=1, source_target_pairs={{0,3},{1,2},{2,1},{3,0},{4,7},{5,6},{6,5},{7,4},{8,11},{9,10},{10,... | collective-permute-start | bytes 1179656 | tf_op jit(solution)/shard_map/ppermute | solution.py:293
  5.6 0.0 copy-done
  5.6 0.0 copy-done.2
  5.6 0.0 copy-done.1
  5.6 2.3 %early.1 = (bf16[4,256,256]{2,1,0:T(8,128)(2,1)S(1)}, bf16[3,1024,256]{2,1,0:T(8,128)(2,1)S(1)}, f32[256,128]{1,0:T(8,128)S(1)}, f32[256,128]{1,0:T(8,128)S(1)}) custom-call(s32[16]{0:T(128)S(1)} %copy-done.2, bf16[16,64,64]{2,1,0:T(8,128)(2,1)S(1)} %copy-done.1, bf16[3,1024,256]{2,1,0:T(8,128)(2,1)S(1)} %copy-done), custom_call_target="tpu_custom_call" | custom-call | tf_op jit(solution)/shard_map/early/pallas_call | solution.py:270
  7.9 0.1 collective-permute-start.3
  8.0 0.7 %collective-permute-start.2 = (bf16[3,256,256]{2,1,0:T(8,128)(2,1)S(1)}, bf16[3,256,256]{2,1,0:T(8,128)(2,1)S(1)}, u32[]{:S(2)}, u32[]{:S(2)}) collective-permute-start(bf16[3,256,256]{2,1,0:T(8,128)(2,1)S(1)} %get-tuple-element.64), channel_id=1, source_target_pairs={{0,1},{1,0},{2,3},{3,2},{4,5},{5,4},{6,7},{7,6},{8,9},{9,8},{10,11... | collective-permute-start | bytes 1179656 | tf_op jit(solution)/shard_map/ppermute | solution.py:293
  8.7 0.6 collective-permute-done.3.other_ref
  9.3 0.6 %collective-permute-start.4 = (bf16[3,256,256]{2,1,0:T(8,128)(2,1)S(1)}, bf16[3,256,256]{2,1,0:T(8,128)(2,1)S(1)}, u32[]{:S(2)}, u32[]{:S(2)}) collective-permute-start(bf16[3,256,256]{2,1,0:T(8,128)(2,1)S(1)} %get-tuple-element.40), channel_id=1, source_target_pairs={{0,2},{1,3},{2,0},{3,1},{4,6},{5,7},{6,4},{7,5},{8,10},{9,11},{10,... | collective-permute-start | bytes 1179656 | tf_op jit(solution)/shard_map/ppermute | solution.py:293
  10.0 4.1 %collective-permute-done.s1_ref = bf16[3,256,256]{2,1,0:T(8,128)(2,1)S(1)} collective-permute-done((bf16[3,256,256]{2,1,0:T(8,128)(2,1)S(1)}, bf16[3,256,256]{2,1,0:T(8,128)(2,1)S(1)}, u32[]{:S(2)}, u32[]{:S(2)}) %collective-permute-start) | collective-permute-done | bytes 393248 | tf_op jit(solution)/shard_map/ppermute | solution.py:293
  14.1 9.9 %collective-permute-done.1.s3_ref = bf16[3,256,256]{2,1,0:T(8,128)(2,1)S(1)} collective-permute-done((bf16[3,256,256]{2,1,0:T(8,128)(2,1)S(1)}, bf16[3,256,256]{2,1,0:T(8,128)(2,1)S(1)}, u32[]{:S(2)}, u32[]{:S(2)}) %collective-permute-start.1) | collective-permute-done | bytes 393248 | tf_op jit(solution)/shard_map/ppermute | solution.py:293
  24.0 1.0 %stage_c.1 = (f32[4,256,128]{2,1,0:T(8,128)S(1)}, s16[1040,128]{1,0:T(8,128)(2,1)S(1)}, bf16[768,256]{1,0:T(8,128)(2,1)S(1)}, bf16[2,256,768]{2,1,0:T(8,128)(2,1)S(1)}, f32[2,256,256]{2,1,0:T(8,128)S(1)}) custom-call(bf16[3,1024,256]{2,1,0:T(8,128)(2,1)S(1)} %copy-done, bf16[3,1024,256]{2,1,0:T(8,128)(2,1)S(1)} %get-tuple-element.34.weighted_ref, ...), custom_call_target="tpu_custom_call" | custom-call | tf_op jit(solution)/shard_map/stage_c/pallas_call | solution.py:270
  25.1 0.1 collective-permute-start.5
  25.2 1.5 %collective-permute-done.5.arrived_ref = s16[1040,128]{1,0:T(8,128)(2,1)S(1)} collective-permute-done((s16[1040,128]{1,0:T(8,128)(2,1)S(1)}, s16[1040,128]{1,0:T(8,128)(2,1)S(1)}, u32[]{:S(2)}, u32[]{:S(2)}) %collective-permute-start.5) | collective-permute-done | bytes 266272 | tf_op jit(solution)/shard_map/ppermute | solution.py:318
  26.7 0.2 combine_c.1
  26.9 1.6 %collective-permute-start.6 = (s16[272,128]{1,0:T(8,128)(2,1)S(1)}, s16[272,128]{1,0:T(8,128)(2,1)S(1)}, u32[]{:S(2)}, u32[]{:S(2)}) collective-permute-start(s16[272,128]{1,0:T(8,128)(2,1)S(1)} %get-tuple-element.44), channel_id=1, source_target_pairs={{0,8},{1,9},{2,10},{3,11},{4,12},{5,13},{6,14},{7,15},{8,0},{9,1},... | collective-permute-start | bytes 208904 | tf_op jit(solution)/shard_map/ppermute | solution.py:305
  28.5 0.5 collective-permute-start.7
  29.0 1.5 %collective-permute-start.8 = (s16[272,128]{1,0:T(8,128)(2,1)S(1)}, s16[272,128]{1,0:T(8,128)(2,1)S(1)}, u32[]{:S(2)}, u32[]{:S(2)}) collective-permute-start(s16[272,128]{1,0:T(8,128)(2,1)S(1)} %get-tuple-element.46), channel_id=1, source_target_pairs={{0,24},{1,25},{2,26},{3,27},{4,28},{5,29},{6,30},{7,31},{8,16},{9,... | collective-permute-start | bytes 208904 | tf_op jit(solution)/shard_map/ppermute | solution.py:305
  30.5 0.8 %collective-permute-done.6.m1_ref = s16[272,128]{1,0:T(8,128)(2,1)S(1)} collective-permute-done((s16[272,128]{1,0:T(8,128)(2,1)S(1)}, s16[272,128]{1,0:T(8,128)(2,1)S(1)}, u32[]{:S(2)}, u32[]{:S(2)}) %collective-permute-start.6) | collective-permute-done | bytes 69664 | tf_op jit(solution)/shard_map/ppermute | solution.py:305
  31.3 2.3 %collective-permute-done.7.m2_ref = s16[272,128]{1,0:T(8,128)(2,1)S(1)} collective-permute-done((s16[272,128]{1,0:T(8,128)(2,1)S(1)}, s16[272,128]{1,0:T(8,128)(2,1)S(1)}, u32[]{:S(2)}, u32[]{:S(2)}) %collective-permute-start.7) | collective-permute-done | bytes 69664 | tf_op jit(solution)/shard_map/ppermute | solution.py:305
  33.6 0.7 %collective-permute-done.8.m3_ref = s16[272,128]{1,0:T(8,128)(2,1)S(1)} collective-permute-done((s16[272,128]{1,0:T(8,128)(2,1)S(1)}, s16[272,128]{1,0:T(8,128)(2,1)S(1)}, u32[]{:S(2)}, u32[]{:S(2)}) %collective-permute-start.8) | collective-permute-done | bytes 69664 | tf_op jit(solution)/shard_map/ppermute | solution.py:305
  34.3 0.1 plane_c.1
  34.4 3.3 %collective-permute-done.2.s1b_ref = bf16[3,256,256]{2,1,0:T(8,128)(2,1)S(1)} collective-permute-done((bf16[3,256,256]{2,1,0:T(8,128)(2,1)S(1)}, bf16[3,256,256]{2,1,0:T(8,128)(2,1)S(1)}, u32[]{:S(2)}, u32[]{:S(2)}) %collective-permute-start.2) | collective-permute-done | bytes 393248 | tf_op jit(solution)/shard_map/ppermute | solution.py:293
  37.7 0.0 collective-permute-done.4.s2_ref
  37.7 1.1 %stage_d.1 = (f32[6,256,128]{2,1,0:T(8,128)S(1)}, s16[1568,128]{1,0:T(8,128)(2,1)S(1)}) custom-call(bf16[3,1024,256]{2,1,0:T(8,128)(2,1)S(1)} %copy-done, bf16[3,1024,256]{2,1,0:T(8,128)(2,1)S(1)} %get-tuple-element.34.weighted_ref, bf16[4,256,256]{2,1,0:T(8,128)(2,1)S(1)} %get-tuple-element.35.diagonal_ref, ...), custom_call_target="tpu_custom_call" | custom-call | tf_op jit(solution)/shard_map/stage_d/pallas_call | solution.py:270
  38.8 0.1 collective-permute-start.9
  38.9 1.7 %collective-permute-done.9.arrived_ref = s16[1568,128]{1,0:T(8,128)(2,1)S(1)} collective-permute-done((s16[1568,128]{1,0:T(8,128)(2,1)S(1)}, s16[1568,128]{1,0:T(8,128)(2,1)S(1)}, u32[]{:S(2)}, u32[]{:S(2)}) %collective-permute-start.9) | collective-permute-done | bytes 401440 | tf_op jit(solution)/shard_map/ppermute | solution.py:318
  40.6 0.4 combine_d.1
  41.0 1.6 %collective-permute-start.10 = (s16[528,128]{1,0:T(8,128)(2,1)S(1)}, s16[528,128]{1,0:T(8,128)(2,1)S(1)}, u32[]{:S(2)}, u32[]{:S(2)}) collective-permute-start(s16[528,128]{1,0:T(8,128)(2,1)S(1)} %get-tuple-element.55), channel_id=1, source_target_pairs={{0,8},{1,9},{2,10},{3,11},{4,12},{5,13},{6,14},{7,15},{8,0},{9,1},... | collective-permute-start | bytes 405512 | tf_op jit(solution)/shard_map/ppermute | solution.py:305
  42.6 0.5 collective-permute-start.11
  43.1 1.5 %collective-permute-start.12 = (s16[528,128]{1,0:T(8,128)(2,1)S(1)}, s16[528,128]{1,0:T(8,128)(2,1)S(1)}, u32[]{:S(2)}, u32[]{:S(2)}) collective-permute-start(s16[528,128]{1,0:T(8,128)(2,1)S(1)} %get-tuple-element.57), channel_id=1, source_target_pairs={{0,24},{1,25},{2,26},{3,27},{4,28},{5,29},{6,30},{7,31},{8,16},{9,... | collective-permute-start | bytes 405512 | tf_op jit(solution)/shard_map/ppermute | solution.py:305
  44.6 7.5 %collective-permute-start.15 = (s16[272,128]{1,0:T(8,128)(2,1)S(1)}, s16[272,128]{1,0:T(8,128)(2,1)S(1)}, u32[]{:S(2)}, u32[]{:S(2)}) collective-permute-start(s16[272,128]{1,0:T(8,128)(2,1)S(1)} %get-tuple-element.62), channel_id=1, source_target_pairs={{1,10},{2,25},{5,14},{6,29},{8,3},{11,16},{12,7},{15,20},{16,11},{... | collective-permute-start | bytes 208904 | tf_op jit(solution)/shard_map/ppermute | solution.py:315
  52.2 0.0 collective-permute-done.10.m1_ref
  52.2 0.0 collective-permute-done.11.m2_ref
  52.2 0.0 collective-permute-done.12.m3_ref
  52.2 0.2 plane_d.1
  52.4 1.3 %collective-permute-start.13 = (s16[272,128]{1,0:T(8,128)(2,1)S(1)}, s16[272,128]{1,0:T(8,128)(2,1)S(1)}, u32[]{:S(2)}, u32[]{:S(2)}) collective-permute-start(s16[272,128]{1,0:T(8,128)(2,1)S(1)} %get-tuple-element.60), channel_id=1, source_target_pairs={{0,2},{1,8},{3,17},{4,6},{5,12},{7,21},{8,1},{9,11},{10,24},{12,5}... | collective-permute-start | bytes 208904 | tf_op jit(solution)/shard_map/ppermute | solution.py:315
  53.7 6.5 %collective-permute-start.14 = (s16[272,128]{1,0:T(8,128)(2,1)S(1)}, s16[272,128]{1,0:T(8,128)(2,1)S(1)}, u32[]{:S(2)}, u32[]{:S(2)}) collective-permute-start(s16[272,128]{1,0:T(8,128)(2,1)S(1)} %get-tuple-element.61), channel_id=1, source_target_pairs={{0,25},{2,3},{4,29},{6,7},{9,16},{11,10},{13,20},{15,14},{16,17},{... | collective-permute-start | bytes 208904 | tf_op jit(solution)/shard_map/ppermute | solution.py:315
  60.2 0.0 collective-permute-done.15.m3_ref
  60.2 0.0 collective-permute-done.13.m1_ref
  60.2 2.3 %collective-permute-done.14.m2_ref = s16[272,128]{1,0:T(8,128)(2,1)S(1)} collective-permute-done((s16[272,128]{1,0:T(8,128)(2,1)S(1)}, s16[272,128]{1,0:T(8,128)(2,1)S(1)}, u32[]{:S(2)}, u32[]{:S(2)}) %collective-permute-start.14) | collective-permute-done | bytes 69664 | tf_op jit(solution)/shard_map/ppermute | solution.py:315
  62.5 0.7 %last.1 = f32[256,128]{1,0:T(8,128)} custom-call(f32[256,128]{1,0:T(8,128)S(1)} %get-tuple-element.59.keep_ref, s16[272,128]{1,0:T(8,128)(2,1)S(1)} %collective-permute-done.13.m1_ref, s16[272,128]{1,0:T(8,128)(2,1)S(1)} %collective-permute-done.14.m2_ref, s16[272,128]{1,0:T(8,128)(2,1)S(1)} %collective-permute-done.15.m3_ref), custom_call_target="tpu_custom_call" | custom-call | tf_op jit(solution)/shard_map/last/pallas_call | solution.py:270
Async XLA Ops:
  0.0 5.6 %copy-start = (bf16[3,1024,256]{2,1,0:T(8,128)(2,1)S(1)}, bf16[3,1024,256]{2,1,0:T(8,128)(2,1)}, u32[]{:S(2)}) copy-start(bf16[3,1024,256]{2,1,0:T(8,128)(2,1)} %s_ref.5) | copy-start | bytes 4718596
  0.0 5.6 %copy-start.2 = (s32[16]{0:T(128)S(1)}, s32[16]{0:T(128)}, u32[]{:S(2)}) copy-start(s32[16]{0:T(128)} %offsets_ref.1) | copy-start | bytes 196
  0.0 5.6 %copy-start.1 = (bf16[16,64,64]{2,1,0:T(8,128)(2,1)S(1)}, bf16[16,64,64]{2,1,0:T(8,128)(2,1)}, u32[]{:S(2)}) copy-start(bf16[16,64,64]{2,1,0:T(8,128)(2,1)} %mass_ref.1) | copy-start | bytes 393220
  1.5 12.6 %collective-permute-start = (bf16[3,256,256]{2,1,0:T(8,128)(2,1)S(1)}, bf16[3,256,256]{2,1,0:T(8,128)(2,1)S(1)}, u32[]{:S(2)}, u32[]{:S(2)}) collective-permute-start(bf16[3,256,256]{2,1,0:T(8,128)(2,1)S(1)} %get-tuple-element.65), channel_id=1, source_target_pairs={{0,1},{1,0},{2,3},{3,2},{4,5},{5,4},{6,7},{7,6},{8,9},{9,8},{10,11... | collective-permute-start | bytes 1179656 | tf_op jit(solution)/shard_map/ppermute | solution.py:293
  3.1 20.9 %collective-permute-start.1 = (bf16[3,256,256]{2,1,0:T(8,128)(2,1)S(1)}, bf16[3,256,256]{2,1,0:T(8,128)(2,1)S(1)}, u32[]{:S(2)}, u32[]{:S(2)}) collective-permute-start(bf16[3,256,256]{2,1,0:T(8,128)(2,1)S(1)} %get-tuple-element.64), channel_id=1, source_target_pairs={{0,3},{1,2},{2,1},{3,0},{4,7},{5,6},{6,5},{7,4},{8,11},{9,10},{10,... | collective-permute-start | bytes 1179656 | tf_op jit(solution)/shard_map/ppermute | solution.py:293
  7.9 1.4 %collective-permute-start.3 = (f32[256,128]{1,0:T(8,128)S(1)}, f32[256,128]{1,0:T(8,128)S(1)}, u32[]{:S(2)}, u32[]{:S(2)}) collective-permute-start(f32[256,128]{1,0:T(8,128)S(1)} %get-tuple-element.39), channel_id=1, source_target_pairs={{0,4},{4,0},{8,12},{12,8},{16,20},{20,16},{24,28},{28,24},{1,5},{5... | collective-permute-start | bytes 393224 | tf_op jit(solution)/shard_map/ppermute | solution.py:318
  8.0 29.7 %collective-permute-start.2 = (bf16[3,256,256]{2,1,0:T(8,128)(2,1)S(1)}, bf16[3,256,256]{2,1,0:T(8,128)(2,1)S(1)}, u32[]{:S(2)}, u32[]{:S(2)}) collective-permute-start(bf16[3,256,256]{2,1,0:T(8,128)(2,1)S(1)} %get-tuple-element.64), channel_id=1, source_target_pairs={{0,1},{1,0},{2,3},{3,2},{4,5},{5,4},{6,7},{7,6},{8,9},{9,8},{10,11... | collective-permute-start | bytes 1179656 | tf_op jit(solution)/shard_map/ppermute | solution.py:293
  9.3 28.4 %collective-permute-start.4 = (bf16[3,256,256]{2,1,0:T(8,128)(2,1)S(1)}, bf16[3,256,256]{2,1,0:T(8,128)(2,1)S(1)}, u32[]{:S(2)}, u32[]{:S(2)}) collective-permute-start(bf16[3,256,256]{2,1,0:T(8,128)(2,1)S(1)} %get-tuple-element.40), channel_id=1, source_target_pairs={{0,2},{1,3},{2,0},{3,1},{4,6},{5,7},{6,4},{7,5},{8,10},{9,11},{10,... | collective-permute-start | bytes 1179656 | tf_op jit(solution)/shard_map/ppermute | solution.py:293
  25.1 1.6 %collective-permute-start.5 = (s16[1040,128]{1,0:T(8,128)(2,1)S(1)}, s16[1040,128]{1,0:T(8,128)(2,1)S(1)}, u32[]{:S(2)}, u32[]{:S(2)}) collective-permute-start(s16[1040,128]{1,0:T(8,128)(2,1)S(1)} %get-tuple-element.42), channel_id=1, source_target_pairs={{0,4},{4,0},{8,12},{12,8},{16,20},{20,16},{24,28},{28,24},{1,5},{5... | collective-permute-start | bytes 798728 | tf_op jit(solution)/shard_map/ppermute | solution.py:318
  26.9 4.4 %collective-permute-start.6 = (s16[272,128]{1,0:T(8,128)(2,1)S(1)}, s16[272,128]{1,0:T(8,128)(2,1)S(1)}, u32[]{:S(2)}, u32[]{:S(2)}) collective-permute-start(s16[272,128]{1,0:T(8,128)(2,1)S(1)} %get-tuple-element.44), channel_id=1, source_target_pairs={{0,8},{1,9},{2,10},{3,11},{4,12},{5,13},{6,14},{7,15},{8,0},{9,1},... | collective-permute-start | bytes 208904 | tf_op jit(solution)/shard_map/ppermute | solution.py:305
  28.5 5.1 %collective-permute-start.7 = (s16[272,128]{1,0:T(8,128)(2,1)S(1)}, s16[272,128]{1,0:T(8,128)(2,1)S(1)}, u32[]{:S(2)}, u32[]{:S(2)}) collective-permute-start(s16[272,128]{1,0:T(8,128)(2,1)S(1)} %get-tuple-element.45), channel_id=1, source_target_pairs={{0,16},{1,17},{2,18},{3,19},{4,20},{5,21},{6,22},{7,23},{8,24},{9,... | collective-permute-start | bytes 208904 | tf_op jit(solution)/shard_map/ppermute | solution.py:305
  29.0 5.3 %collective-permute-start.8 = (s16[272,128]{1,0:T(8,128)(2,1)S(1)}, s16[272,128]{1,0:T(8,128)(2,1)S(1)}, u32[]{:S(2)}, u32[]{:S(2)}) collective-permute-start(s16[272,128]{1,0:T(8,128)(2,1)S(1)} %get-tuple-element.46), channel_id=1, source_target_pairs={{0,24},{1,25},{2,26},{3,27},{4,28},{5,29},{6,30},{7,31},{8,16},{9,... | collective-permute-start | bytes 208904 | tf_op jit(solution)/shard_map/ppermute | solution.py:305
  38.8 1.8 %collective-permute-start.9 = (s16[1568,128]{1,0:T(8,128)(2,1)S(1)}, s16[1568,128]{1,0:T(8,128)(2,1)S(1)}, u32[]{:S(2)}, u32[]{:S(2)}) collective-permute-start(s16[1568,128]{1,0:T(8,128)(2,1)S(1)} %get-tuple-element.51), channel_id=1, source_target_pairs={{0,4},{4,0},{8,12},{12,8},{16,20},{20,16},{24,28},{28,24},{1,5},{5... | collective-permute-start | bytes 1204232 | tf_op jit(solution)/shard_map/ppermute | solution.py:318
  41.0 11.1 %collective-permute-start.10 = (s16[528,128]{1,0:T(8,128)(2,1)S(1)}, s16[528,128]{1,0:T(8,128)(2,1)S(1)}, u32[]{:S(2)}, u32[]{:S(2)}) collective-permute-start(s16[528,128]{1,0:T(8,128)(2,1)S(1)} %get-tuple-element.55), channel_id=1, source_target_pairs={{0,8},{1,9},{2,10},{3,11},{4,12},{5,13},{6,14},{7,15},{8,0},{9,1},... | collective-permute-start | bytes 405512 | tf_op jit(solution)/shard_map/ppermute | solution.py:305
  42.6 9.6 %collective-permute-start.11 = (s16[528,128]{1,0:T(8,128)(2,1)S(1)}, s16[528,128]{1,0:T(8,128)(2,1)S(1)}, u32[]{:S(2)}, u32[]{:S(2)}) collective-permute-start(s16[528,128]{1,0:T(8,128)(2,1)S(1)} %get-tuple-element.56), channel_id=1, source_target_pairs={{0,16},{1,17},{2,18},{3,19},{4,20},{5,21},{6,22},{7,23},{8,24},{9,... | collective-permute-start | bytes 405512 | tf_op jit(solution)/shard_map/ppermute | solution.py:305
  43.1 9.1 %collective-permute-start.12 = (s16[528,128]{1,0:T(8,128)(2,1)S(1)}, s16[528,128]{1,0:T(8,128)(2,1)S(1)}, u32[]{:S(2)}, u32[]{:S(2)}) collective-permute-start(s16[528,128]{1,0:T(8,128)(2,1)S(1)} %get-tuple-element.57), channel_id=1, source_target_pairs={{0,24},{1,25},{2,26},{3,27},{4,28},{5,29},{6,30},{7,31},{8,16},{9,... | collective-permute-start | bytes 405512 | tf_op jit(solution)/shard_map/ppermute | solution.py:305
  44.6 15.6 %collective-permute-start.15 = (s16[272,128]{1,0:T(8,128)(2,1)S(1)}, s16[272,128]{1,0:T(8,128)(2,1)S(1)}, u32[]{:S(2)}, u32[]{:S(2)}) collective-permute-start(s16[272,128]{1,0:T(8,128)(2,1)S(1)} %get-tuple-element.62), channel_id=1, source_target_pairs={{1,10},{2,25},{5,14},{6,29},{8,3},{11,16},{12,7},{15,20},{16,11},{... | collective-permute-start | bytes 208904 | tf_op jit(solution)/shard_map/ppermute | solution.py:315
  52.4 7.8 %collective-permute-start.13 = (s16[272,128]{1,0:T(8,128)(2,1)S(1)}, s16[272,128]{1,0:T(8,128)(2,1)S(1)}, u32[]{:S(2)}, u32[]{:S(2)}) collective-permute-start(s16[272,128]{1,0:T(8,128)(2,1)S(1)} %get-tuple-element.60), channel_id=1, source_target_pairs={{0,2},{1,8},{3,17},{4,6},{5,12},{7,21},{8,1},{9,11},{10,24},{12,5}... | collective-permute-start | bytes 208904 | tf_op jit(solution)/shard_map/ppermute | solution.py:315
  53.7 8.8 %collective-permute-start.14 = (s16[272,128]{1,0:T(8,128)(2,1)S(1)}, s16[272,128]{1,0:T(8,128)(2,1)S(1)}, u32[]{:S(2)}, u32[]{:S(2)}) collective-permute-start(s16[272,128]{1,0:T(8,128)(2,1)S(1)} %get-tuple-element.61), channel_id=1, source_target_pairs={{0,25},{2,3},{4,29},{6,7},{9,16},{11,10},{13,20},{15,14},{16,17},{... | collective-permute-start | bytes 208904 | tf_op jit(solution)/shard_map/ppermute | solution.py:315

commit v9 on v8

--- a/solution.py
+++ b/solution.py
@@ -36,11 +36,12 @@
 
 
 STAGE_C = ((1, 3), (3, 0), (3, 1), (0, 3))
-STAGE_D = ((2, 0), (1, 0), (0, 2), (2, 1))
+STAGE_D = ((2, 0), (2, 1), (0, 2), (1, 0))
 STAGE_B = ((0, 1), (1, 2))
 GO_EARLY = {1: (3, 0), 2: (3, 1)}
-GO_FIRST = {0: (2, 0), 1: (1, 0), 3: (2, 1)}
-GO_LAST = {0: (1, 3), 2: (1, 2)}
+GO_FIRST = {0: (2, 0), 1: (2, 1), 3: (1, 0)}
+GO_NEXT = {0: (1, 3)}
+GO_LAST = {2: (1, 2)}
 
 
 def tdot(left, right):
@@ -174,7 +175,7 @@
     emit(scale, [blocks[name] for name in STAGE_D + STAGE_B], own_ref, other_ref)
 
 
-GROUP = 64
+GROUP = 128
 STEPS = 256.0
 TOP = 32700.0
 LEAST = 1e-33
@@ -254,13 +255,14 @@
     total = plane_sum(total_ref, (m1_ref, m2_ref, m3_ref))
     sum_c = sum_c_ref[...]
     encode(total[:1], first_ref)
-    encode(jnp.where(q == 0, sum_c, total[1:]), last_ref)
+    encode(total[1:], last_ref)
     keep_ref[...] = jnp.where(q < 2, total[1], jnp.where(q == 3, sum_c[0], total[0]))
 
 
-def last_kernel(keep_ref, m1_ref, m2_ref, m3_ref, out_ref):
+def last_kernel(keep_ref, *refs):
+    *message_refs, out_ref = refs
     total = keep_ref[...]
-    for ref in (m1_ref, m2_ref, m3_ref):
+    for ref in message_refs:
         total += decode(ref, 1, total.shape[0])[0]
     out_ref[...] = total
 
@@ -369,6 +371,7 @@
     arrived = [send(out[m - 1], m, 0, (0, 1, 2, 3)) for m in (1, 2, 3)]
     sum_c, early = call(plane_c_kernel, [floats(1), coded(1)], "plane_c", total, *arrived)
     from3 = reach(early, GO_EARLY)
+    from1 = reach(early, GO_NEXT)
     s1b, s2, sum_c = lax.optimization_barrier((s1b, s2, sum_c))
 
     own, other = call(
@@ -398,7 +401,7 @@
     keep, first, last = call(
         plane_d_kernel, [floats(), coded(1), coded(1)], "plane_d", total, *arrived, sum_c
     )
-    arrived = [reach(first, GO_FIRST), reach(last, GO_LAST), from3]
+    arrived = [reach(first, GO_FIRST), reach(last, GO_LAST), from3, from1]
     return call(last_kernel, [floats()], "last", keep, *arrived)[0]
 
 

time: 63.8 us -> 63.7 us (level)
  the two profiles are of different devices: /device:TPU:4 before, /device:TPU:18 now
where the time goes in v9:
time: 63.7 us; the launch traced here: 63.5 us
  waiting for transfers between devices  33.7 us (53%)
  starting transfers between devices  22.2 us (35%)
  Pallas kernels  6.03 us (9%)
  local copies, waits for them, and re-layouts  1.46 us (2%)
    ppermute x4, waiting for transfers between devices, to_plane(): return lax.ppermute(array, 'snap', [(i, i ^ m) for i in range(planes)])  17.8 us
    ppermute x4, starting transfers between devices, reach(): return lax.ppermute(array, ('cells', 'snap'), pairs)  9.06 us
    ppermute x6, waiting for transfers between devices, send(): return lax.ppermute(array, ('cells', 'snap'), pairs)  7.8 us
    ppermute x6, starting transfers between devices, send(): return lax.ppermute(array, ('cells', 'snap'), pairs)  7.11 us
    pallas_call x8, Pallas kernels, call(): pl.pallas_call(kernel, out_shape=[jax.ShapeDtypeStruct(s, t) for s, t in...  6.03 us
    ppermute x4, starting transfers between devices, to_plane(): return lax.ppermute(array, 'snap', [(i, i ^ m) for i in range(planes)])  5.77 us
    ppermute x4, waiting for transfers between devices, reach(): return lax.ppermute(array, ('cells', 'snap'), pairs)  4.89 us
    ppermute x3, waiting for transfers between devices, swap(): return lax.ppermute(array, 'cells', [(c, c ^ 1) for c in range(devices)])  3.25 us
  transfers between devices with their start and end apart: 17, of which 14 were waited for; matrix products, arithmetic and copies ran while one was open for 0% of the time, Pallas kernels for 6%

profile of v9, /device:TPU:18, one launch (start us, length us, event | category | flops | bytes accessed | tf_op | source)
XLA Modules:
  0.0 63.5 jit_solution(12641887407774977778)
XLA Ops:
  0.0 0.0 copy-start
  0.0 0.0 copy-start.2
  0.0 0.0 copy-start.1
  0.0 1.4 %constant_dynamic-slice_fusion = (bf16[3,256,256]{2,1,0:T(8,128)(2,1)S(1)}, bf16[3,256,256]{2,1,0:T(8,128)(2,1)S(1)}, bf16[3,256,256]{2,1,0:T(8,128)(2,1)S(1)}) fusion(bf16[3,1024,256]{2,1,0:T(8,128)(2,1)} %s_ref.5, s32[]{:T(128)S(6)} %select_n.11, s32[]{:T(128)S(6)} %select_n.10, s32[]{:T(128)S(6)} %select_n.9), kind=kLoop, calls=%fused_computation | loop fusion | bytes 2359308 | tf_op jit(solution)/shard_map/dynamic_slice | solution.py:298
  1.5 1.6 %collective-permute-start = (bf16[3,256,256]{2,1,0:T(8,128)(2,1)S(1)}, bf16[3,256,256]{2,1,0:T(8,128)(2,1)S(1)}, u32[]{:S(2)}, u32[]{:S(2)}) collective-permute-start(bf16[3,256,256]{2,1,0:T(8,128)(2,1)S(1)} %get-tuple-element.65), channel_id=1, source_target_pairs={{0,1},{1,0},{2,3},{3,2},{4,5},{5,4},{6,7},{7,6},{8,9},{9,8},{10,11... | collective-permute-start | bytes 1179656 | tf_op jit(solution)/shard_map/ppermute | solution.py:295
  3.1 0.0 collective-permute-start.1
  3.1 0.0 copy-done
  3.1 0.0 copy-done.2
  3.1 0.0 copy-done.1
  3.1 2.3 %early.1 = (bf16[4,256,256]{2,1,0:T(8,128)(2,1)S(1)}, bf16[3,1024,256]{2,1,0:T(8,128)(2,1)S(1)}, f32[256,128]{1,0:T(8,128)S(1)}, f32[256,128]{1,0:T(8,128)S(1)}) custom-call(s32[16]{0:T(128)S(1)} %copy-done.2, bf16[16,64,64]{2,1,0:T(8,128)(2,1)S(1)} %copy-done.1, bf16[3,1024,256]{2,1,0:T(8,128)(2,1)S(1)} %copy-done), custom_call_target="tpu_custom_call" | custom-call | tf_op jit(solution)/shard_map/early/pallas_call | solution.py:272
  5.4 0.1 collective-permute-start.3
  5.5 1.8 %collective-permute-start.2 = (bf16[3,256,256]{2,1,0:T(8,128)(2,1)S(1)}, bf16[3,256,256]{2,1,0:T(8,128)(2,1)S(1)}, u32[]{:S(2)}, u32[]{:S(2)}) collective-permute-start(bf16[3,256,256]{2,1,0:T(8,128)(2,1)S(1)} %get-tuple-element.64), channel_id=1, source_target_pairs={{0,1},{1,0},{2,3},{3,2},{4,5},{5,4},{6,7},{7,6},{8,9},{9,8},{10,11... | collective-permute-start | bytes 1179656 | tf_op jit(solution)/shard_map/ppermute | solution.py:295
  7.4 0.0 collective-permute-done.3.other_ref
  7.4 2.3 %collective-permute-start.4 = (bf16[3,256,256]{2,1,0:T(8,128)(2,1)S(1)}, bf16[3,256,256]{2,1,0:T(8,128)(2,1)S(1)}, u32[]{:S(2)}, u32[]{:S(2)}) collective-permute-start(bf16[3,256,256]{2,1,0:T(8,128)(2,1)S(1)} %get-tuple-element.40), channel_id=1, source_target_pairs={{0,2},{1,3},{2,0},{3,1},{4,6},{5,7},{6,4},{7,5},{8,10},{9,11},{10,... | collective-permute-start | bytes 1179656 | tf_op jit(solution)/shard_map/ppermute | solution.py:295
  9.7 12.3 %collective-permute-done.s1_ref = bf16[3,256,256]{2,1,0:T(8,128)(2,1)S(1)} collective-permute-done((bf16[3,256,256]{2,1,0:T(8,128)(2,1)S(1)}, bf16[3,256,256]{2,1,0:T(8,128)(2,1)S(1)}, u32[]{:S(2)}, u32[]{:S(2)}) %collective-permute-start) | collective-permute-done | bytes 393248 | tf_op jit(solution)/shard_map/ppermute | solution.py:295
  22.0 1.6 %collective-permute-done.1.s3_ref = bf16[3,256,256]{2,1,0:T(8,128)(2,1)S(1)} collective-permute-done((bf16[3,256,256]{2,1,0:T(8,128)(2,1)S(1)}, bf16[3,256,256]{2,1,0:T(8,128)(2,1)S(1)}, u32[]{:S(2)}, u32[]{:S(2)}) %collective-permute-start.1) | collective-permute-done | bytes 393248 | tf_op jit(solution)/shard_map/ppermute | solution.py:295
  23.6 1.0 %stage_c.1 = (f32[4,256,128]{2,1,0:T(8,128)S(1)}, s16[1040,128]{1,0:T(8,128)(2,1)S(1)}, bf16[768,256]{1,0:T(8,128)(2,1)S(1)}, bf16[2,256,768]{2,1,0:T(8,128)(2,1)S(1)}, f32[2,256,256]{2,1,0:T(8,128)S(1)}) custom-call(bf16[3,1024,256]{2,1,0:T(8,128)(2,1)S(1)} %copy-done, bf16[3,1024,256]{2,1,0:T(8,128)(2,1)S(1)} %get-tuple-element.34.weighted_ref, ...), custom_call_target="tpu_custom_call" | custom-call | tf_op jit(solution)/shard_map/stage_c/pallas_call | solution.py:272
  24.6 0.1 collective-permute-start.5
  24.7 1.5 %collective-permute-done.5.arrived_ref = s16[1040,128]{1,0:T(8,128)(2,1)S(1)} collective-permute-done((s16[1040,128]{1,0:T(8,128)(2,1)S(1)}, s16[1040,128]{1,0:T(8,128)(2,1)S(1)}, u32[]{:S(2)}, u32[]{:S(2)}) %collective-permute-start.5) | collective-permute-done | bytes 266272 | tf_op jit(solution)/shard_map/ppermute | solution.py:320
  26.2 0.2 combine_c.1
  26.4 0.6 collective-permute-start.6
  27.0 1.5 %collective-permute-start.7 = (s16[272,128]{1,0:T(8,128)(2,1)S(1)}, s16[272,128]{1,0:T(8,128)(2,1)S(1)}, u32[]{:S(2)}, u32[]{:S(2)}) collective-permute-start(s16[272,128]{1,0:T(8,128)(2,1)S(1)} %get-tuple-element.45), channel_id=1, source_target_pairs={{0,16},{1,17},{2,18},{3,19},{4,20},{5,21},{6,22},{7,23},{8,24},{9,... | collective-permute-start | bytes 208904 | tf_op jit(solution)/shard_map/ppermute | solution.py:307
  28.6 1.4 %collective-permute-start.8 = (s16[272,128]{1,0:T(8,128)(2,1)S(1)}, s16[272,128]{1,0:T(8,128)(2,1)S(1)}, u32[]{:S(2)}, u32[]{:S(2)}) collective-permute-start(s16[272,128]{1,0:T(8,128)(2,1)S(1)} %get-tuple-element.46), channel_id=1, source_target_pairs={{0,24},{1,25},{2,26},{3,27},{4,28},{5,29},{6,30},{7,31},{8,16},{9,... | collective-permute-start | bytes 208904 | tf_op jit(solution)/shard_map/ppermute | solution.py:307
  30.0 1.0 %collective-permute-done.6.m1_ref = s16[272,128]{1,0:T(8,128)(2,1)S(1)} collective-permute-done((s16[272,128]{1,0:T(8,128)(2,1)S(1)}, s16[272,128]{1,0:T(8,128)(2,1)S(1)}, u32[]{:S(2)}, u32[]{:S(2)}) %collective-permute-start.6) | collective-permute-done | bytes 69664 | tf_op jit(solution)/shard_map/ppermute | solution.py:307
  31.0 0.3 collective-permute-done.7.m2_ref
  31.4 2.4 %collective-permute-done.8.m3_ref = s16[272,128]{1,0:T(8,128)(2,1)S(1)} collective-permute-done((s16[272,128]{1,0:T(8,128)(2,1)S(1)}, s16[272,128]{1,0:T(8,128)(2,1)S(1)}, u32[]{:S(2)}, u32[]{:S(2)}) %collective-permute-start.8) | collective-permute-done | bytes 69664 | tf_op jit(solution)/shard_map/ppermute | solution.py:307
  33.8 0.1 plane_c.1
  33.9 1.6 %collective-permute-done.2.s1b_ref = bf16[3,256,256]{2,1,0:T(8,128)(2,1)S(1)} collective-permute-done((bf16[3,256,256]{2,1,0:T(8,128)(2,1)S(1)}, bf16[3,256,256]{2,1,0:T(8,128)(2,1)S(1)}, u32[]{:S(2)}, u32[]{:S(2)}) %collective-permute-start.2) | collective-permute-done | bytes 393248 | tf_op jit(solution)/shard_map/ppermute | solution.py:295
  35.5 2.2 %collective-permute-done.4.s2_ref = bf16[3,256,256]{2,1,0:T(8,128)(2,1)S(1)} collective-permute-done((bf16[3,256,256]{2,1,0:T(8,128)(2,1)S(1)}, bf16[3,256,256]{2,1,0:T(8,128)(2,1)S(1)}, u32[]{:S(2)}, u32[]{:S(2)}) %collective-permute-start.4) | collective-permute-done | bytes 393248 | tf_op jit(solution)/shard_map/ppermute | solution.py:295
  37.7 1.1 %stage_d.1 = (f32[6,256,128]{2,1,0:T(8,128)S(1)}, s16[1552,128]{1,0:T(8,128)(2,1)S(1)}) custom-call(bf16[3,1024,256]{2,1,0:T(8,128)(2,1)S(1)} %copy-done, bf16[3,1024,256]{2,1,0:T(8,128)(2,1)S(1)} %get-tuple-element.34.weighted_ref, bf16[4,256,256]{2,1,0:T(8,128)(2,1)S(1)} %get-tuple-element.35.diagonal_ref, ...), custom_call_target="tpu_custom_call" | custom-call | tf_op jit(solution)/shard_map/stage_d/pallas_call | solution.py:272
  38.8 0.1 collective-permute-start.9
  38.9 1.7 %collective-permute-done.9.arrived_ref = s16[1552,128]{1,0:T(8,128)(2,1)S(1)} collective-permute-done((s16[1552,128]{1,0:T(8,128)(2,1)S(1)}, s16[1552,128]{1,0:T(8,128)(2,1)S(1)}, u32[]{:S(2)}, u32[]{:S(2)}) %collective-permute-start.9) | collective-permute-done | bytes 397344 | tf_op jit(solution)/shard_map/ppermute | solution.py:320
  40.6 0.4 combine_d.1
  41.0 0.6 collective-permute-start.10
  41.6 1.5 %collective-permute-start.11 = (s16[528,128]{1,0:T(8,128)(2,1)S(1)}, s16[528,128]{1,0:T(8,128)(2,1)S(1)}, u32[]{:S(2)}, u32[]{:S(2)}) collective-permute-start(s16[528,128]{1,0:T(8,128)(2,1)S(1)} %get-tuple-element.56), channel_id=1, source_target_pairs={{0,16},{1,17},{2,18},{3,19},{4,20},{5,21},{6,22},{7,23},{8,24},{9,... | collective-permute-start | bytes 405512 | tf_op jit(solution)/shard_map/ppermute | solution.py:307
  43.1 1.4 %collective-permute-start.12 = (s16[528,128]{1,0:T(8,128)(2,1)S(1)}, s16[528,128]{1,0:T(8,128)(2,1)S(1)}, u32[]{:S(2)}, u32[]{:S(2)}) collective-permute-start(s16[528,128]{1,0:T(8,128)(2,1)S(1)} %get-tuple-element.57), channel_id=1, source_target_pairs={{0,24},{1,25},{2,26},{3,27},{4,28},{5,29},{6,30},{7,31},{8,16},{9,... | collective-permute-start | bytes 405512 | tf_op jit(solution)/shard_map/ppermute | solution.py:307
  44.6 0.7 %collective-permute-start.16 = (s16[272,128]{1,0:T(8,128)(2,1)S(1)}, s16[272,128]{1,0:T(8,128)(2,1)S(1)}, u32[]{:S(2)}, u32[]{:S(2)}) collective-permute-start(s16[272,128]{1,0:T(8,128)(2,1)S(1)} %get-tuple-element.62), channel_id=1, source_target_pairs={{0,25},{4,29},{9,16},{13,20},{18,11},{22,15},{27,2},{31,6}} | collective-permute-start | bytes 208904 | tf_op jit(solution)/shard_map/ppermute | solution.py:317
  45.2 1.3 %collective-permute-start.15 = (s16[272,128]{1,0:T(8,128)(2,1)S(1)}, s16[272,128]{1,0:T(8,128)(2,1)S(1)}, u32[]{:S(2)}, u32[]{:S(2)}) collective-permute-start(s16[272,128]{1,0:T(8,128)(2,1)S(1)} %get-tuple-element.62), channel_id=1, source_target_pairs={{1,10},{2,25},{5,14},{6,29},{8,3},{11,16},{12,7},{15,20},{16,11},{... | collective-permute-start | bytes 208904 | tf_op jit(solution)/shard_map/ppermute | solution.py:317
  46.5 1.0 %collective-permute-done.10.m1_ref = s16[528,128]{1,0:T(8,128)(2,1)S(1)} collective-permute-done((s16[528,128]{1,0:T(8,128)(2,1)S(1)}, s16[528,128]{1,0:T(8,128)(2,1)S(1)}, u32[]{:S(2)}, u32[]{:S(2)}) %collective-permute-start.10) | collective-permute-done | bytes 135200 | tf_op jit(solution)/shard_map/ppermute | solution.py:307
  47.5 1.4 %collective-permute-done.11.m2_ref = s16[528,128]{1,0:T(8,128)(2,1)S(1)} collective-permute-done((s16[528,128]{1,0:T(8,128)(2,1)S(1)}, s16[528,128]{1,0:T(8,128)(2,1)S(1)}, u32[]{:S(2)}, u32[]{:S(2)}) %collective-permute-start.11) | collective-permute-done | bytes 135200 | tf_op jit(solution)/shard_map/ppermute | solution.py:307
  48.9 1.6 %collective-permute-done.12.m3_ref = s16[528,128]{1,0:T(8,128)(2,1)S(1)} collective-permute-done((s16[528,128]{1,0:T(8,128)(2,1)S(1)}, s16[528,128]{1,0:T(8,128)(2,1)S(1)}, u32[]{:S(2)}, u32[]{:S(2)}) %collective-permute-start.12) | collective-permute-done | bytes 135200 | tf_op jit(solution)/shard_map/ppermute | solution.py:307
  50.5 0.2 plane_d.1
  50.7 5.8 %collective-permute-start.13 = (s16[272,128]{1,0:T(8,128)(2,1)S(1)}, s16[272,128]{1,0:T(8,128)(2,1)S(1)}, u32[]{:S(2)}, u32[]{:S(2)}) collective-permute-start(s16[272,128]{1,0:T(8,128)(2,1)S(1)} %get-tuple-element.60), channel_id=1, source_target_pairs={{0,2},{1,3},{3,26},{4,6},{5,7},{7,30},{8,10},{9,11},{10,19},{12,14... | collective-permute-start | bytes 208904 | tf_op jit(solution)/shard_map/ppermute | solution.py:317
  56.6 1.3 %collective-permute-start.14 = (s16[272,128]{1,0:T(8,128)(2,1)S(1)}, s16[272,128]{1,0:T(8,128)(2,1)S(1)}, u32[]{:S(2)}, u32[]{:S(2)}) collective-permute-start(s16[272,128]{1,0:T(8,128)(2,1)S(1)} %get-tuple-element.61), channel_id=1, source_target_pairs={{2,3},{6,7},{11,10},{15,14},{16,17},{20,21},{25,24},{29,28}} | collective-permute-start | bytes 208904 | tf_op jit(solution)/shard_map/ppermute | solution.py:317
  57.9 0.0 collective-permute-done.16.refs_3_
  57.9 0.0 collective-permute-done.15.refs_2_
  57.9 1.3 %collective-permute-done.13.refs_0_ = s16[272,128]{1,0:T(8,128)(2,1)S(1)} collective-permute-done((s16[272,128]{1,0:T(8,128)(2,1)S(1)}, s16[272,128]{1,0:T(8,128)(2,1)S(1)}, u32[]{:S(2)}, u32[]{:S(2)}) %collective-permute-start.13) | collective-permute-done | bytes 69664 | tf_op jit(solution)/shard_map/ppermute | solution.py:317
  59.1 3.6 %collective-permute-done.14.refs_1_ = s16[272,128]{1,0:T(8,128)(2,1)S(1)} collective-permute-done((s16[272,128]{1,0:T(8,128)(2,1)S(1)}, s16[272,128]{1,0:T(8,128)(2,1)S(1)}, u32[]{:S(2)}, u32[]{:S(2)}) %collective-permute-start.14) | collective-permute-done | bytes 69664 | tf_op jit(solution)/shard_map/ppermute | solution.py:317
  62.8 0.7 %last.1 = f32[256,128]{1,0:T(8,128)} custom-call(f32[256,128]{1,0:T(8,128)S(1)} %get-tuple-element.59.keep_ref, s16[272,128]{1,0:T(8,128)(2,1)S(1)} %collective-permute-done.13.refs_0_, s16[272,128]{1,0:T(8,128)(2,1)S(1)} %collective-permute-done.14.refs_1_, s16[272,128]{1,0:T(8,128)(2,1)S(1)} %collective-permute-done.15.refs_2_, ...), custom_call_target="tpu_custom_call" | custom-call | tf_op jit(solution)/shard_map/last/pallas_call | solution.py:272
Async XLA Ops:
  0.0 3.1 %copy-start = (bf16[3,1024,256]{2,1,0:T(8,128)(2,1)S(1)}, bf16[3,1024,256]{2,1,0:T(8,128)(2,1)}, u32[]{:S(2)}) copy-start(bf16[3,1024,256]{2,1,0:T(8,128)(2,1)} %s_ref.5) | copy-start | bytes 4718596
  0.0 3.1 %copy-start.2 = (s32[16]{0:T(128)S(1)}, s32[16]{0:T(128)}, u32[]{:S(2)}) copy-start(s32[16]{0:T(128)} %offsets_ref.1) | copy-start | bytes 196
  0.0 3.1 %copy-start.1 = (bf16[16,64,64]{2,1,0:T(8,128)(2,1)S(1)}, bf16[16,64,64]{2,1,0:T(8,128)(2,1)}, u32[]{:S(2)}) copy-start(bf16[16,64,64]{2,1,0:T(8,128)(2,1)} %mass_ref.1) | copy-start | bytes 393220
  1.5 20.5 %collective-permute-start = (bf16[3,256,256]{2,1,0:T(8,128)(2,1)S(1)}, bf16[3,256,256]{2,1,0:T(8,128)(2,1)S(1)}, u32[]{:S(2)}, u32[]{:S(2)}) collective-permute-start(bf16[3,256,256]{2,1,0:T(8,128)(2,1)S(1)} %get-tuple-element.65), channel_id=1, source_target_pairs={{0,1},{1,0},{2,3},{3,2},{4,5},{5,4},{6,7},{7,6},{8,9},{9,8},{10,11... | collective-permute-start | bytes 1179656 | tf_op jit(solution)/shard_map/ppermute | solution.py:295
  3.1 20.5 %collective-permute-start.1 = (bf16[3,256,256]{2,1,0:T(8,128)(2,1)S(1)}, bf16[3,256,256]{2,1,0:T(8,128)(2,1)S(1)}, u32[]{:S(2)}, u32[]{:S(2)}) collective-permute-start(bf16[3,256,256]{2,1,0:T(8,128)(2,1)S(1)} %get-tuple-element.64), channel_id=1, source_target_pairs={{0,3},{1,2},{2,1},{3,0},{4,7},{5,6},{6,5},{7,4},{8,11},{9,10},{10,... | collective-permute-start | bytes 1179656 | tf_op jit(solution)/shard_map/ppermute | solution.py:295
  5.4 1.9 %collective-permute-start.3 = (f32[256,128]{1,0:T(8,128)S(1)}, f32[256,128]{1,0:T(8,128)S(1)}, u32[]{:S(2)}, u32[]{:S(2)}) collective-permute-start(f32[256,128]{1,0:T(8,128)S(1)} %get-tuple-element.39), channel_id=1, source_target_pairs={{0,4},{4,0},{8,12},{12,8},{16,20},{20,16},{24,28},{28,24},{1,5},{5... | collective-permute-start | bytes 393224 | tf_op jit(solution)/shard_map/ppermute | solution.py:320
  5.5 30.0 %collective-permute-start.2 = (bf16[3,256,256]{2,1,0:T(8,128)(2,1)S(1)}, bf16[3,256,256]{2,1,0:T(8,128)(2,1)S(1)}, u32[]{:S(2)}, u32[]{:S(2)}) collective-permute-start(bf16[3,256,256]{2,1,0:T(8,128)(2,1)S(1)} %get-tuple-element.64), channel_id=1, source_target_pairs={{0,1},{1,0},{2,3},{3,2},{4,5},{5,4},{6,7},{7,6},{8,9},{9,8},{10,11... | collective-permute-start | bytes 1179656 | tf_op jit(solution)/shard_map/ppermute | solution.py:295
  7.4 30.3 %collective-permute-start.4 = (bf16[3,256,256]{2,1,0:T(8,128)(2,1)S(1)}, bf16[3,256,256]{2,1,0:T(8,128)(2,1)S(1)}, u32[]{:S(2)}, u32[]{:S(2)}) collective-permute-start(bf16[3,256,256]{2,1,0:T(8,128)(2,1)S(1)} %get-tuple-element.40), channel_id=1, source_target_pairs={{0,2},{1,3},{2,0},{3,1},{4,6},{5,7},{6,4},{7,5},{8,10},{9,11},{10,... | collective-permute-start | bytes 1179656 | tf_op jit(solution)/shard_map/ppermute | solution.py:295
  24.6 1.6 %collective-permute-start.5 = (s16[1040,128]{1,0:T(8,128)(2,1)S(1)}, s16[1040,128]{1,0:T(8,128)(2,1)S(1)}, u32[]{:S(2)}, u32[]{:S(2)}) collective-permute-start(s16[1040,128]{1,0:T(8,128)(2,1)S(1)} %get-tuple-element.42), channel_id=1, source_target_pairs={{0,4},{4,0},{8,12},{12,8},{16,20},{20,16},{24,28},{28,24},{1,5},{5... | collective-permute-start | bytes 798728 | tf_op jit(solution)/shard_map/ppermute | solution.py:320
  26.4 4.6 %collective-permute-start.6 = (s16[272,128]{1,0:T(8,128)(2,1)S(1)}, s16[272,128]{1,0:T(8,128)(2,1)S(1)}, u32[]{:S(2)}, u32[]{:S(2)}) collective-permute-start(s16[272,128]{1,0:T(8,128)(2,1)S(1)} %get-tuple-element.44), channel_id=1, source_target_pairs={{0,8},{1,9},{2,10},{3,11},{4,12},{5,13},{6,14},{7,15},{8,0},{9,1},... | collective-permute-start | bytes 208904 | tf_op jit(solution)/shard_map/ppermute | solution.py:307
  27.0 4.3 %collective-permute-start.7 = (s16[272,128]{1,0:T(8,128)(2,1)S(1)}, s16[272,128]{1,0:T(8,128)(2,1)S(1)}, u32[]{:S(2)}, u32[]{:S(2)}) collective-permute-start(s16[272,128]{1,0:T(8,128)(2,1)S(1)} %get-tuple-element.45), channel_id=1, source_target_pairs={{0,16},{1,17},{2,18},{3,19},{4,20},{5,21},{6,22},{7,23},{8,24},{9,... | collective-permute-start | bytes 208904 | tf_op jit(solution)/shard_map/ppermute | solution.py:307
  28.6 5.2 %collective-permute-start.8 = (s16[272,128]{1,0:T(8,128)(2,1)S(1)}, s16[272,128]{1,0:T(8,128)(2,1)S(1)}, u32[]{:S(2)}, u32[]{:S(2)}) collective-permute-start(s16[272,128]{1,0:T(8,128)(2,1)S(1)} %get-tuple-element.46), channel_id=1, source_target_pairs={{0,24},{1,25},{2,26},{3,27},{4,28},{5,29},{6,30},{7,31},{8,16},{9,... | collective-permute-start | bytes 208904 | tf_op jit(solution)/shard_map/ppermute | solution.py:307
  38.8 1.8 %collective-permute-start.9 = (s16[1552,128]{1,0:T(8,128)(2,1)S(1)}, s16[1552,128]{1,0:T(8,128)(2,1)S(1)}, u32[]{:S(2)}, u32[]{:S(2)}) collective-permute-start(s16[1552,128]{1,0:T(8,128)(2,1)S(1)} %get-tuple-element.51), channel_id=1, source_target_pairs={{0,4},{4,0},{8,12},{12,8},{16,20},{20,16},{24,28},{28,24},{1,5},{5... | collective-permute-start | bytes 1191944 | tf_op jit(solution)/shard_map/ppermute | solution.py:320
  41.0 6.5 %collective-permute-start.10 = (s16[528,128]{1,0:T(8,128)(2,1)S(1)}, s16[528,128]{1,0:T(8,128)(2,1)S(1)}, u32[]{:S(2)}, u32[]{:S(2)}) collective-permute-start(s16[528,128]{1,0:T(8,128)(2,1)S(1)} %get-tuple-element.55), channel_id=1, source_target_pairs={{0,8},{1,9},{2,10},{3,11},{4,12},{5,13},{6,14},{7,15},{8,0},{9,1},... | collective-permute-start | bytes 405512 | tf_op jit(solution)/shard_map/ppermute | solution.py:307
  41.6 7.3 %collective-permute-start.11 = (s16[528,128]{1,0:T(8,128)(2,1)S(1)}, s16[528,128]{1,0:T(8,128)(2,1)S(1)}, u32[]{:S(2)}, u32[]{:S(2)}) collective-permute-start(s16[528,128]{1,0:T(8,128)(2,1)S(1)} %get-tuple-element.56), channel_id=1, source_target_pairs={{0,16},{1,17},{2,18},{3,19},{4,20},{5,21},{6,22},{7,23},{8,24},{9,... | collective-permute-start | bytes 405512 | tf_op jit(solution)/shard_map/ppermute | solution.py:307
  43.1 7.4 %collective-permute-start.12 = (s16[528,128]{1,0:T(8,128)(2,1)S(1)}, s16[528,128]{1,0:T(8,128)(2,1)S(1)}, u32[]{:S(2)}, u32[]{:S(2)}) collective-permute-start(s16[528,128]{1,0:T(8,128)(2,1)S(1)} %get-tuple-element.57), channel_id=1, source_target_pairs={{0,24},{1,25},{2,26},{3,27},{4,28},{5,29},{6,30},{7,31},{8,16},{9,... | collective-permute-start | bytes 405512 | tf_op jit(solution)/shard_map/ppermute | solution.py:307
  44.6 13.3 %collective-permute-start.16 = (s16[272,128]{1,0:T(8,128)(2,1)S(1)}, s16[272,128]{1,0:T(8,128)(2,1)S(1)}, u32[]{:S(2)}, u32[]{:S(2)}) collective-permute-start(s16[272,128]{1,0:T(8,128)(2,1)S(1)} %get-tuple-element.62), channel_id=1, source_target_pairs={{0,25},{4,29},{9,16},{13,20},{18,11},{22,15},{27,2},{31,6}} | collective-permute-start | bytes 208904 | tf_op jit(solution)/shard_map/ppermute | solution.py:317
  45.2 12.7 %collective-permute-start.15 = (s16[272,128]{1,0:T(8,128)(2,1)S(1)}, s16[272,128]{1,0:T(8,128)(2,1)S(1)}, u32[]{:S(2)}, u32[]{:S(2)}) collective-permute-start(s16[272,128]{1,0:T(8,128)(2,1)S(1)} %get-tuple-element.62), channel_id=1, source_target_pairs={{1,10},{2,25},{5,14},{6,29},{8,3},{11,16},{12,7},{15,20},{16,11},{... | collective-permute-start | bytes 208904 | tf_op jit(solution)/shard_map/ppermute | solution.py:317
  50.7 8.4 %collective-permute-start.13 = (s16[272,128]{1,0:T(8,128)(2,1)S(1)}, s16[272,128]{1,0:T(8,128)(2,1)S(1)}, u32[]{:S(2)}, u32[]{:S(2)}) collective-permute-start(s16[272,128]{1,0:T(8,128)(2,1)S(1)} %get-tuple-element.60), channel_id=1, source_target_pairs={{0,2},{1,3},{3,26},{4,6},{5,7},{7,30},{8,10},{9,11},{10,19},{12,14... | collective-permute-start | bytes 208904 | tf_op jit(solution)/shard_map/ppermute | solution.py:317
  56.6 6.2 %collective-permute-start.14 = (s16[272,128]{1,0:T(8,128)(2,1)S(1)}, s16[272,128]{1,0:T(8,128)(2,1)S(1)}, u32[]{:S(2)}, u32[]{:S(2)}) collective-permute-start(s16[272,128]{1,0:T(8,128)(2,1)S(1)} %get-tuple-element.61), channel_id=1, source_target_pairs={{2,3},{6,7},{11,10},{15,14},{16,17},{20,21},{25,24},{29,28}} | collective-permute-start | bytes 208904 | tf_op jit(solution)/shard_map/ppermute | solution.py:317
